TPU v7x, 32 devices: a whole 2x2x4 slice. The times are simulated.
32 devices in a mesh: dp: 4 (over y, core), expert: 8 (over z, x).
Axes of the slice: x: 2, y: 2, z: 4, core: 2. Of those that a mesh axis runs over, the one named last changes fastest.
Arguments:
- x_in: bfloat16 [12608, 512], P(('dp', 'expert')), may hold values from -6 to 6
- norm_gains: bfloat16 [2, 2, 512], P(None, None, ('dp', 'expert')), may hold values from 0.099609375 to 1.8984375
- norm_biases: bfloat16 [2, 2, 512], P(None, None, ('dp', 'expert')), may hold values from -3 to 3
- w_qkv: bfloat16 [2, 512, 1536], P(None, ('dp', 'expert')), may hold values from -0.375 to 0.375
- w_o: bfloat16 [2, 512, 512], P(None, ('dp', 'expert')), may hold values from -1 to 1
- w_router: bfloat16 [2, 512, 8], P(None, ('dp', 'expert')), may hold values from -0.5 to 0.5
- w_in: bfloat16 [2, 8, 512, 2048], P(None, 'expert'), may hold values from -0.25 to 0.25
- w_out: bfloat16 [2, 8, 2048, 512], P(None, 'expert'), may hold values from -0.1875 to 0.1875
- routes: int32 [2, 12608, 2], P(None, ('dp', 'expert')), may hold values from 0 to 7, all different within a row; in each aligned block of 394 rows (0 to 393, 394 to 787, ..., all dimensions but the last counted through in order) at most 197 rows name the same one
- threshold: float32 [2, 8], replicated, may hold values from 4 to 20
- cotangent: bfloat16 [12608, 512], P(('dp', 'expert')), may hold values from -6 to 6
Outputs:
- out_act: float32 [12608, 512], P(('dp', 'expert'))
- grad_x: float32 [12608, 512], P(('dp', 'expert'))
- grad_norm_gains: float32 [2, 2, 512], P(None, None, ('dp', 'expert'))
- grad_norm_biases: float32 [2, 2, 512], P(None, None, ('dp', 'expert'))
- grad_w_qkv: float32 [2, 512, 1536], P(None, ('dp', 'expert'))
- grad_w_o: float32 [2, 512, 512], P(None, ('dp', 'expert'))
- grad_w_router: float32 [2, 512, 8], P(None, ('dp', 'expert'))
- grad_w_in: float32 [2, 8, 512, 2048], P(None, 'expert', None, 'dp')
- grad_w_out: float32 [2, 8, 2048, 512], P(None, 'expert', 'dp')
- head_max: float32 [2, 8], replicated
- clipped_qk: float32 [2, 512, 1024], P(None, ('dp', 'expert'))
- grad_second_biases: float32 [2, 512], P(None, ('dp', 'expert'))
Inputs may be any that keep to these rules, and one draw needn't show every extreme that they name: `routes`: each row names 2 different experts. In each layer no expert is named by more than 197 of the rows of one device, and on some device some expert is named by exactly 197 of them.
All inputs are finite; a program needn't handle non-finite values.
Results may differ from a plain program's by a relative error of at most 0.024.
Values may be sent and summed in bfloat16 or wider, within the bound.
No kernel may reach another device: no remote copies, remote signals or barrier semaphores. Data moves between devices by JAX's collectives and lax.ppermute only.
A program may use at most 192 MiB of HBM per device.

v0:
```python
import jax
import jax.numpy as jnp
from jax import lax
from jax.sharding import PartitionSpec as P

HEADS = 8
HEAD_DIM = 64
SEQ = 197
TOP = 2
LAYERS = 2


epsilon = 1e-06


def norm_forward(values, gain_row, shift_row):
    center = values - jnp.mean(values, axis=-1, keepdims=True)
    spread = jnp.mean(center * center, axis=-1, keepdims=True)
    inverse = lax.rsqrt(spread + epsilon)
    normed = center * inverse
    return (normed * gain_row + shift_row, normed, inverse)


def norm_backward(upstream, normed, inverse, gain_row):
    scaled = upstream * gain_row
    mean_plain = jnp.mean(scaled, axis=-1, keepdims=True)
    mean_normed = jnp.mean(scaled * normed, axis=-1, keepdims=True)
    return (
        inverse * (scaled - mean_plain - normed * mean_normed),
        jnp.sum(upstream * normed, axis=0),
        jnp.sum(upstream, axis=0),
    )


def heads_apart(packed, images):
    by_head = packed.reshape(images, -1, 3, HEADS, HEAD_DIM)
    return (by_head[:, :, 0], by_head[:, :, 1], by_head[:, :, 2])


def attend_forward(packed, images, score_scale):
    queries, keys_in, values_in = heads_apart(packed, images)
    scores = (
        jnp.einsum("bqhd,bkhd->bhqk", queries, keys_in, preferred_element_type=jnp.float32)
        * score_scale
    )
    highest = jnp.max(scores, axis=-1, keepdims=True)
    log_total = highest + jnp.log(jnp.sum(jnp.exp(scores - highest), axis=-1, keepdims=True))
    weights_low = jnp.exp(scores - log_total).astype(jnp.bfloat16)
    mixed_rows = jnp.einsum(
        "bhqk,bkhd->bqhd", weights_low, values_in, preferred_element_type=jnp.float32
    )
    head_top = jnp.max(highest, axis=(0, 2, 3))
    return (mixed_rows.reshape(-1, HEADS * HEAD_DIM).astype(jnp.bfloat16), log_total, head_top)


def attend_backward(packed, log_total, grad_mixed, images, score_scale):
    queries, keys_in, values_in = heads_apart(packed, images)
    scores = (
        jnp.einsum("bqhd,bkhd->bhqk", queries, keys_in, preferred_element_type=jnp.float32)
        * score_scale
    )
    weights_full = jnp.exp(scores - log_total)
    weights_low = weights_full.astype(jnp.bfloat16)
    grad_heads = grad_mixed.reshape(images, -1, HEADS, HEAD_DIM)
    grad_values = jnp.einsum(
        "bhqk,bqhd->bkhd", weights_low, grad_heads, preferred_element_type=jnp.float32
    )
    grad_weights = jnp.einsum(
        "bqhd,bkhd->bhqk", grad_heads, values_in, preferred_element_type=jnp.float32
    )
    grad_scores = (
        weights_full * (grad_weights - jnp.sum(grad_weights * weights_full, axis=-1, keepdims=True))
    ).astype(jnp.bfloat16)
    grad_queries = (
        jnp.einsum("bhqk,bkhd->bqhd", grad_scores, keys_in, preferred_element_type=jnp.float32)
        * score_scale
    )
    grad_keys = (
        jnp.einsum("bhqk,bqhd->bkhd", grad_scores, queries, preferred_element_type=jnp.float32)
        * score_scale
    )
    stacked = jnp.stack([grad_queries, grad_keys, grad_values], axis=2)
    return stacked.reshape(-1, 3 * HEADS * HEAD_DIM).astype(jnp.bfloat16)


def slot_places(route_rows, experts, capacity):
    flat_routes = route_rows.reshape(-1)
    matches = (flat_routes[:, None] == jnp.arange(experts, dtype=jnp.int32)[None, :]).astype(
        jnp.int32
    )
    before = jnp.cumsum(matches, axis=0) - matches
    return flat_routes * capacity + jnp.sum(before * matches, axis=1)


def place_rows(rows_in, places, experts, capacity):
    blank_rows = jnp.zeros((experts * capacity, rows_in.shape[-1]), rows_in.dtype)
    return blank_rows.at[places].set(rows_in).reshape(experts, capacity, -1)


def expert_forward(rows_in, weight_in, weight_out):
    hidden = jnp.dot(rows_in, weight_in, preferred_element_type=jnp.float32)
    active = jax.nn.gelu(hidden).astype(jnp.bfloat16)
    return (hidden, active, jnp.dot(active, weight_out, preferred_element_type=jnp.float32))


def expert_backward(rows_in, hidden, active, grad_out_rows, weight_in, weight_out):
    grad_wout = jnp.dot(active.T, grad_out_rows, preferred_element_type=jnp.float32)
    grad_active = jnp.dot(grad_out_rows, weight_out.T, preferred_element_type=jnp.float32)
    grad_hidden = jax.vjp(jax.nn.gelu, hidden)[1](grad_active)[0].astype(jnp.bfloat16)
    grad_win = jnp.dot(rows_in.T, grad_hidden, preferred_element_type=jnp.float32)
    grad_rows = jnp.dot(grad_hidden, weight_in.T, preferred_element_type=jnp.float32)
    return (grad_win, grad_wout, grad_rows)


def body(
    x_in, norm_gains, norm_biases, w_qkv, w_o, w_router, w_in, w_out, routes, threshold, cotangent
):
    token_count = x_in.shape[0]
    features = x_in.shape[1]
    images = token_count // SEQ
    score_scale = HEAD_DIM ** (-0.5)
    experts = lax.axis_size("expert")
    capacity = 4 * token_count // experts
    current = x_in.astype(jnp.float32)
    stored = []
    head_tops = []
    for layer_at in range(LAYERS):
        full_qkv, full_o, full_router, gain_rows, shift_rows = (
            lax.all_gather(w_qkv[layer_at], ("dp", "expert"), axis=0, tiled=True),
            lax.all_gather(w_o[layer_at], ("dp", "expert"), axis=0, tiled=True),
            lax.all_gather(w_router[layer_at], ("dp", "expert"), axis=0, tiled=True),
            lax.all_gather(norm_gains[layer_at], ("dp", "expert"), axis=1, tiled=True),
            lax.all_gather(norm_biases[layer_at], ("dp", "expert"), axis=1, tiled=True),
        )
        gain_rows = gain_rows.astype(jnp.float32)
        shift_rows = shift_rows.astype(jnp.float32)
        normed_one, unit_one, inverse_one = norm_forward(current, gain_rows[0], shift_rows[0])
        normed_one = normed_one.astype(jnp.bfloat16)
        packed = jnp.dot(normed_one, full_qkv, preferred_element_type=jnp.float32).astype(
            jnp.bfloat16
        )
        mixed_rows, log_total, head_top = attend_forward(packed, images, score_scale)
        head_tops.append(head_top)
        middle = current + jnp.dot(mixed_rows, full_o, preferred_element_type=jnp.float32)
        normed_two, unit_two, inverse_two = norm_forward(middle, gain_rows[1], shift_rows[1])
        normed_two = normed_two.astype(jnp.bfloat16)
        logits = jnp.dot(normed_two, full_router, preferred_element_type=jnp.float32)
        router_probs = jax.nn.softmax(logits, axis=-1)
        chosen = (routes[layer_at][:, :, None] == jnp.arange(experts, dtype=jnp.int32)).astype(
            jnp.float32
        )
        picked = jnp.sum(chosen * router_probs[:, None, :], axis=-1)
        picked_total = jnp.sum(picked, axis=1, keepdims=True)
        gate_values = picked / picked_total
        places = slot_places(routes[layer_at], experts, capacity)
        outgoing = place_rows(jnp.repeat(normed_two, TOP, axis=0), places, experts, capacity)
        incoming = lax.all_to_all(outgoing, "expert", split_axis=0, concat_axis=0, tiled=True)
        rows_in = incoming.reshape(-1, features)
        hidden, active, produced = expert_forward(rows_in, w_in[layer_at, 0], w_out[layer_at, 0])
        produced = produced.astype(jnp.bfloat16).reshape(experts, capacity, features)
        expert_kept = (rows_in, hidden, active, w_in[layer_at, 0], w_out[layer_at, 0])
        returned = lax.all_to_all(produced, "expert", split_axis=0, concat_axis=0, tiled=True)
        routed = (
            returned.reshape(-1, features)[places]
            .astype(jnp.float32)
            .reshape(token_count, TOP, features)
        )
        current = middle + jnp.sum(gate_values[:, :, None] * routed, axis=1)
        stored.append(
            (
                unit_one,
                inverse_one,
                normed_one,
                packed,
                log_total,
                mixed_rows,
                unit_two,
                inverse_two,
                normed_two,
                router_probs,
                chosen,
                picked,
                picked_total,
                gate_values,
                places,
                routed,
                expert_kept,
                full_qkv,
                full_o,
                full_router,
                gain_rows,
            )
        )
    upstream = cotangent.astype(jnp.float32)
    layer_grads = [None] * LAYERS
    win_grads = [None] * LAYERS
    wout_grads = [None] * LAYERS
    for layer_at in reversed(range(LAYERS)):
        (
            unit_one,
            inverse_one,
            normed_one,
            packed,
            log_total,
            mixed_rows,
            unit_two,
            inverse_two,
            normed_two,
            router_probs,
            chosen,
            picked,
            picked_total,
            gate_values,
            places,
            routed,
            expert_kept,
            full_qkv,
            full_o,
            full_router,
            gain_rows,
        ) = stored[layer_at]
        grad_gates = jnp.sum(upstream[:, None, :] * routed, axis=-1)
        grad_routed = (
            (gate_values[:, :, None] * upstream[:, None, :])
            .astype(jnp.bfloat16)
            .reshape(-1, features)
        )
        grad_incoming = lax.all_to_all(
            place_rows(grad_routed, places, experts, capacity),
            "expert",
            split_axis=0,
            concat_axis=0,
            tiled=True,
        )
        rows_kept, hidden, active, weight_in, weight_out = expert_kept
        grad_win, grad_wout, grad_rows = expert_backward(
            rows_kept, hidden, active, grad_incoming.reshape(-1, features), weight_in, weight_out
        )
        returning = grad_rows.astype(jnp.bfloat16).reshape(experts, capacity, features)
        win_grads[layer_at] = grad_win
        wout_grads[layer_at] = grad_wout
        grad_back = lax.all_to_all(returning, "expert", split_axis=0, concat_axis=0, tiled=True)
        grad_copies = (
            grad_back.reshape(-1, features)[places]
            .astype(jnp.float32)
            .reshape(token_count, TOP, features)
        )
        weighted = jnp.sum(grad_gates * gate_values, axis=1, keepdims=True)
        grad_picked = (grad_gates - weighted) / picked_total
        amount = grad_picked * picked
        grad_logits = (
            jnp.sum(amount[:, :, None] * chosen, axis=1)
            - router_probs * jnp.sum(amount, axis=1, keepdims=True)
        ).astype(jnp.bfloat16)
        grad_router = jnp.dot(normed_two.T, grad_logits, preferred_element_type=jnp.float32)
        grad_normed_two = jnp.sum(grad_copies, axis=1) + jnp.dot(
            grad_logits, full_router.T, preferred_element_type=jnp.float32
        )
        grad_upper_norm, grad_gain_two, grad_shift_two = norm_backward(
            grad_normed_two, unit_two, inverse_two, gain_rows[1]
        )
        grad_middle = upstream + grad_upper_norm
        grad_attn = grad_middle.astype(jnp.bfloat16)
        grad_wo = jnp.dot(mixed_rows.T, grad_attn, preferred_element_type=jnp.float32)
        grad_mixed = jnp.dot(grad_attn, full_o.T, preferred_element_type=jnp.float32).astype(
            jnp.bfloat16
        )
        grad_packed = attend_backward(packed, log_total, grad_mixed, images, score_scale)
        grad_wqkv = jnp.dot(normed_one.T, grad_packed, preferred_element_type=jnp.float32)
        grad_normed_one = jnp.dot(grad_packed, full_qkv.T, preferred_element_type=jnp.float32)
        grad_lower_norm, grad_gain_one, grad_shift_one = norm_backward(
            grad_normed_one, unit_one, inverse_one, gain_rows[0]
        )
        upstream = grad_middle + grad_lower_norm
        layer_grads[layer_at] = (
            lax.psum_scatter(grad_wqkv, ("dp", "expert"), scatter_dimension=0, tiled=True),
            lax.psum_scatter(grad_wo, ("dp", "expert"), scatter_dimension=0, tiled=True),
            lax.psum_scatter(grad_router, ("dp", "expert"), scatter_dimension=0, tiled=True),
            lax.psum_scatter(
                jnp.stack([grad_gain_one, grad_gain_two]),
                ("dp", "expert"),
                scatter_dimension=1,
                tiled=True,
            ),
            lax.psum_scatter(
                jnp.stack([grad_shift_one, grad_shift_two]),
                ("dp", "expert"),
                scatter_dimension=1,
                tiled=True,
            ),
        )
    stacked_in = jnp.stack(win_grads)[:, None]
    stacked_out = jnp.stack(wout_grads)[:, None]
    stacked_in, stacked_out = (
        lax.psum_scatter(
            stacked_in.astype(jnp.bfloat16), "dp", scatter_dimension=3, tiled=True
        ).astype(jnp.float32),
        lax.psum_scatter(
            stacked_out.astype(jnp.bfloat16), "dp", scatter_dimension=2, tiled=True
        ).astype(jnp.float32),
    )
    grad_w_qkv = jnp.stack([member[0] for member in layer_grads])
    grad_w_o = jnp.stack([member[1] for member in layer_grads])
    grad_w_router = jnp.stack([member[2] for member in layer_grads])
    grad_norm_gains = jnp.stack([member[3] for member in layer_grads])
    grad_norm_biases = jnp.stack([member[4] for member in layer_grads])
    grad_second_biases = grad_norm_biases[:, 1]
    head_max = lax.pmax(jnp.stack(head_tops), ("dp", "expert"))
    factor = jnp.sqrt(threshold / jnp.maximum(head_max, threshold))
    columns = jnp.repeat(factor, HEAD_DIM, axis=1)
    clipped_qk = (
        w_qkv[:, :, : 2 * features].astype(jnp.float32)
        * jnp.concatenate([columns, columns], axis=1)[:, None, :]
    )
    return (
        current,
        upstream,
        grad_norm_gains,
        grad_norm_biases,
        grad_w_qkv,
        grad_w_o,
        grad_w_router,
        stacked_in,
        stacked_out,
        head_max,
        clipped_qk,
        grad_second_biases,
    )


def solution(mesh):
    in_specs = (
        P(("dp", "expert"), None),
        P(None, None, ("dp", "expert")),
        P(None, None, ("dp", "expert")),
        P(None, ("dp", "expert"), None),
        P(None, ("dp", "expert"), None),
        P(None, ("dp", "expert"), None),
        P(None, "expert", None, None),
        P(None, "expert", None, None),
        P(None, ("dp", "expert"), None),
        P(),
        P(("dp", "expert"), None),
    )
    out_specs = (
        P(("dp", "expert"), None),
        P(("dp", "expert"), None),
        P(None, None, ("dp", "expert")),
        P(None, None, ("dp", "expert")),
        P(None, ("dp", "expert"), None),
        P(None, ("dp", "expert"), None),
        P(None, ("dp", "expert"), None),
        P(None, "expert", None, "dp"),
        P(None, "expert", "dp", None),
        P(),
        P(None, ("dp", "expert"), None),
        P(None, ("dp", "expert")),
    )
    return jax.shard_map(body, mesh=mesh, in_specs=in_specs, out_specs=out_specs, check_vma=False)
```

profile of v0, /device:TPU:0, one launch (start us, length us, event | category | flops | bytes accessed | tf_op | source)
XLA Modules:
  0.0 2458.1 jit_solution(310785596486169712)
XLA Ops:
  9.6 71.4 %all-gather.1 = bf16[1,2,512]{1,0,2:T(2,128)(2,1)S(1)} all-gather(bf16[1,2,16]{1,0,2:T(2,128)(2,1)S(1)} %copy.302), channel_id=3, replica_groups=mesh['dp'=4,'expert'=8] {'dp','expert'}, dimensions={2}, use_global_device_ids=true | all-gather | bytes 2112 | tf_op jit(solution)/shard_map/all_gather | solution.py:133
  82.0 64.7 %all-gather = bf16[1,2,512]{1,0,2:T(2,128)(2,1)S(1)} all-gather(bf16[1,2,16]{1,0,2:T(2,128)(2,1)S(1)} %copy.301), channel_id=2, replica_groups=mesh['dp'=4,'expert'=8] {'dp','expert'}, dimensions={2}, use_global_device_ids=true | all-gather | bytes 2112 | tf_op jit(solution)/shard_map/all_gather | solution.py:132
  157.5 69.5 %all-gather.3 = bf16[1,512,512]{2,1,0:T(8,128)(2,1)S(1)} all-gather(bf16[1,16,512]{2,1,0:T(8,128)(2,1)S(1)} %get-tuple-element.63), channel_id=5, replica_groups=mesh['dp'=4,'expert'=8] {'dp','expert'}, dimensions={1}, use_global_device_ids=true | all-gather | bytes 540672 | tf_op jit(solution)/shard_map/all_gather | solution.py:130
  246.3 7.3 scatter_custom_fusion
  255.5 39.1 %all_to_all.40 = bf16[8,197,512]{2,1,0:T(8,128)(2,1)} all-to-all(bf16[8,197,512]{2,1,0:T(8,128)(2,1)S(1)} %reshape.532), channel_id=1, replica_groups=mesh['dp'=4,'expert'=8] {'expert'}, dimensions={0} | all-to-all | bytes 3227648 | tf_op jit(solution)/shard_map/all_to_all | solution.py:157
  296.6 10.4 multiply_convert_fusion.1
  323.1 90.3 %all-gather.4 = bf16[1,512,8]{2,0,1:T(2,128)(2,1)S(1)} all-gather(bf16[1,16,8]{2,0,1:T(2,128)(2,1)S(1)} %copy.306), channel_id=6, replica_groups=mesh['dp'=4,'expert'=8] {'dp','expert'}, dimensions={1}, use_global_device_ids=true | all-gather | bytes 8448 | tf_op jit(solution)/shard_map/all_gather | solution.py:131
  413.6 64.7 %all-gather.6 = bf16[1,2,512]{1,0,2:T(2,128)(2,1)S(1)} all-gather(bf16[1,2,16]{1,0,2:T(2,128)(2,1)S(1)} %copy.308), channel_id=8, replica_groups=mesh['dp'=4,'expert'=8] {'dp','expert'}, dimensions={2}, use_global_device_ids=true | all-gather | bytes 2112 | tf_op jit(solution)/shard_map/all_gather | solution.py:133
  478.7 67.0 %all-gather.5 = bf16[1,2,512]{1,0,2:T(2,128)(2,1)S(1)} all-gather(bf16[1,2,16]{1,0,2:T(2,128)(2,1)S(1)} %copy.307), channel_id=7, replica_groups=mesh['dp'=4,'expert'=8] {'dp','expert'}, dimensions={2}, use_global_device_ids=true | all-gather | bytes 2112 | tf_op jit(solution)/shard_map/all_gather | solution.py:132
  551.9 71.0 %all-gather.8 = bf16[1,512,512]{2,1,0:T(8,128)(2,1)} all-gather(bf16[1,16,512]{2,1,0:T(8,128)(2,1)S(1)} %get-tuple-element.62), channel_id=10, replica_groups=mesh['dp'=4,'expert'=8] {'dp','expert'}, dimensions={1}, use_global_device_ids=true | all-gather | bytes 540672 | tf_op jit(solution)/shard_map/all_gather | solution.py:130
  661.8 7.3 scatter_custom_fusion.1
  682.9 88.2 %all-gather.9 = bf16[1,512,8]{2,0,1:T(2,128)(2,1)S(1)} all-gather(bf16[1,16,8]{2,0,1:T(2,128)(2,1)} %copy.312), channel_id=11, replica_groups=mesh['dp'=4,'expert'=8] {'dp','expert'}, dimensions={1}, use_global_device_ids=true | all-gather | bytes 8448 | tf_op jit(solution)/shard_map/all_gather | solution.py:131
  774.7 10.1 scatter_custom_fusion.2
  787.9 4.7 all-to-all-start.4
  795.7 11.4 multiply_convert_fusion
  807.1 19.4 all-to-all-done.4
  829.6 14.3 fusion.13
  846.5 5.2 convolution_convert_fusion.5
  854.8 4.5 all-to-all-start.5
  859.2 8.1 convolution_convert_fusion.6
  870.5 25.2 %all-to-all-done.5 = bf16[8,197,512]{2,1,0:T(8,128)(2,1)} async-done(((bf16[8,197,512]{2,1,0:T(8,128)(2,1)}), bf16[8,197,512]{2,1,0:T(8,128)(2,1)}, u32[]{:S(2)}, u32[]{:S(2)}) %all-to-all-start.5) | async-done | bytes 1613856 | tf_op jit(solution)/shard_map/all_to_all | solution.py:242
  906.7 5.6 gather_fusion.2
  915.3 22.5 all-to-all-done.3
  940.9 5.6 gather_fusion.1
  949.5 6.4 multiply_reduce_fusion.7
  989.9 9.4 scatter_custom_fusion.3
  1001.0 42.9 %all_to_all.41 = bf16[8,197,512]{2,1,0:T(8,128)(2,1)} all-to-all(bf16[8,197,512]{2,1,0:T(8,128)(2,1)} %reshape.549), channel_id=1, replica_groups=mesh['dp'=4,'expert'=8] {'expert'}, dimensions={0} | all-to-all | bytes 3227648 | tf_op jit(solution)/shard_map/all_to_all | solution.py:228
  1045.9 13.5 fusion.6
  1062.1 5.2 convolution_convert_fusion.4
  1080.7 32.1 %all-to-all-done.7 = bf16[8,197,512]{2,1,0:T(8,128)(2,1)} async-done(((bf16[8,197,512]{2,1,0:T(8,128)(2,1)}), bf16[8,197,512]{2,1,0:T(8,128)(2,1)}, u32[]{:S(2)}, u32[]{:S(2)}) %all-to-all-start.7) | async-done | bytes 1613856 | tf_op jit(solution)/shard_map/all_to_all | solution.py:242
  1150.6 4.4 fusion.135
  1159.5 7.5 fusion.15
  1167.1 7.2 fusion.14
  1176.8 7.4 fusion.17
  1184.2 7.5 fusion.16
  1194.1 25.1 %reduce-scatter.39.cloned.1.call-done = f32[16,2]{1,0:T(8,128)} async-done(((f32[512,2]{1,0:T(8,128)}), f32[16,2]{1,0:T(8,128)}) %reduce-scatter.39.cloned.1.call-update) | async-done | bytes 144
  1220.0 130.8 %reduce-scatter.43.cloned.1.call-done = f32[16,2]{1,0:T(8,128)} async-done(((f32[512,2]{1,0:T(8,128)}), f32[16,2]{1,0:T(8,128)}) %reduce-scatter.43.cloned.1.call-update) | async-done | bytes 144
  1351.5 131.1 %reduce-scatter.47.cloned.1.call-done = f32[16,8]{1,0:T(8,128)} async-done(((f32[512,8]{1,0:T(8,128)}), f32[16,8]{1,0:T(8,128)}) %reduce-scatter.47.cloned.1.call-update) | async-done | bytes 528
  1483.4 131.2 %reduce-scatter.45.cloned.1.call-done = f32[16,8]{1,0:T(8,128)} async-done(((f32[512,8]{1,0:T(8,128)}), f32[16,8]{1,0:T(8,128)}) %reduce-scatter.45.cloned.1.call-update) | async-done | bytes 528
  1615.9 36.9 %pmax.7 = f32[2,8]{1,0:T(2,128)S(1)} all-reduce(f32[2,8]{1,0:T(2,128)S(1)} %pad_maximum_fusion.14), channel_id=1, replica_groups=mesh['dp'=4,'expert'=8] {'dp','expert'}, use_global_device_ids=true, to_apply=%region_74.75 | all-reduce | flops 16 | bytes 128 | tf_op jit(solution)/shard_map/pmax | solution.py:308
  1654.9 91.7 %reduce-scatter.37.cloned.1.call-done = f32[16,2]{1,0:T(8,128)} async-done(((f32[512,2]{1,0:T(8,128)}), f32[16,2]{1,0:T(8,128)}) %reduce-scatter.37.cloned.1.call-update) | async-done | bytes 144
  1747.3 131.3 %reduce-scatter.41.cloned.1.call-done = f32[16,2]{1,0:T(8,128)} async-done(((f32[512,2]{1,0:T(8,128)}), f32[16,2]{1,0:T(8,128)}) %reduce-scatter.41.cloned.1.call-update) | async-done | bytes 144
  1881.1 131.6 %reduce-scatter.31.cloned.1.call-done = f32[16,512]{1,0:T(8,128)} async-done(((f32[512,512]{1,0:T(8,128)}), f32[16,512]{1,0:T(8,128)}) %reduce-scatter.31.cloned.1.call-update) | async-done | bytes 32784 | tf_op jit(solution)/shard_map/reduce_scatter | solution.py:277
  2012.8 133.6 %reduce-scatter.29.cloned.1.call-done = f32[16,512]{1,0:T(8,128)} async-done(((f32[512,512]{1,0:T(8,128)}), f32[16,512]{1,0:T(8,128)}) %reduce-scatter.29.cloned.1.call-update) | async-done | bytes 32784 | tf_op jit(solution)/shard_map/reduce_scatter | solution.py:277
  2147.8 101.9 %reduce-scatter.27.cloned.1.call-done = f32[16,1536]{1,0:T(8,128)} async-done(((f32[512,1536]{1,0:T(8,128)}), f32[16,1536]{1,0:T(8,128)}) %reduce-scatter.27.cloned.1.call-update) | async-done | bytes 98320 | tf_op jit(solution)/shard_map/reduce_scatter | solution.py:276
  2249.6 105.8 %reduce-scatter.25.cloned.1.call-done = f32[16,1536]{1,0:T(8,128)} async-done(((f32[512,1536]{1,0:T(8,128)}), f32[16,1536]{1,0:T(8,128)}) %reduce-scatter.25.cloned.1.call-update) | async-done | bytes 98320 | tf_op jit(solution)/shard_map/reduce_scatter | solution.py:276
  2357.1 44.4 %reduce-scatter.33.cloned.1.call-done = bf16[2,1,512,512]{3,2,1,0:T(8,128)(2,1)} async-done(((bf16[2,1,512,2048]{3,2,1,0:T(8,128)(2,1)}), bf16[2,1,512,512]{3,2,1,0:T(8,128)(2,1)}) %reduce-scatter.33.cloned.1.call-update) | async-done | bytes 1048592 | tf_op jit(solution)/shard_map/reduce_scatter | solution.py:295
  2404.3 44.2 %reduce-scatter.35.cloned.1.call-done = bf16[2,1,512,512]{3,2,1,0:T(8,128)(2,1)} async-done(((bf16[2,1,2048,512]{3,2,1,0:T(8,128)(2,1)}), bf16[2,1,512,512]{3,2,1,0:T(8,128)(2,1)}) %reduce-scatter.35.cloned.1.call-update) | async-done | bytes 1048592 | tf_op jit(solution)/shard_map/reduce_scatter | solution.py:298
  (480 shorter events, 271.3 us)
Async XLA Ops:
  7.2 144.4 %copy-start.16 = (bf16[394,512]{1,0:T(8,128)(2,1)S(1)}, bf16[394,512]{1,0:T(8,128)(2,1)}, u32[]{:S(2)}) copy-start(bf16[394,512]{1,0:T(8,128)(2,1)} %param.11) | copy-start | bytes 1210372
  7.2 150.3 %copy-start.66 = (bf16[2,16,512]{2,1,0:T(8,128)(2,1)S(1)}, bf16[2,16,512]{2,1,0:T(8,128)(2,1)}, u32[]{:S(2)}) copy-start(bf16[2,16,512]{2,1,0:T(8,128)(2,1)} %param.15) | copy-start | bytes 98308
  7.2 219.8 %all-gather.13.cloned.1.call-start = ((), (), s32[]{:S(2)}) async-start(), calls=%async_computation.26 | async-start | bytes 1622016 | tf_op jit(solution)/shard_map/all_gather | solution.py:129
  148.3 475.4 %copy-start.61 = (s32[394,2]{0,1:T(2,128)}, s32[394,2]{0,1:T(2,128)S(1)}, u32[]{:S(2)}) copy-start(s32[394,2]{0,1:T(2,128)S(1)} %get-tuple-element.65) | copy-start | bytes 9460
  151.6 394.7 %copy-start.89 = (s32[788]{0:T(1024)}, s32[788]{0:T(1024)S(1)}, u32[]{:S(2)}) copy-start(s32[788]{0:T(1024)S(1)} %fusion.124) | copy-start | bytes 9460
  151.7 75.3 %copy-start.79 = (f32[394]{0:T(512)}, f32[394]{0:T(512)S(1)}, u32[]{:S(2)}) copy-start(f32[394]{0:T(512)S(1)} %broadcast_multiply_fusion.13) | copy-start | bytes 4732
  154.7 72.3 %copy-start.100 = (f32[512]{0:T(512)}, f32[512]{0:T(512)S(1)}, u32[]{:S(2)}) copy-start(f32[512]{0:T(512)S(1)} %get-tuple-element.41) | copy-start | bytes 6148
  157.5 69.6 %copy-start.92 = (f32[512]{0:T(512)}, f32[512]{0:T(512)S(1)}, u32[]{:S(2)}) copy-start(f32[512]{0:T(512)S(1)} %get-tuple-element.39) | copy-start | bytes 6148
  157.5 86.9 %copy-start.75 = (f32[512]{0:T(512)}, f32[512]{0:T(512)S(1)}, u32[]{:S(2)}) copy-start(f32[512]{0:T(512)S(1)} %get-tuple-element.38) | copy-start | bytes 6148
  157.5 69.5 %copy-start.96 = (f32[394]{0:T(512)}, f32[394]{0:T(512)S(1)}, u32[]{:S(2)}) copy-start(f32[394]{0:T(512)S(1)} %add_rsqrt_fusion.3) | copy-start | bytes 4732
  227.0 16.6 copy-start.24
  244.1 391.2 %copy-start.2 = (f32[394,512]{1,0:T(8,128)}, f32[394,512]{1,0:T(8,128)S(1)}, u32[]{:S(2)}) copy-start(f32[394,512]{1,0:T(8,128)S(1)} %get-tuple-element.79) | copy-start | bytes 2420740
  244.6 378.2 %copy-start.18 = (bf16[394,512]{1,0:T(8,128)(2,1)}, bf16[394,512]{1,0:T(8,128)(2,1)S(1)}, u32[]{:S(2)}) copy-start(bf16[394,512]{1,0:T(8,128)(2,1)S(1)} %add_convert_fusion.2) | copy-start | bytes 1210372
  315.1 309.5 %all-to-all-start.1 = ((bf16[8,197,512]{2,1,0:T(8,128)(2,1)}), bf16[8,197,512]{2,1,0:T(8,128)(2,1)}, u32[]{:S(2)}, u32[]{:S(2)}) async-start(bf16[8,197,512]{2,1,0:T(8,128)(2,1)} %reshape.534), calls=%async_computation.1 | async-start | bytes 3276800 | tf_op jit(solution)/shard_map/all_to_all | solution.py:162
  319.4 316.4 %all-gather.15.cloned.1.call-start = ((), (), s32[]{:S(2)}) async-start(), calls=%async_computation.27 | async-start | bytes 1622016 | tf_op jit(solution)/shard_map/all_gather | solution.py:129
  413.5 211.1 %copy-start.50 = (bf16[1,512,8]{1,2,0:T(8,128)(2,1)}, bf16[1,512,8]{1,2,0:T(8,128)(2,1)S(1)}, u32[]{:S(2)}) copy-start(bf16[1,512,8]{1,2,0:T(8,128)(2,1)S(1)} %copy.232) | copy-start | bytes 24580
  546.3 84.2 %copy-start.59 = (s32[1024]{0:T(1024)}, s32[1024]{0:T(1024)S(1)}, u32[]{:S(2)}) copy-start(s32[1024]{0:T(1024)S(1)} %pad_clamp_fusion.1) | copy-start | bytes 12292
  546.3 115.4 %copy-start.90 = (s32[788]{0:T(1024)}, s32[788]{0:T(1024)S(1)}, u32[]{:S(2)}) copy-start(s32[788]{0:T(1024)S(1)} %fusion.125) | copy-start | bytes 9460
  549.1 86.7 %copy-start.94 = (f32[512]{0:T(512)}, f32[512]{0:T(512)S(1)}, u32[]{:S(2)}) copy-start(f32[512]{0:T(512)S(1)} %get-tuple-element.37) | copy-start | bytes 6148
  551.8 84.0 %copy-start.84 = (f32[512]{0:T(512)}, f32[512]{0:T(512)S(1)}, u32[]{:S(2)}) copy-start(f32[512]{0:T(512)S(1)} %get-tuple-element.35) | copy-start | bytes 6148
  551.8 103.9 %copy-start.69 = (f32[512]{0:T(512)}, f32[512]{0:T(512)S(1)}, u32[]{:S(2)}) copy-start(f32[512]{0:T(512)S(1)} %get-tuple-element.34) | copy-start | bytes 6148
  655.5 16.7 copy-start.55
  655.7 16.4 copy-start.73
  672.2 115.7 %all-to-all-start.2 = ((bf16[8,197,512]{2,1,0:T(8,128)(2,1)}), bf16[8,197,512]{2,1,0:T(8,128)(2,1)}, u32[]{:S(2)}, u32[]{:S(2)}) async-start(bf16[8,197,512]{2,1,0:T(8,128)(2,1)} %reshape.540), calls=%async_computation.2 | async-start | bytes 3276800 | tf_op jit(solution)/shard_map/all_to_all | solution.py:157
  787.9 38.7 %all-to-all-start.4 = ((bf16[8,197,512]{2,1,0:T(8,128)(2,1)}), bf16[8,197,512]{2,1,0:T(8,128)(2,1)}, u32[]{:S(2)}, u32[]{:S(2)}) async-start(bf16[8,197,512]{2,1,0:T(8,128)(2,1)} %reshape.544), calls=%async_computation.4 | async-start | bytes 3276800 | tf_op jit(solution)/shard_map/all_to_all | solution.py:228
  829.6 16.9 copy-start.104
  854.8 40.9 %all-to-all-start.5 = ((bf16[8,197,512]{2,1,0:T(8,128)(2,1)}), bf16[8,197,512]{2,1,0:T(8,128)(2,1)}, u32[]{:S(2)}, u32[]{:S(2)}) async-start(bf16[8,197,512]{2,1,0:T(8,128)(2,1)} %reshape.546), calls=%async_computation.5 | async-start | bytes 3276800 | tf_op jit(solution)/shard_map/all_to_all | solution.py:242
  867.4 34.6 %copy-start.91 = (s32[788]{0:T(1024)S(1)}, s32[788]{0:T(1024)}, u32[]{:S(2)}) copy-start(s32[788]{0:T(1024)} %copy-done.90) | copy-start | bytes 9460
  895.7 42.1 %all-to-all-start.3 = ((bf16[8,197,512]{2,1,0:T(8,128)(2,1)}), bf16[8,197,512]{2,1,0:T(8,128)(2,1)}, u32[]{:S(2)}, u32[]{:S(2)}) async-start(bf16[8,197,512]{2,1,0:T(8,128)(2,1)} %reshape.542), calls=%async_computation.3 | async-start | bytes 3276800 | tf_op jit(solution)/shard_map/all_to_all | solution.py:162
  987.1 89.8 %copy-start.12 = (f32[394,512]{1,0:T(8,128)}, f32[394,512]{1,0:T(8,128)S(1)}, u32[]{:S(2)}) copy-start(f32[394,512]{1,0:T(8,128)S(1)} %multiply_add_fusion.1) | copy-start | bytes 2420740
  1070.5 42.4 %all-to-all-start.7 = ((bf16[8,197,512]{2,1,0:T(8,128)(2,1)}), bf16[8,197,512]{2,1,0:T(8,128)(2,1)}, u32[]{:S(2)}, u32[]{:S(2)}) async-start(bf16[8,197,512]{2,1,0:T(8,128)(2,1)} %reshape.551), calls=%async_computation.7 | async-start | bytes 3276800 | tf_op jit(solution)/shard_map/all_to_all | solution.py:242
  1074.9 144.3 %reduce-scatter.39.cloned.1.call-start = ((), (), s32[]{:S(2)}) async-start(), calls=%async_computation.29 | async-start | bytes 270336
  1075.9 274.9 %reduce-scatter.43.cloned.1.call-start = ((), (), s32[]{:S(2)}) async-start(), calls=%async_computation.31 | async-start | bytes 270336
  1076.9 405.7 %reduce-scatter.47.cloned.1.call-start = ((), (), s32[]{:S(2)}) async-start(), calls=%async_computation.33 | async-start | bytes 270336
  1077.9 36.8 %copy-start.60 = (s32[1024]{0:T(1024)S(1)}, s32[1024]{0:T(1024)}, u32[]{:S(2)}) copy-start(s32[1024]{0:T(1024)} %copy-done.59) | copy-start | bytes 12292
  1079.2 535.4 %reduce-scatter.45.cloned.1.call-start = ((), (), s32[]{:S(2)}) async-start(), calls=%async_computation.32 | async-start | bytes 270336
  1080.7 665.8 %reduce-scatter.37.cloned.1.call-start = ((), (), s32[]{:S(2)}) async-start(), calls=%async_computation.28 | async-start | bytes 270336
  1145.5 733.1 %reduce-scatter.41.cloned.1.call-start = ((), (), s32[]{:S(2)}) async-start(), calls=%async_computation.30 | async-start | bytes 270336
  1146.5 866.3 %reduce-scatter.31.cloned.1.call-start = ((), (), s32[]{:S(2)}) async-start(), calls=%async_computation.23 | async-start | bytes 1081344 | tf_op jit(solution)/shard_map/reduce_scatter | solution.py:277
  1149.1 997.3 %reduce-scatter.29.cloned.1.call-start = ((), (), s32[]{:S(2)}) async-start(), calls=%async_computation.22 | async-start | bytes 1081344 | tf_op jit(solution)/shard_map/reduce_scatter | solution.py:277
  1150.6 1099.1 %reduce-scatter.27.cloned.1.call-start = ((), (), s32[]{:S(2)}) async-start(), calls=%async_computation.21 | async-start | bytes 3244032 | tf_op jit(solution)/shard_map/reduce_scatter | solution.py:276
  1155.1 1200.4 %reduce-scatter.25.cloned.1.call-start = ((), (), s32[]{:S(2)}) async-start(), calls=%async_computation.20 | async-start | bytes 3244032 | tf_op jit(solution)/shard_map/reduce_scatter | solution.py:276
  1159.5 1242.0 %reduce-scatter.33.cloned.1.call-start = ((), (), s32[]{:S(2)}) async-start(), calls=%async_computation.24 | async-start | bytes 5242880 | tf_op jit(solution)/shard_map/reduce_scatter | solution.py:295
  1176.6 1272.0 %reduce-scatter.35.cloned.1.call-start = ((), (), s32[]{:S(2)}) async-start(), calls=%async_computation.25 | async-start | bytes 5242880 | tf_op jit(solution)/shard_map/reduce_scatter | solution.py:298
  1194.1 458.7 %copy-start.102 = (f32[2,8]{1,0:T(2,128)S(1)}, f32[2,8]{1,0:T(2,128)}, u32[]{:S(2)}) copy-start(f32[2,8]{1,0:T(2,128)} %param.20) | copy-start | bytes 196
  1194.1 458.9 %copy-start.47 = (bf16[2,16,1536]{2,1,0:T(8,128)(2,1)S(1)}, bf16[2,16,1536]{2,1,0:T(8,128)(2,1)}, u32[]{:S(2)}) copy-start(bf16[2,16,1536]{2,1,0:T(8,128)(2,1)} %param.14) | copy-start | bytes 294916
  1194.1 459.6 %copy-start.44 = (f32[394,512]{1,0:T(8,128)S(1)}, f32[394,512]{1,0:T(8,128)}, u32[]{:S(2)}) copy-start(f32[394,512]{1,0:T(8,128)} %get-tuple-element.97) | copy-start | bytes 2420740
  1652.8 751.6 %copy-start.98 = (f32[2,8]{1,0:T(2,128)}, f32[2,8]{1,0:T(2,128)S(1)}, u32[]{:S(2)}) copy-start(f32[2,8]{1,0:T(2,128)S(1)} %pmax.7) | copy-start | bytes 196
  (81 other events, 383.0 us)
Sparse Core Ops, SparseCore 0:
  11.6 58.1 all-gather.12
  323.8 62.8 all-gather.14
  1078.0 141.1 reduce-scatter.38
  1221.4 129.3 reduce-scatter.42
  1352.8 129.7 reduce-scatter.46
  1484.8 129.7 reduce-scatter.44
  1616.8 129.7 reduce-scatter.36
  1748.8 129.7 reduce-scatter.40
  1881.5 131.2 reduce-scatter.30
  2015.0 131.3 reduce-scatter.28
  2151.8 97.8 reduce-scatter.26
  2254.9 100.5 reduce-scatter.24
  2358.0 43.4 reduce-scatter.32
  2404.0 44.4 reduce-scatter.34
where the time goes:
time: 2470 us; the launch traced here: 2460 us
  waiting for transfers between devices  1300 us (53%)
  blocking collectives  706 us (29%)
  local copies, waits for them, and re-layouts  181 us (7%)
  matrix products  151 us (6%)
  other arithmetic  74.1 us (3%)
  starting transfers between devices  27.5 us (1%)
    unnamed x20, waiting for transfers between devices  642 us
    reduce_scatter x2, waiting for transfers between devices, body(): lax.psum_scatter(grad_wo, ('dp', 'expert'), scatter_dimension=0, tiled=True)  265 us
    reduce_scatter x2, waiting for transfers between devices, body(): lax.psum_scatter(grad_wqkv, ('dp', 'expert'), scatter_dimension=0, tiled=...  208 us
    all_gather x2, blocking collectives, body(): lax.all_gather(w_router[layer_at], ('dp', 'expert'), axis=0, tiled=True)  178 us
    all_gather x2, blocking collectives, body(): lax.all_gather(w_o[layer_at], ('dp', 'expert'), axis=0, tiled=True)  141 us
    all_gather x2, blocking collectives, body(): lax.all_gather(norm_biases[layer_at], ('dp', 'expert'), axis=1, tiled=True)  136 us
    all_gather x2, blocking collectives, body(): lax.all_gather(norm_gains[layer_at], ('dp', 'expert'), axis=1, tiled=True)  132 us
    all_to_all x2, waiting for transfers between devices, body(): lax.all_to_all(returning, 'expert', split_axis=0, concat_axis=0, tiled=True)  57.3 us
  transfers between devices with their start and end apart: 20, of which 16 were waited for; matrix products, arithmetic and copies ran while one was open for 8% of the time, Pallas kernels for 0%

commit v1 on v0

v1 whole, which is shorter than its diff:
```python
import functools

import jax
import jax.numpy as jnp
import numpy as np
from jax import lax
from jax.experimental import pallas as pl
from jax.experimental.pallas import tpu as pltpu
from jax.sharding import Mesh
from jax.sharding import PartitionSpec as P

HEADS = 8
HEAD_DIM = 64
SEQ = 197
TOP = 2
LAYERS = 2
EPSILON = 1e-06
BF = jnp.bfloat16
F32 = jnp.float32
LANES = 128
PIECES = 4
VMEM = 50 * 1024 * 1024


def up16(size):
    return -(-size // 16) * 16


def dot(a, b):
    return jnp.dot(a, b, preferred_element_type=F32)


def dot_last(a, b):
    return lax.dot_general(a, b, (((1,), (1,)), ((), ())), preferred_element_type=F32)


def dot_first(a, b):
    return lax.dot_general(a, b, (((0,), (0,)), ((), ())), preferred_element_type=F32)


def lane_of(rows, lanes=LANES):
    return lax.broadcasted_iota(jnp.int32, (rows, lanes), 1)


def row_of(rows, lanes=LANES):
    return lax.broadcasted_iota(jnp.int32, (rows, lanes), 0)


def normalize(values):
    center = values - jnp.mean(values, axis=-1, keepdims=True)
    inverse = lax.rsqrt(jnp.mean(center * center, axis=-1, keepdims=True) + EPSILON)
    return center * inverse, inverse


def norm_backward(upstream, normed, inverse, gain_row):
    scaled = upstream * gain_row
    mean_plain = jnp.mean(scaled, axis=-1, keepdims=True)
    mean_normed = jnp.mean(scaled * normed, axis=-1, keepdims=True)
    return inverse * (scaled - mean_plain - normed * mean_normed)


def norm_rows(tail, experts):
    picks = (lane_of(8) == row_of(8) + experts).astype(F32).astype(BF)
    return dot_last(picks, tail)


def places_kernel(experts, capacity, cols_ref, rows_ref, *out_refs):
    tokens = cols_ref.shape[1]
    slots = experts * capacity
    square_row = lax.broadcasted_iota(jnp.int32, (tokens, tokens), 0)
    square_col = lax.broadcasted_iota(jnp.int32, (tokens, tokens), 1)
    earlier = (square_col < square_row).astype(F32).astype(BF)
    later = (square_row < square_col).astype(F32).astype(BF)
    wide = max(16, experts)
    for layer_at in range(LAYERS):
        to_tokens, to_slots = out_refs[4 * layer_at : 4 * layer_at + 2], out_refs[
            4 * layer_at + 2 : 4 * layer_at + 4
        ]
        cols = cols_ref[layer_at]
        first, second = cols[:, 0:1], cols[:, 1:2]
        lane = lane_of(tokens)
        matches = jnp.where((lane == first) | (lane == second), 1.0, 0.0)
        before = dot(earlier, matches.astype(BF))
        slot_lane = lax.broadcasted_iota(jnp.int32, (tokens, slots), 1)
        for chosen, out_ref in zip((first, second), to_tokens):
            rank = jnp.sum(jnp.where(lane == chosen, before, 0.0), axis=1, keepdims=True)
            slot = chosen * capacity + rank.astype(jnp.int32)
            out_ref[...] = jnp.where(slot_lane == slot, 1.0, 0.0).astype(BF)
        rows = rows_ref[layer_at]
        first, second = rows[0:1], rows[1:2]
        which = lax.broadcasted_iota(jnp.int32, (wide, tokens), 0)
        matches = jnp.where((which == first) | (which == second), 1.0, 0.0)
        before = dot(matches.astype(BF), later)
        slot_row = lax.broadcasted_iota(jnp.int32, (slots, tokens), 0)
        for chosen, out_ref in zip((first, second), to_slots):
            rank = jnp.sum(jnp.where(which == chosen, before, 0.0), axis=0, keepdims=True)
            slot = chosen * capacity + rank.astype(jnp.int32)
            out_ref[...] = jnp.where(slot_row == slot, 1.0, 0.0).astype(BF)


def call(kernel, out_shapes, args, flops, scratch=()):
    moved = sum(a.size * a.dtype.itemsize for a in args) + sum(
        int(np.prod(o.shape)) * o.dtype.itemsize for o in out_shapes
    )
    return pl.pallas_call(
        kernel,
        out_shape=out_shapes,
        scratch_shapes=list(scratch),
        compiler_params=pltpu.CompilerParams(vmem_limit_bytes=VMEM),
        cost_estimate=pl.CostEstimate(
            flops=int(flops), bytes_accessed=int(moved), transcendentals=0
        ),
    )(*args)


def shape(dims, dtype):
    return jax.ShapeDtypeStruct(dims, dtype)


def half_masks():
    lane = lane_of(1)
    return (
        jnp.where(lane < HEAD_DIM, 1.0, 0.0).astype(BF),
        jnp.where(lane < HEAD_DIM, 0.0, 1.0).astype(BF),
    )


def dense_forward_kernel(experts, images, combine, last, *refs):
    refs = list(refs)
    take = lambda: refs.pop(0)
    x_ref = take()
    if combine:
        back_ref, take_first, take_second, gates_before = take(), take(), take(), take()
    full_ref, to_first, to_second, cols_ref = take(), take(), take(), take()
    if last:
        cot_ref = take()
    if combine:
        x_out, first_out, second_out = take(), take(), take()
    x1_out, qkv_out, mixed_out, lse_out, probs_out, gates_out, send_out, top_out = (
        take() for _ in range(8)
    )
    if last:
        send_grad_out = take()
    tokens, width = x_ref.shape
    rows_of = tokens // images
    x = x_ref[...]
    if combine:
        back = back_ref[...]
        first = dot(take_first[...], back)
        second = dot(take_second[...], back)
        gates = gates_before[...]
        x = x + (gates[:, 0:1] * first + gates[:, 1:2] * second)
        x_out[...] = x
        first_out[...] = first.astype(BF)
        second_out[...] = second.astype(BF)
    tail = full_ref[:, 4 * width :]
    norms = norm_rows(tail, experts)
    unit, _ = normalize(x)
    n1 = (unit * norms[0:1] + norms[2:3]).astype(BF)
    qkv_out[...] = dot(n1, full_ref[:, : 3 * width]).astype(BF)
    masks = half_masks()
    key_at = lax.broadcasted_iota(jnp.int32, (rows_of, rows_of), 1)
    query_at = lax.broadcasted_iota(jnp.int32, (rows_of, 1), 0)
    lane = lane_of(rows_of)
    top_lane = lane_of(8)
    tops = jnp.full((8, LANES), -jnp.inf, F32)
    scale = HEAD_DIM**-0.5
    for image in range(images):
        rows = slice(image * rows_of, (image + 1) * rows_of)
        lse = jnp.zeros((rows_of, LANES), F32)
        for pair in range(HEADS // 2):
            at = pair * LANES
            q = qkv_out[rows, at : at + LANES]
            k = qkv_out[rows, width + at : width + at + LANES]
            v = qkv_out[rows, 2 * width + at : 2 * width + at + LANES]
            mixed = None
            for half in range(2):
                scores = dot_last(q * masks[half], k) * scale
                scores = jnp.where(key_at < SEQ, scores, -jnp.inf)
                highest = jnp.max(scores, axis=-1, keepdims=True)
                top = jnp.max(
                    jnp.where(query_at < SEQ, highest, -jnp.inf), axis=0, keepdims=True
                )
                weights = jnp.exp(scores - highest)
                total = jnp.sum(weights, axis=-1, keepdims=True)
                weights = (weights * (1.0 / total)).astype(BF)
                part = dot(weights, v * masks[half])
                mixed = part if mixed is None else mixed + part
                head = 2 * pair + half
                lse = jnp.where(lane == head, highest + jnp.log(total), lse)
                tops = jnp.where(top_lane == head, jnp.maximum(tops, top), tops)
            mixed_out[rows, at : at + LANES] = mixed.astype(BF)
        lse_out[rows, :] = lse
    top_out[...] = tops
    x1 = x + dot(mixed_out[...], full_ref[:, 3 * width : 4 * width])
    x1_out[...] = x1
    unit, _ = normalize(x1)
    n2 = (unit * norms[1:2] + norms[3:4]).astype(BF)
    lane = lane_of(tokens)
    logits = jnp.where(lane < experts, dot(n2, tail), -jnp.inf)
    probs = jnp.exp(logits - jnp.max(logits, axis=-1, keepdims=True))
    probs = probs / jnp.sum(probs, axis=-1, keepdims=True)
    probs_out[...] = probs
    first, second = cols_ref[:, 0:1], cols_ref[:, 1:2]
    picked = [
        jnp.sum(jnp.where(lane == chosen, probs, 0.0), axis=1, keepdims=True)
        for chosen in (first, second)
    ]
    total = jnp.where(first >= 0, picked[0] + picked[1], 1.0)
    gates = [one / total for one in picked]
    packed = jnp.zeros((tokens, LANES), F32)
    for at, column in enumerate((gates[0], gates[1], total, picked[0], picked[1])):
        packed = jnp.where(lane == at, column, packed)
    gates_out[...] = packed
    send_out[...] = (dot(to_first[...], n2) + dot(to_second[...], n2)).astype(BF)
    if last:
        cot = cot_ref[...]
        send_grad_out[...] = (
            dot(to_first[...], (gates[0] * cot).astype(BF))
            + dot(to_second[...], (gates[1] * cot).astype(BF))
        ).astype(BF)


def expert_forward_kernel(rows_ref, win_ref, wout_ref, active_out, slope_out, out_ref, sums):
    at = pl.program_id(0)
    chunk = rows_ref.shape[0] // 4
    factor = (2.0 / np.pi) ** 0.5

    @pl.loop(0, 4)
    def _(step):
        rows = pl.ds(pl.multiple_of(step * chunk, 16), chunk)
        hidden = dot(rows_ref[rows, :], win_ref[...])
        square = hidden * hidden
        bend = jnp.tanh(factor * hidden * (1.0 + 0.044715 * square))
        half = 0.5 * (1.0 + bend)
        active = (hidden * half).astype(BF)
        active_out[rows, :] = active
        slope_out[rows, :] = (
            half
            + (0.5 * factor)
            * hidden
            * (1.0 - bend * bend)
            * (1.0 + (3 * 0.044715) * square)
        ).astype(BF)
        part = dot(active, wout_ref[...])

        @pl.when(at == 0)
        def _():
            sums[rows, :] = part

        @pl.when(at > 0)
        def _():
            sums[rows, :] += part

        @pl.when(at == PIECES - 1)
        def _():
            out_ref[rows, :] = sums[rows, :].astype(BF)


def expert_forward(rows_in, weight_in, weight_out):
    slots, width = rows_in.shape
    hidden_units = weight_in.shape[1]
    block = hidden_units // PIECES
    return pl.pallas_call(
        expert_forward_kernel,
        grid=(PIECES,),
        in_specs=[
            pl.BlockSpec((slots, width), lambda i: (0, 0)),
            pl.BlockSpec((width, block), lambda i: (0, i)),
            pl.BlockSpec((block, width), lambda i: (i, 0)),
        ],
        out_specs=[
            pl.BlockSpec((slots, block), lambda i: (0, i)),
            pl.BlockSpec((slots, block), lambda i: (0, i)),
            pl.BlockSpec((slots, width), lambda i: (0, 0)),
        ],
        out_shape=[
            shape((slots, hidden_units), BF),
            shape((slots, hidden_units), BF),
            shape((slots, width), BF),
        ],
        scratch_shapes=[pltpu.VMEM((slots, width), F32)],
        compiler_params=pltpu.CompilerParams(vmem_limit_bytes=VMEM),
        cost_estimate=pl.CostEstimate(
            flops=4 * slots * width * hidden_units,
            bytes_accessed=slots * (hidden_units * 4 + width * 4) + 4 * width * hidden_units,
            transcendentals=slots * hidden_units,
        ),
    )(rows_in, weight_in, weight_out)


def expert_backward_kernel(grad_ref, slope_ref, win_ref, wout_ref, hidden_out, out_ref, sums):
    at = pl.program_id(0)
    chunk = grad_ref.shape[0] // 4

    @pl.loop(0, 4)
    def _(step):
        rows = pl.ds(pl.multiple_of(step * chunk, 16), chunk)
        grad_active = dot_last(grad_ref[rows, :], wout_ref[...])
        grad_hidden = (grad_active * slope_ref[rows, :].astype(F32)).astype(BF)
        hidden_out[rows, :] = grad_hidden
        part = dot_last(grad_hidden, win_ref[...])

        @pl.when(at == 0)
        def _():
            sums[rows, :] = part

        @pl.when(at > 0)
        def _():
            sums[rows, :] += part

        @pl.when(at == PIECES - 1)
        def _():
            out_ref[rows, :] = sums[rows, :].astype(BF)


def expert_backward(grad_rows, slope, weight_in, weight_out):
    slots, width = grad_rows.shape
    hidden_units = weight_in.shape[1]
    block = hidden_units // PIECES
    return pl.pallas_call(
        expert_backward_kernel,
        grid=(PIECES,),
        in_specs=[
            pl.BlockSpec((slots, width), lambda i: (0, 0)),
            pl.BlockSpec((slots, block), lambda i: (0, i)),
            pl.BlockSpec((width, block), lambda i: (0, i)),
            pl.BlockSpec((block, width), lambda i: (i, 0)),
        ],
        out_specs=[
            pl.BlockSpec((slots, block), lambda i: (0, i)),
            pl.BlockSpec((slots, width), lambda i: (0, 0)),
        ],
        out_shape=[shape((slots, hidden_units), BF), shape((slots, width), BF)],
        scratch_shapes=[pltpu.VMEM((slots, width), F32)],
        compiler_params=pltpu.CompilerParams(vmem_limit_bytes=VMEM),
        cost_estimate=pl.CostEstimate(
            flops=4 * slots * width * hidden_units,
            bytes_accessed=slots * (hidden_units * 4 + width * 4) + 4 * width * hidden_units,
            transcendentals=0,
        ),
    )(grad_rows, slope, weight_in, weight_out)


def expert_weights_kernel(rows_ref, hidden_ref, active_ref, grad_ref, in_out, out_out):
    in_out[0] = dot_first(rows_ref[...], hidden_ref[...]).astype(BF)
    out_out[0] = dot_first(active_ref[...], grad_ref[...]).astype(BF)


def expert_weights(rows_in, grad_hidden, active, grad_rows, pieces):
    slots, width = rows_in.shape
    hidden_units = active.shape[1]
    block = hidden_units // pieces
    return pl.pallas_call(
        expert_weights_kernel,
        grid=(pieces,),
        in_specs=[
            pl.BlockSpec((slots, width), lambda i: (0, 0)),
            pl.BlockSpec((slots, block), lambda i: (0, i)),
            pl.BlockSpec((slots, block), lambda i: (0, i)),
            pl.BlockSpec((slots, width), lambda i: (0, 0)),
        ],
        out_specs=[
            pl.BlockSpec((1, width, block), lambda i: (i, 0, 0)),
            pl.BlockSpec((1, block, width), lambda i: (i, 0, 0)),
        ],
        out_shape=[shape((pieces, width, block), BF), shape((pieces, block, width), BF)],
        compiler_params=pltpu.CompilerParams(vmem_limit_bytes=VMEM),
        cost_estimate=pl.CostEstimate(
            flops=4 * slots * width * hidden_units,
            bytes_accessed=slots * (hidden_units * 4 + width * 4) + 4 * width * hidden_units,
            transcendentals=0,
        ),
    )(rows_in, grad_hidden, active, grad_rows)


def dense_backward_kernel(experts, images, last, first_layer, *refs):
    refs = list(refs)
    take = lambda: refs.pop(0)
    g_ref, rows_ref, take_first, take_second = take(), take(), take(), take()
    if last:
        out_rows_ref = take()
    else:
        first_ref, second_ref = take(), take()
    probs_ref, gates_ref, cols_ref, x_ref, x1_ref = (take() for _ in range(5))
    full_ref, qkv_ref, mixed_ref, lse_ref = (take() for _ in range(4))
    if not first_layer:
        to_first, to_second, gates_below = take(), take(), take()
    g_out, weights_out = take(), take()
    if not first_layer:
        send_out = take()
    if last:
        act_out = take()
    grad_qkv = take()
    tokens, width = g_ref.shape
    rows_of = tokens // images
    g = g_ref[...]
    gates = gates_ref[...]
    x1 = x1_ref[...]
    if last:
        out_rows = out_rows_ref[...]
        first = dot(take_first[...], out_rows)
        second = dot(take_second[...], out_rows)
        act_out[...] = x1 + (gates[:, 0:1] * first + gates[:, 1:2] * second)
    else:
        first = first_ref[...].astype(F32)
        second = second_ref[...].astype(F32)
    grad_gates = [jnp.sum(g * one, axis=1, keepdims=True) for one in (first, second)]
    weighted = grad_gates[0] * gates[:, 0:1] + grad_gates[1] * gates[:, 1:2]
    amounts = [
        (grad_gates[at] - weighted) / gates[:, 2:3] * gates[:, 3 + at : 4 + at]
        for at in range(TOP)
    ]
    lane = lane_of(tokens)
    chosen = [jnp.where(lane == cols_ref[:, at : at + 1], amounts[at], 0.0) for at in range(TOP)]
    grad_logits = (
        (chosen[0] + chosen[1]) - probs_ref[...] * (amounts[0] + amounts[1])
    ).astype(BF)
    tail = full_ref[:, 4 * width :]
    norms = norm_rows(tail, experts)
    rows = rows_ref[...]
    grad_n2 = (
        dot(take_first[...], rows) + dot(take_second[...], rows) + dot_last(grad_logits, tail)
    )
    unit2, inverse2 = normalize(x1)
    n2 = (unit2 * norms[1:2] + norms[3:4]).astype(BF)
    grad_x1 = g + norm_backward(grad_n2, unit2, inverse2, norms[1:2])
    grad_attn = grad_x1.astype(BF)
    grad_mixed = dot_last(grad_attn, full_ref[:, 3 * width : 4 * width]).astype(BF)
    masks = half_masks()
    key_at = lax.broadcasted_iota(jnp.int32, (rows_of, rows_of), 1)
    scale = HEAD_DIM**-0.5
    for image in range(images):
        rows = slice(image * rows_of, (image + 1) * rows_of)
        for pair in range(HEADS // 2):
            at = pair * LANES
            q = qkv_ref[rows, at : at + LANES]
            k = qkv_ref[rows, width + at : width + at + LANES]
            v = qkv_ref[rows, 2 * width + at : 2 * width + at + LANES]
            gm = grad_mixed[rows, at : at + LANES]
            sums = [None] * 3
            for half in range(2):
                head = 2 * pair + half
                mask = masks[half]
                scores = dot_last(q * mask, k) * scale
                weights = jnp.exp(scores - lse_ref[rows, head : head + 1])
                weights = jnp.where(key_at < SEQ, weights, 0.0)
                grad_weights = dot_last(gm * mask, v)
                inner = jnp.sum(grad_weights * weights, axis=-1, keepdims=True)
                grad_scores = (weights * (grad_weights - inner)).astype(BF)
                parts = (
                    dot(grad_scores, k * mask),
                    dot_first(grad_scores, q * mask),
                    dot_first(weights.astype(BF), gm * mask),
                )
                sums = [b if a is None else a + b for a, b in zip(sums, parts)]
            grad_qkv[rows, at : at + LANES] = (sums[0] * scale).astype(BF)
            grad_qkv[rows, width + at : width + at + LANES] = (sums[1] * scale).astype(BF)
            grad_qkv[rows, 2 * width + at : 2 * width + at + LANES] = sums[2].astype(BF)
    unit1, inverse1 = normalize(x_ref[...])
    n1 = (unit1 * norms[0:1] + norms[2:3]).astype(BF)
    grad_n1 = dot_last(grad_qkv[...], full_ref[:, : 3 * width])
    g_below = grad_x1 + norm_backward(grad_n1, unit1, inverse1, norms[0:1])
    g_out[...] = g_below
    if not first_layer:
        gates = gates_below[...]
        send_out[...] = (
            dot(to_first[...], (gates[:, 0:1] * g_below).astype(BF))
            + dot(to_second[...], (gates[:, 1:2] * g_below).astype(BF))
        ).astype(BF)
    weights_out[:, : 3 * width] = dot_first(n1, grad_qkv[...]).astype(BF)
    weights_out[:, 3 * width : 4 * width] = dot_first(mixed_ref[...], grad_attn).astype(BF)
    row = lax.broadcasted_iota(jnp.int32, (8, width), 0)
    norm_grads = jnp.zeros((8, width), F32)
    for at, total in enumerate((grad_n1 * unit1, grad_n2 * unit2, grad_n1, grad_n2)):
        norm_grads = jnp.where(row == at, jnp.sum(total, axis=0, keepdims=True), norm_grads)
    picks = (lane_of(8) == row_of(8) + experts).astype(F32).astype(BF)
    weights_out[:, 4 * width :] = (
        dot_first(n2, grad_logits) + dot_first(norm_grads.astype(BF), picks)
    ).astype(BF)


def other(values, axis):
    return lax.ppermute(values, axis, [(0, 1), (1, 0)])


def across(values, core_axis, axis):
    if axis < core_axis:
        return lax.ppermute(values, (axis, core_axis), [(1, 3), (3, 1)])
    return lax.ppermute(values, (core_axis, axis), [(2, 3), (3, 2)])


def expert_moved(weight, split_at, dp_axes, ex_axes):
    row_axes, core_axis = dp_axes[:-1], dp_axes[-1]
    count = 2 ** len(row_axes)
    size = weight.shape[split_at] // count
    place = lax.axis_index(row_axes) if row_axes else 0
    own = [
        lax.dynamic_slice_in_dim(weight, (place ^ p) * size, size, split_at)
        for p in range(count)
    ]
    first = lax.axis_index(core_axis) == 0
    got = [across(own[0], core_axis, ex_axes[0])]
    for axis in row_axes[::-1]:
        got = got + [across(one, core_axis, axis) for one in got]
    return jnp.concatenate(
        [jnp.where(first, a, b) for a, b in zip(own, got)], axis=split_at
    )


def expert_returned(pieces, dp_axes, ex_axes):
    row_axes, core_axis = dp_axes[:-1], dp_axes[-1]
    pieces = pieces.reshape((2,) * len(row_axes) + (2,) + pieces.shape[1:])
    for axis in row_axes:
        pieces = add_low(pieces[0], other(pieces[1], axis))
    moved = across(pieces, core_axis, ex_axes[0])
    core = lax.axis_index(core_axis)
    mine = jnp.where(core == 0, pieces, moved)
    keep = lax.dynamic_index_in_dim(mine, core, 0, keepdims=False)
    send = lax.dynamic_index_in_dim(mine, 1 - core, 0, keepdims=False)
    return keep.astype(F32) + other(send, core_axis).astype(F32)


def add_low(a, b):
    return (a.astype(F32) + b.astype(F32)).astype(BF)


def gather_all(shard, axes, order):
    whole = shard[None]
    for axis in order:
        theirs = other(whole, axis)
        mine_first = lax.axis_index(axis) == 0
        whole = jnp.stack(
            [jnp.where(mine_first, whole, theirs), jnp.where(mine_first, theirs, whole)]
        )
    whole = whole.reshape((2,) * len(axes) + shard.shape)
    places = tuple(order[::-1].index(axis) for axis in axes)
    whole = whole.transpose(places + tuple(range(len(axes), whole.ndim)))
    return whole.reshape((-1,) + shard.shape[1:])


def scatter_sum(values, axes, order):
    left = list(axes)
    values = values.reshape((2,) * len(axes) + (-1,) + values.shape[1:])
    for axis in order:
        at = left.index(axis)
        mine = lax.axis_index(axis)
        keep = lax.dynamic_index_in_dim(values, mine, at, keepdims=False)
        send = lax.dynamic_index_in_dim(values, 1 - mine, at, keepdims=False)
        values = keep.astype(F32) + other(send, axis).astype(F32)
        left.remove(axis)
        if left:
            values = values.astype(BF)
    return values


def body(
    dp_axes,
    ex_axes,
    x_in,
    norm_gains,
    norm_biases,
    w_qkv,
    w_o,
    w_router,
    w_in,
    w_out,
    routes,
    threshold,
    cotangent,
):
    axes = dp_axes + ex_axes
    group = dp_axes[-1:] + ex_axes[1:]
    order_out = ex_axes[::-1][1:] + ex_axes[-1:] + dp_axes
    order_in = dp_axes[::-1] + ex_axes[::-1]
    experts = 2 ** len(ex_axes)
    parts = 2 ** len(dp_axes)
    tokens, width = x_in.shape
    images = tokens // SEQ
    padded = up16(SEQ)
    capacity = up16(4 * tokens // experts)
    slots = experts * capacity
    total = images * padded

    def pad(values, fill=0):
        values = values.reshape((images, SEQ) + values.shape[1:])
        values = jnp.pad(
            values, ((0, 0), (0, padded - SEQ), (0, 0)), constant_values=fill
        )
        return values.reshape((total,) + values.shape[2:])

    def unpad(values):
        return values.reshape(images, padded, -1)[:, :SEQ].reshape(tokens, -1)

    shards = [
        jnp.concatenate(
            [
                w_qkv[at],
                w_o[at],
                w_router[at],
                norm_gains[at].T,
                norm_biases[at].T,
                jnp.zeros((w_o.shape[1], LANES - experts - 4), BF),
            ],
            axis=1,
        )
        for at in range(LAYERS)
    ]
    full = [gather_all(shards[0], axes, order_out)] + [
        lax.all_gather(shards[at], axes, axis=0, tiled=True) for at in range(1, LAYERS)
    ]
    cols = [pad(routes[at], -1) for at in range(LAYERS)]
    shift = lax.axis_index(ex_axes[0]) * (experts // 2)
    route_cols = jnp.stack(
        [pad((routes[at] + shift) % experts, -1) for at in range(LAYERS)]
    )
    weights_in, weights_out = [], []
    for at in range(LAYERS):
        weights_in.append(expert_moved(w_in[at, 0], 1, dp_axes, ex_axes))
        weights_out.append(expert_moved(w_out[at, 0], 0, dp_axes, ex_axes))
    to_and_from = call(
        functools.partial(places_kernel, experts, capacity),
        [shape(s, BF) for s in ((total, slots),) * 2 + ((slots, total),) * 2] * LAYERS,
        (route_cols, route_cols.transpose(0, 2, 1)),
        LAYERS * 4 * total * total * LANES,
    )
    collect = [to_and_from[4 * at : 4 * at + 2] for at in range(LAYERS)]
    spread = [to_and_from[4 * at + 2 : 4 * at + 4] for at in range(LAYERS)]
    cot = pad(cotangent.astype(F32))
    current = pad(x_in.astype(F32))

    def exchange(rows):
        return lax.all_to_all(rows, group, split_axis=0, concat_axis=0, tiled=True)

    dense_flops = 2 * total * width * (4 * width) + 6 * total * slots * width
    kept = []
    tops = []
    back = gates = None
    for at in range(LAYERS):
        combine, last = at > 0, at == LAYERS - 1
        args = [current]
        outs = []
        if combine:
            args += [back, *collect[at - 1], gates]
            outs += [shape((total, width), F32), shape((total, width), BF), shape((total, width), BF)]
        args += [full[at], *spread[at], cols[at]]
        if last:
            args.append(cot)
        outs += [
            shape((total, width), F32),
            shape((total, 3 * width), BF),
            shape((total, width), BF),
            shape((total, LANES), F32),
            shape((total, LANES), F32),
            shape((total, LANES), F32),
            shape((slots, width), BF),
            shape((8, LANES), F32),
        ]
        if last:
            outs.append(shape((slots, width), BF))
        made = list(
            call(
                functools.partial(dense_forward_kernel, experts, images, combine, last),
                outs,
                args,
                dense_flops,
            )
        )
        if combine:
            current, first, second = made[:3]
            made = made[3:]
            kept[-1]["routed"] = (first, second)
        x1, qkv, mixed, lse, probs, gates, send, top = made[:8]
        tops.append(top[0, :HEADS])
        rows = exchange(send)
        if last:
            grad_rows = exchange(made[8])
        active, slope, out_rows = expert_forward(rows, weights_in[at], weights_out[at])
        back = exchange(out_rows)
        kept.append(
            dict(
                x=current,
                x1=x1,
                qkv=qkv,
                mixed=mixed,
                lse=lse,
                probs=probs,
                gates=gates,
                rows=rows,
                active=active,
                slope=slope,
            )
        )
        current = x1
    tops = jnp.pad(jnp.concatenate(tops), (0, LANES - LAYERS * HEADS))
    everyone = 2 ** len(axes)
    tops = lax.all_to_all(
        jnp.broadcast_to(tops, (everyone, LANES)), axes, split_axis=0, concat_axis=0, tiled=True
    )
    head_max = jnp.max(tops, axis=0)[: LAYERS * HEADS].reshape(LAYERS, HEADS)
    upstream = cot
    expert_grads = [None] * LAYERS
    dense_grads = [None] * LAYERS
    for at in reversed(range(LAYERS)):
        own = kept[at]
        last, first_layer = at == LAYERS - 1, at == 0
        grad_hidden, grad_back = expert_backward(
            grad_rows, own["slope"], weights_in[at], weights_out[at]
        )
        grad_back = exchange(grad_back)
        expert_grads[at] = [
            expert_returned(one, dp_axes, ex_axes)
            for one in expert_weights(
                own["rows"], grad_hidden, own["active"], grad_rows, parts
            )
        ]
        args = [upstream, grad_back, *collect[at]]
        if last:
            args.append(back)
        else:
            args += own["routed"]
        args += [own["probs"], own["gates"], cols[at], own["x"], own["x1"]]
        args += [full[at], own["qkv"], own["mixed"], own["lse"]]
        outs = [shape((total, width), F32), shape((width, 4 * width + LANES), BF)]
        if not first_layer:
            args += [*spread[at - 1], kept[at - 1]["gates"]]
            outs.append(shape((slots, width), BF))
        if last:
            outs.append(shape((total, width), F32))
        made = list(
            call(
                functools.partial(dense_backward_kernel, experts, images, last, first_layer),
                outs,
                args,
                2 * dense_flops,
                [pltpu.VMEM((total, 3 * width), BF)],
            )
        )
        upstream, weight_grads = made[:2]
        if not first_layer:
            grad_rows = exchange(made[2])
        if last:
            out_act = made[-1]
        dense_grads[at] = scatter_sum(weight_grads, axes, order_in)
    dense = jnp.stack(dense_grads)
    tail = dense[:, :, 4 * width :]
    grad_norm_gains = tail[:, :, experts : experts + 2].transpose(0, 2, 1)
    grad_norm_biases = tail[:, :, experts + 2 : experts + 4].transpose(0, 2, 1)
    grad_in, grad_out = (
        jnp.stack([expert_grads[at][which] for at in range(LAYERS)])[:, None] for which in range(2)
    )
    factor = jnp.sqrt(threshold / jnp.maximum(head_max, threshold))
    columns = jnp.repeat(factor, HEAD_DIM, axis=1)
    clipped_qk = (
        w_qkv[:, :, : 2 * width].astype(F32)
        * jnp.concatenate([columns, columns], axis=1)[:, None, :]
    )
    return (
        unpad(out_act),
        unpad(upstream),
        grad_norm_gains,
        grad_norm_biases,
        dense[:, :, : 3 * width],
        dense[:, :, 3 * width : 4 * width],
        tail[:, :, :experts],
        grad_in,
        grad_out,
        head_max,
        clipped_qk,
        grad_norm_biases[:, 1],
    )


def solution(mesh):
    dp_bits = int(mesh.shape["dp"]).bit_length() - 1
    ex_bits = int(mesh.shape["expert"]).bit_length() - 1
    dp_axes = tuple(f"d{at}" for at in range(dp_bits))
    ex_axes = tuple(f"e{at}" for at in range(ex_bits))
    split = Mesh(mesh.devices.reshape((2,) * (dp_bits + ex_bits)), dp_axes + ex_axes)
    both = dp_axes + ex_axes
    in_specs = (
        P(both, None),
        P(None, None, both),
        P(None, None, both),
        P(None, both, None),
        P(None, both, None),
        P(None, both, None),
        P(None, ex_axes, None, None),
        P(None, ex_axes, None, None),
        P(None, both, None),
        P(),
        P(both, None),
    )
    out_specs = (
        P(both, None),
        P(both, None),
        P(None, None, both),
        P(None, None, both),
        P(None, both, None),
        P(None, both, None),
        P(None, both, None),
        P(None, ex_axes, None, dp_axes),
        P(None, ex_axes, dp_axes, None),
        P(),
        P(None, both, None),
        P(None, both),
    )
    return jax.shard_map(
        functools.partial(body, dp_axes, ex_axes),
        mesh=split,
        in_specs=in_specs,
        out_specs=out_specs,
        check_vma=False,
    )
```

time: 2470 us -> 651 us (0.26)
  waiting for transfers between devices: 1300 us -> 154 us
  blocking collectives: 706 us -> 26 us
  Pallas kernels: 0 us -> 162 us
  matrix products: 151 us -> 0 us
  starting transfers between devices: 27.5 us -> 176 us
  local copies, waits for them, and re-layouts: 181 us -> 62.6 us
  other arithmetic: 74.1 us -> 43 us
    unnamed x20 -> x1, waiting for transfers between devices: 642 us -> 0.02 us
    all_gather x8 -> x0, blocking collectives: 587 us -> none  [the longest x2 178 us: body(): lax.all_gather(w_router[layer_at], ('dp', 'expert'), axis=0, tiled=True)]
    reduce_scatter x6 -> x0, waiting for transfers between devices: 562 us -> none  [the longest x2 265 us: body(): lax.psum_scatter(grad_wo, ('dp', 'expert'), scatter_dimension=0, tiled=True)]
    pallas_call x0 -> x11, Pallas kernels: none -> 162 us  [the longest x5 64.3 us: call(): pl.pallas_call(kernel, out_shape=out_shapes, scratch_shapes=list(scratch)...]
    dot_general x40 -> x0, matrix products: 149 us -> none  [the longest x2 27.8 us: expert_backward(): jnp.dot(grad_out_rows, weight_out.T, preferred_element_type=jnp.float32)]
    ppermute x0 -> x35, starting transfers between devices: none -> 100 us  [the longest x23 71.4 us: other(): return lax.ppermute(values, axis, [(0, 1), (1, 0)])]
    ppermute x0 -> x35, waiting for transfers between devices: none -> 79.3 us  [the longest x23 79.2 us: other(): return lax.ppermute(values, axis, [(0, 1), (1, 0)])]
    reshape x24 -> x5, local copies, waits for them, and re-layouts: 60.6 us -> 4.42 us  [the longest x2 3.08 us: unpad(): return values.reshape(images, padded, -1)[:, :SEQ].reshape(tokens, -1)]
  transfers between devices with their start and end apart: 20 -> 44, of which waited for: 16 -> 16; matrix products, arithmetic and copies ran while one was open for 8% -> 11% of each run, Pallas kernels for 0% -> 23%
where the time goes in v1:
time: 651 us; the launch traced here: 639 us
  starting transfers between devices  176 us (27%)
  Pallas kernels  162 us (25%)
  waiting for transfers between devices  154 us (24%)
  local copies, waits for them, and re-layouts  62.6 us (10%)
  other arithmetic  43 us (7%)
  blocking collectives  26 us (4%)
  between operations  15.5 us (2%)
    ppermute x23, waiting for transfers between devices, other(): return lax.ppermute(values, axis, [(0, 1), (1, 0)])  79.2 us
    all_to_all x7, waiting for transfers between devices, exchange(): return lax.all_to_all(rows, group, split_axis=0, concat_axis=0, tiled=True)  75.2 us
    ppermute x23, starting transfers between devices, other(): return lax.ppermute(values, axis, [(0, 1), (1, 0)])  71.4 us
    pallas_call x5, Pallas kernels, call(): pl.pallas_call(kernel, out_shape=out_shapes, scratch_shapes=list(scratch)...  64.3 us
    all_to_all x7, starting transfers between devices, exchange(): return lax.all_to_all(rows, group, split_axis=0, concat_axis=0, tiled=True)  55.7 us
    pallas_call x2, Pallas kernels, expert_forward(): pl.pallas_call(expert_forward_kernel, grid=(PIECES,), in_specs=[pl.BlockS...  43.5 us
    pallas_call x2, Pallas kernels, expert_backward(): pl.pallas_call(expert_backward_kernel, grid=(PIECES,), in_specs=[pl.Block...  30.7 us
    all_to_all x1, blocking collectives, exchange(): return lax.all_to_all(rows, group, split_axis=0, concat_axis=0, tiled=True)  26 us
  transfers between devices with their start and end apart: 44, of which 16 were waited for; matrix products, arithmetic and copies ran while one was open for 11% of the time, Pallas kernels for 23%

profile of v1, /device:TPU:0, one launch (start us, length us, event | category | flops | bytes accessed | tf_op | source)
XLA Modules:
  0.0 639.2 jit_solution(8117120014924313436)
XLA Ops:
  11.2 3.0 collective-permute-start
  14.2 2.3 collective-permute-done
  16.5 3.1 collective-permute-start.1
  19.6 5.5 collective-permute-done.1
  26.9 5.0 collective-permute-done.2
  33.7 9.2 %collective-permute-done.3 = bf16[2,2,2,1,16,2176]{5,4,2,1,0,3:T(8,128)(2,1)S(1)} collective-permute-done((bf16[2,2,2,1,16,2176]{5,4,2,1,0,3:T(8,128)(2,1)S(1)}, bf16[2,2,2,1,16,2176]{5,4,2,1,0,3:T(8,128)(2,1)S(1)}, u32[]{:S(2)}, u32[]{:S(2)}) %collective-permute-start.3) | collective-permute-done | bytes 557088 | tf_op jit(solution)/shard_map/ppermute | solution.py:484
  52.0 6.6 %shard_map.202 = (bf16[416,1664]{1,0:T(8,128)(2,1)S(1)}, bf16[416,1664]{1,0:T(8,128)(2,1)S(1)}, bf16[1664,416]{1,0:T(8,128)(2,1)}, bf16[1664,416]{1,0:T(8,128)(2...) custom-call(s32[2,416,2]{2,1,0:T(8,128)S(1)} %copy.210.cols_ref, ...), custom_call_target="tpu_custom_call" | custom-call | flops 177209344 | bytes 11088896 | tf_op jit(solution)/shard_map/pallas_call | solution.py:105
  63.4 9.5 %shard_map.203 = (f32[416,512]{1,0:T(8,128)S(1)}, bf16[416,1536]{1,0:T(8,128)(2,1)}, bf16[416,512]{1,0:T(8,128)(2,1)S(1)}, f32[416,128]{1,0:T(8,128)S(1)}, f32[4...) custom-call(f32[416,512]{1,0:T(8,128)S(1)} %bitcast_convert_fusion.refs_0_.refs_9_, ...), custom_call_target="tpu_custom_call" | custom-call | flops 2998927360 | bytes 10755328 | tf_op jit(solution)/shard_map/pallas_call | solution.py:105
  75.9 9.2 %all-to-all-start = ((bf16[8,208,512]{2,1,0:T(8,128)(2,1)}), bf16[8,208,512]{2,1,0:T(8,128)(2,1)S(1)}, u32[]{:S(2)}, u32[]{:S(2)}) async-start(bf16[8,208,512]{2,1,0:T(8,128)(2,1)} %bitcast.280), calls=%async_computation | async-start | bytes 3407872 | tf_op jit(solution)/shard_map/all_to_all | solution.py:633
  85.4 3.8 fusion.28
  102.8 14.8 %all-to-all-done = bf16[8,208,512]{2,1,0:T(8,128)(2,1)S(1)} async-done(((bf16[8,208,512]{2,1,0:T(8,128)(2,1)}), bf16[8,208,512]{2,1,0:T(8,128)(2,1)S(1)}, u32[]{:S(2)}, u32[]{:S(2)}) %all-to-all-start) | async-done | bytes 1703968 | tf_op jit(solution)/shard_map/all_to_all | solution.py:633
  117.6 21.3 %shard_map.204 = (bf16[1664,2048]{1,0:T(8,128)(2,1)}, bf16[1664,2048]{1,0:T(8,128)(2,1)}, bf16[1664,512]{1,0:T(8,128)(2,1)}) custom-call(bf16[1664,512]{1,0:T(8,128)(2,1)S(1)} %bitcast.259, bf16[512,2048]{1,0:T(8,128)(2,1)} %pad_maximum_fusion.win_ref, bf16[2048,512]{1,0:T(8,128)(2,1)} %pad_maximum_fusion.1.wout_ref), custom_call_target="tpu_custom_call" | custom-call | flops 6979321856 | bytes 21233664 | tf_op jit(solution)/shard_map/pallas_call | solution.py:264
  138.9 24.0 %all-to-all-start.1 = ((bf16[8,208,512]{2,1,0:T(8,128)(2,1)}), bf16[8,208,512]{2,1,0:T(8,128)(2,1)}, u32[]{:S(2)}, u32[]{:S(2)}) async-start(bf16[8,208,512]{2,1,0:T(8,128)(2,1)} %bitcast.43), calls=%async_computation.1 | async-start | bytes 3407872 | tf_op jit(solution)/shard_map/all_to_all | solution.py:633
  164.4 20.6 %all-to-all-done.1 = bf16[8,208,512]{2,1,0:T(8,128)(2,1)} async-done(((bf16[8,208,512]{2,1,0:T(8,128)(2,1)}), bf16[8,208,512]{2,1,0:T(8,128)(2,1)}, u32[]{:S(2)}, u32[]{:S(2)}) %all-to-all-start.1) | async-done | bytes 1703968 | tf_op jit(solution)/shard_map/all_to_all | solution.py:633
  185.0 14.7 %shard_map.205 = (f32[416,512]{1,0:T(8,128)S(1)}, bf16[416,512]{1,0:T(8,128)(2,1)S(1)}, bf16[416,512]{1,0:T(8,128)(2,1)S(1)}, f32[416,512]{1,0:T(8,128)S(1)}, bf...) custom-call(f32[416,512]{1,0:T(8,128)} %copy-done.4, ...), custom_call_target="tpu_custom_call" | custom-call | flops 2998927360 | bytes 19700992 | tf_op jit(solution)/shard_map/pallas_call | solution.py:105
  205.9 4.3 all-to-all-start.3
  216.7 28.8 %all-to-all-done.3 = bf16[8,208,512]{2,1,0:T(8,128)(2,1)} async-done(((bf16[8,208,512]{2,1,0:T(8,128)(2,1)}), bf16[8,208,512]{2,1,0:T(8,128)(2,1)}, u32[]{:S(2)}, u32[]{:S(2)}) %all-to-all-start.3) | async-done | bytes 1703968 | tf_op jit(solution)/shard_map/all_to_all | solution.py:633
  245.5 4.3 all-to-all-start.2
  249.8 12.9 %collective-permute-start.12 = (bf16[1024,512]{1,0:T(8,128)(2,1)}, bf16[1024,512]{1,0:T(8,128)(2,1)S(1)}, u32[]{:S(2)}, u32[]{:S(2)}) collective-permute-start(bf16[1024,512]{1,0:T(8,128)(2,1)} %collective-permute-done.11), channel_id=1, source_target_pairs={{8,24},{24,8},{9,25},{25,9},{10,26},{26,10},{11,27},{27,11},{12,28... | collective-permute-start | bytes 3145736 | tf_op jit(solution)/shard_map/ppermute | solution.py:489
  269.8 22.2 %shard_map.206 = (bf16[1664,2048]{1,0:T(8,128)(2,1)}, bf16[1664,2048]{1,0:T(8,128)(2,1)}, bf16[1664,512]{1,0:T(8,128)(2,1)}) custom-call(bf16[1664,512]{1,0:T(8,128)(2,1)} %bitcast.57.rows_ref, bf16[512,2048]{1,0:T(8,128)(2,1)} %pad_maximum_fusion.2.win_ref, bf16[2048,512]{1,0:T(8,128)(2,1)} %pad_maximum_fusion.3.wout_ref), custom_call_target="tpu_custom_call" | custom-call | flops 6979321856 | bytes 21233664 | tf_op jit(solution)/shard_map/pallas_call | solution.py:264
  292.6 19.3 %all-to-all-start.8 = ((f32[32,1,128]{2,1,0:T(1,128)}), f32[32,1,128]{2,1,0:T(1,128)S(1)}, u32[]{:S(2)}, u32[]{:S(2)}) async-start(f32[32,1,128]{2,1,0:T(1,128)} %broadcast_in_dim.19), calls=%async_computation.8 | async-start | bytes 32768 | tf_op jit(solution)/shard_map/all_to_all | solution.py:697
  311.9 15.7 %shard_map.207 = (bf16[1664,2048]{1,0:T(8,128)(2,1)}, bf16[1664,512]{1,0:T(8,128)(2,1)S(1)}) custom-call(bf16[1664,512]{1,0:T(8,128)(2,1)} %bitcast.55.grad_ref, bf16[1664,2048]{1,0:T(8,128)(2,1)} %get-tuple-element.72.slope_ref, bf16[512,2048]{1,0:T(8,128)(2,1)} %pad_maximum_fusion.2.win_ref, bf16[2048,512]{1,0:T(8,128)(2,1)} %pad_maximum_fusion.3.wout_ref), custom_call_target="tpu_custom_call" | custom-call | flops 6979321856 | bytes 21233664 | tf_op jit(solution)/shard_map/pallas_call | solution.py:321
  327.6 26.0 %all_to_all.94 = bf16[8,208,512]{2,1,0:T(8,128)(2,1)} all-to-all(bf16[8,208,512]{2,1,0:T(8,128)(2,1)S(1)} %bitcast.264), channel_id=1, replica_groups=mesh['d0'=2,'d1'=2,'e0'=2,'e1'=2,'e2'=2] {'d1','e1','e2'}, dimensions={0} | all-to-all | bytes 3407872 | tf_op jit(solution)/shard_map/all_to_all | solution.py:633
  353.7 4.3 all-to-all-start.5
  358.1 12.5 %shard_map.212 = (bf16[4,512,512]{2,1,0:T(8,128)(2,1)}, bf16[4,512,512]{2,1,0:T(8,128)(2,1)}) custom-call(bf16[1664,512]{1,0:T(8,128)(2,1)} %bitcast.57.rows_ref, bf16[1664,2048]{1,0:T(8,128)(2,1)} %get-tuple-element.101.hidden_ref, bf16[1664,2048]{1,0:T(8,128)(2,1)} %get-tuple-element.102.active_ref, bf16[1664,512]{1,0:T(8,128)(2,1)} %bitcast.55.grad_ref), custom_call_target="tpu_custom_call" | custom-call | flops 6979321856 | bytes 21233664 | tf_op jit(solution)/shard_map/pallas_call | solution.py:354
  370.6 2.4 slice.160
  376.2 3.8 all-to-all-done.5
  382.7 19.2 %shard_map.208 = (f32[416,512]{1,0:T(8,128)S(1)}, bf16[512,2176]{1,0:T(8,128)(2,1)}, bf16[1664,512]{1,0:T(8,128)(2,1)}, f32[416,512]{1,0:T(8,128)S(1)}) custom-call(f32[416,512]{1,0:T(8,128)S(1)} %copy-done, bf16[1664,512]{1,0:T(8,128)(2,1)} %bitcast.278, bf16[416,1664]{1,0:T(8,128)(2,1)} %get-tuple-element.74.refs_2_, ...), custom_call_target="tpu_custom_call" | custom-call | flops 5997854720 | bytes 21925120 | tf_op jit(solution)/shard_map/pallas_call | solution.py:105
  403.9 2.4 dynamic-slice_bitcast_fusion
  407.4 2.8 add_convert_fusion
  411.9 9.4 %collective-permute-done.26 = bf16[2,512,512]{2,1,0:T(8,128)(2,1)} collective-permute-done((bf16[2,512,512]{2,1,0:T(8,128)(2,1)}, bf16[2,512,512]{2,1,0:T(8,128)(2,1)}, u32[]{:S(2)}, u32[]{:S(2)}) %collective-permute-start.26) | collective-permute-done | bytes 1048608 | tf_op jit(solution)/shard_map/ppermute | solution.py:484
  421.3 2.5 add_convert_fusion.2
  425.4 5.2 all-to-all-start.6
  436.4 15.7 %collective-permute-start.34 = (bf16[512,512]{1,0:T(8,128)(2,1)}, bf16[512,512]{1,0:T(8,128)(2,1)}, u32[]{:S(2)}, u32[]{:S(2)}) collective-permute-start(bf16[512,512]{1,0:T(8,128)(2,1)} %dynamic-slice_bitcast_fusion.8), channel_id=1, source_target_pairs={{0,8},{8,0},{1,9},{9,1},{2,10},{10,2},{3,11},{11,3},{4,12},{12,4},... | collective-permute-start | bytes 1572872 | tf_op jit(solution)/shard_map/ppermute | solution.py:484
  454.3 9.0 %collective-permute-start.28 = (bf16[512,512]{1,0:T(8,128)(2,1)}, bf16[512,512]{1,0:T(8,128)(2,1)}, u32[]{:S(2)}, u32[]{:S(2)}) collective-permute-start(bf16[512,512]{1,0:T(8,128)(2,1)} %dynamic-slice_bitcast_fusion.10), channel_id=1, source_target_pairs={{0,8},{8,0},{1,9},{9,1},{2,10},{10,2},{3,11},{11,3},{4,12},{12,4},... | collective-permute-start | bytes 1572872 | tf_op jit(solution)/shard_map/ppermute | solution.py:484
  464.4 7.1 %all-to-all-done.6 = bf16[8,208,512]{2,1,0:T(8,128)(2,1)S(1)} async-done(((bf16[8,208,512]{2,1,0:T(8,128)(2,1)}), bf16[8,208,512]{2,1,0:T(8,128)(2,1)S(1)}, u32[]{:S(2)}, u32[]{:S(2)}) %all-to-all-start.6) | async-done | bytes 1703968 | tf_op jit(solution)/shard_map/all_to_all | solution.py:633
  471.5 15.0 %shard_map.209 = (bf16[1664,2048]{1,0:T(8,128)(2,1)}, bf16[1664,512]{1,0:T(8,128)(2,1)S(1)}) custom-call(bf16[1664,512]{1,0:T(8,128)(2,1)S(1)} %bitcast.261, bf16[1664,2048]{1,0:T(8,128)(2,1)} %get-tuple-element.87.slope_ref, bf16[512,2048]{1,0:T(8,128)(2,1)} %pad_maximum_fusion.win_ref, bf16[2048,512]{1,0:T(8,128)(2,1)} %pad_maximum_fusion.1.wout_ref), custom_call_target="tpu_custom_call" | custom-call | flops 6979321856 | bytes 21233664 | tf_op jit(solution)/shard_map/pallas_call | solution.py:321
  487.7 4.3 all-to-all-start.7
  492.0 2.5 fusion.5
  503.5 13.0 %collective-permute-done.21 = bf16[2,16,2176]{2,1,0:T(8,128)(2,1)} collective-permute-done((bf16[2,16,2176]{2,1,0:T(8,128)(2,1)S(1)}, bf16[2,16,2176]{2,1,0:T(8,128)(2,1)}, u32[]{:S(2)}, u32[]{:S(2)}) %collective-permute-start.21) | collective-permute-done | bytes 139296 | tf_op jit(solution)/shard_map/ppermute | solution.py:484
  518.3 11.2 %shard_map.211 = (bf16[4,512,512]{2,1,0:T(8,128)(2,1)}, bf16[4,512,512]{2,1,0:T(8,128)(2,1)}) custom-call(bf16[1664,512]{1,0:T(8,128)(2,1)S(1)} %bitcast.260, bf16[1664,2048]{1,0:T(8,128)(2,1)} %get-tuple-element.98.hidden_ref, bf16[1664,2048]{1,0:T(8,128)(2,1)} %get-tuple-element.99.active_ref, bf16[1664,512]{1,0:T(8,128)(2,1)S(1)} %bitcast.262), custom_call_target="tpu_custom_call" | custom-call | flops 6979321856 | bytes 21233664 | tf_op jit(solution)/shard_map/pallas_call | solution.py:354
  529.6 2.4 slice.158
  536.4 14.3 %shard_map.210 = (f32[416,512]{1,0:T(8,128)S(1)}, bf16[512,2176]{1,0:T(8,128)(2,1)}) custom-call(f32[416,512]{1,0:T(8,128)S(1)} %copy-done.30, bf16[1664,512]{1,0:T(8,128)(2,1)} %bitcast.70.refs_1_, bf16[416,1664]{1,0:T(8,128)(2,1)} %copy-done.2, bf16[416,1664]{1,0:T(8,128)(2,1)} %copy-done.3, bf16[416,512]{1,0:T(8,128)(2,1)S(1)} %copy-done.18, ...), custom_call_target="tpu_custom_call" | custom-call | flops 5997854720 | bytes 15535360 | tf_op jit(solution)/shard_map/pallas_call | solution.py:105
  553.3 5.2 collective-permute-done.29
  560.9 18.6 %collective-permute-done.23 = bf16[2,512,512]{2,1,0:T(8,128)(2,1)} collective-permute-done((bf16[2,512,512]{2,1,0:T(8,128)(2,1)}, bf16[2,512,512]{2,1,0:T(8,128)(2,1)}, u32[]{:S(2)}, u32[]{:S(2)}) %collective-permute-start.23) | collective-permute-done | bytes 1048608 | tf_op jit(solution)/shard_map/ppermute | solution.py:484
  586.0 21.6 %collective-permute-start.25 = (bf16[512,512]{1,0:T(8,128)(2,1)S(1)}, bf16[512,512]{1,0:T(8,128)(2,1)S(1)}, u32[]{:S(2)}, u32[]{:S(2)}) collective-permute-start(bf16[512,512]{1,0:T(8,128)(2,1)S(1)} %dynamic-slice_bitcast_fusion.11), channel_id=1, source_target_pairs={{0,8},{8,0},{1,9},{9,1},{2,10},{10,2},{3,11},{11,3},{4,12},{12,4},... | collective-permute-start | bytes 1572872 | tf_op jit(solution)/shard_map/ppermute | solution.py:484
  609.8 6.7 %collective-permute-done.15 = bf16[2,2,16,2176]{3,2,1,0:T(8,128)(2,1)S(1)} collective-permute-done((bf16[2,2,16,2176]{3,2,1,0:T(8,128)(2,1)S(1)}, bf16[2,2,16,2176]{3,2,1,0:T(8,128)(2,1)S(1)}, u32[]{:S(2)}, u32[]{:S(2)}) %collective-permute-start.15) | collective-permute-done | bytes 278560 | tf_op jit(solution)/shard_map/ppermute | solution.py:484
  618.9 2.8 collective-permute-done.16
  (312 shorter events, 123.6 us)
Async XLA Ops:
  11.2 5.3 collective-permute-start
  16.5 8.6 %collective-permute-start.1 = (bf16[2,1,16,2176]{3,2,0,1:T(8,128)(2,1)S(1)}, bf16[2,1,16,2176]{3,2,0,1:T(8,128)(2,1)S(1)}, u32[]{:S(2)}, u32[]{:S(2)}) collective-permute-start(bf16[2,1,16,2176]{3,2,0,1:T(8,128)(2,1)S(1)} %fusion.22), channel_id=1, source_target_pairs={{0,4},{4,0},{1,5},{5,1},{2,6},{6,2},{3,7},{7,3},{8,12},{12,8},{9,1... | collective-permute-start | bytes 417800 | tf_op jit(solution)/shard_map/ppermute | solution.py:484
  25.3 6.6 %collective-permute-start.2 = (bf16[2,2,1,16,2176]{4,3,1,0,2:T(8,128)(2,1)S(1)}, bf16[2,2,1,16,2176]{4,3,1,0,2:T(8,128)(2,1)S(1)}, u32[]{:S(2)}, u32[]{:S(2)}) collective-permute-start(bf16[2,2,1,16,2176]{4,3,1,0,2:T(8,128)(2,1)S(1)} %fusion.18), channel_id=1, source_target_pairs={{0,1},{1,0},{2,3},{3,2},{4,5},{5,4},{6,7},{7,6},{8,9},{9,8},{10,11... | collective-permute-start | bytes 835592 | tf_op jit(solution)/shard_map/ppermute | solution.py:484
  32.0 10.8 %collective-permute-start.3 = (bf16[2,2,2,1,16,2176]{5,4,2,1,0,3:T(8,128)(2,1)S(1)}, bf16[2,2,2,1,16,2176]{5,4,2,1,0,3:T(8,128)(2,1)S(1)}, u32[]{:S(2)}, u32[]{:S(2)}) collective-permute-start(bf16[2,2,2,1,16,2176]{5,4,2,1,0,3:T(8,128)(2,1)S(1)} %fusion.13), channel_id=1, source_target_pairs={{0,16},{16,0},{1,17},{17,1},{2,18},{18,2},{3,19},{19,3},{4,20},{20... | collective-permute-start | bytes 1671176 | tf_op jit(solution)/shard_map/ppermute | solution.py:484
  44.2 14.6 %collective-permute-start.4 = (bf16[2,2,2,2,1,16,2176]{6,5,3,2,1,0,4:T(8,128)(2,1)}, bf16[2,2,2,2,1,16,2176]{6,5,3,2,1,0,4:T(8,128)(2,1)}, u32[]{:S(2)}, u32[]{:S(2)}) collective-permute-start(bf16[2,2,2,2,1,16,2176]{6,5,3,2,1,0,4:T(8,128)(2,1)} %fusion.9), channel_id=1, source_target_pairs={{0,8},{8,0},{1,9},{9,1},{2,10},{10,2},{3,11},{11,3},{4,12},{12,4},... | collective-permute-start | bytes 3342344 | tf_op jit(solution)/shard_map/ppermute | solution.py:484
  48.4 43.9 %collective-permute-start.5 = (bf16[512,1024]{1,0:T(8,128)(2,1)}, bf16[512,1024]{1,0:T(8,128)(2,1)}, u32[]{:S(2)}, u32[]{:S(2)}) collective-permute-start(bf16[512,1024]{1,0:T(8,128)(2,1)} %dynamic-slice_bitcast_fusion.5), channel_id=1, source_target_pairs={{8,12},{12,8},{9,13},{13,9},{10,14},{14,10},{11,15},{15,11},{24,28... | collective-permute-start | bytes 3145736 | tf_op jit(solution)/shard_map/ppermute | solution.py:490
  75.9 109.1 %copy-start.12 = (f32[416,128]{1,0:T(8,128)}, f32[416,128]{1,0:T(8,128)S(1)}, u32[]{:S(2)}) copy-start(f32[416,128]{1,0:T(8,128)S(1)} %get-tuple-element.67.refs_4_.refs_16_.refs_7_) | copy-start | bytes 638980
  75.9 41.8 %all-to-all-start = ((bf16[8,208,512]{2,1,0:T(8,128)(2,1)}), bf16[8,208,512]{2,1,0:T(8,128)(2,1)S(1)}, u32[]{:S(2)}, u32[]{:S(2)}) async-start(bf16[8,208,512]{2,1,0:T(8,128)(2,1)} %bitcast.280), calls=%async_computation | async-start | bytes 3407872 | tf_op jit(solution)/shard_map/all_to_all | solution.py:633
  85.1 79.2 %all-gather.2.cloned.1.call-start = ((), (), s32[]{:S(2)}) async-start(), calls=%async_computation.9 | async-start | bytes 2297856 | tf_op jit(solution)/shard_map/all_gather | solution.py:610
  90.6 4.4 collective-permute-start.7
  92.3 5.6 collective-permute-start.6
  95.0 6.0 collective-permute-start.8
  138.9 46.0 %all-to-all-start.1 = ((bf16[8,208,512]{2,1,0:T(8,128)(2,1)}), bf16[8,208,512]{2,1,0:T(8,128)(2,1)}, u32[]{:S(2)}, u32[]{:S(2)}) async-start(bf16[8,208,512]{2,1,0:T(8,128)(2,1)} %bitcast.43), calls=%async_computation.1 | async-start | bytes 3407872 | tf_op jit(solution)/shard_map/all_to_all | solution.py:633
  163.2 36.5 %copy-start.6 = (s32[2,208,2]{2,1,0:T(8,128)}, s32[2,208,2]{2,1,0:T(8,128)S(1)}, u32[]{:S(2)}) copy-start(s32[2,208,2]{2,1,0:T(8,128)S(1)} %pad.31) | copy-start | bytes 9988
  205.9 39.6 %all-to-all-start.3 = ((bf16[8,208,512]{2,1,0:T(8,128)(2,1)}), bf16[8,208,512]{2,1,0:T(8,128)(2,1)}, u32[]{:S(2)}, u32[]{:S(2)}) async-start(bf16[8,208,512]{2,1,0:T(8,128)(2,1)} %bitcast.282), calls=%async_computation.3 | async-start | bytes 3407872 | tf_op jit(solution)/shard_map/all_to_all | solution.py:633
  211.6 3.4 collective-permute-start.9
  213.4 36.4 %collective-permute-start.11 = (bf16[1024,512]{1,0:T(8,128)(2,1)S(1)}, bf16[1024,512]{1,0:T(8,128)(2,1)}, u32[]{:S(2)}, u32[]{:S(2)}) collective-permute-start(bf16[1024,512]{1,0:T(8,128)(2,1)S(1)} %dynamic-slice_bitcast_fusion.2), channel_id=1, source_target_pairs={{8,12},{12,8},{9,13},{13,9},{10,14},{14,10},{11,15},{15,11},{24,28... | collective-permute-start | bytes 3145736 | tf_op jit(solution)/shard_map/ppermute | solution.py:490
  215.1 49.7 %collective-permute-start.10 = (bf16[512,1024]{1,0:T(8,128)(2,1)}, bf16[512,1024]{1,0:T(8,128)(2,1)}, u32[]{:S(2)}, u32[]{:S(2)}) collective-permute-start(bf16[512,1024]{1,0:T(8,128)(2,1)} %collective-permute-done.9), channel_id=1, source_target_pairs={{8,24},{24,8},{9,25},{25,9},{10,26},{26,10},{11,27},{27,11},{12,28... | collective-permute-start | bytes 3145736 | tf_op jit(solution)/shard_map/ppermute | solution.py:489
  245.5 46.5 %all-to-all-start.2 = ((bf16[8,208,512]{2,1,0:T(8,128)(2,1)}), bf16[8,208,512]{2,1,0:T(8,128)(2,1)}, u32[]{:S(2)}, u32[]{:S(2)}) async-start(bf16[8,208,512]{2,1,0:T(8,128)(2,1)} %bitcast.281), calls=%async_computation.2 | async-start | bytes 3407872 | tf_op jit(solution)/shard_map/all_to_all | solution.py:633
  249.8 18.1 %collective-permute-start.12 = (bf16[1024,512]{1,0:T(8,128)(2,1)}, bf16[1024,512]{1,0:T(8,128)(2,1)S(1)}, u32[]{:S(2)}, u32[]{:S(2)}) collective-permute-start(bf16[1024,512]{1,0:T(8,128)(2,1)} %collective-permute-done.11), channel_id=1, source_target_pairs={{8,24},{24,8},{9,25},{25,9},{10,26},{26,10},{11,27},{27,11},{12,28... | collective-permute-start | bytes 3145736 | tf_op jit(solution)/shard_map/ppermute | solution.py:489
  292.6 35.0 %all-to-all-start.8 = ((f32[32,1,128]{2,1,0:T(1,128)}), f32[32,1,128]{2,1,0:T(1,128)S(1)}, u32[]{:S(2)}, u32[]{:S(2)}) async-start(f32[32,1,128]{2,1,0:T(1,128)} %broadcast_in_dim.19), calls=%async_computation.8 | async-start | bytes 32768 | tf_op jit(solution)/shard_map/all_to_all | solution.py:697
  353.7 26.2 %all-to-all-start.5 = ((bf16[8,208,512]{2,1,0:T(8,128)(2,1)}), bf16[8,208,512]{2,1,0:T(8,128)(2,1)}, u32[]{:S(2)}, u32[]{:S(2)}) async-start(bf16[8,208,512]{2,1,0:T(8,128)(2,1)} %bitcast.64), calls=%async_computation.5 | async-start | bytes 3407872 | tf_op jit(solution)/shard_map/all_to_all | solution.py:633
  358.1 48.4 %copy-start.62 = (f32[2,8]{1,0:T(2,128)}, f32[2,8]{1,0:T(2,128)S(1)}, u32[]{:S(2)}) copy-start(f32[2,8]{1,0:T(2,128)S(1)} %reshape.183) | copy-start | bytes 196
  373.1 34.4 %collective-permute-start.32 = (bf16[2,512,512]{2,1,0:T(8,128)(2,1)}, bf16[2,512,512]{2,1,0:T(8,128)(2,1)}, u32[]{:S(2)}, u32[]{:S(2)}) collective-permute-start(bf16[2,512,512]{2,1,0:T(8,128)(2,1)} %slice.160), channel_id=1, source_target_pairs={{0,16},{16,0},{1,17},{17,1},{2,18},{18,2},{3,19},{19,3},{4,20},{20... | collective-permute-start | bytes 3145736 | tf_op jit(solution)/shard_map/ppermute | solution.py:484
  375.6 45.7 %collective-permute-start.26 = (bf16[2,512,512]{2,1,0:T(8,128)(2,1)}, bf16[2,512,512]{2,1,0:T(8,128)(2,1)}, u32[]{:S(2)}, u32[]{:S(2)}) collective-permute-start(bf16[2,512,512]{2,1,0:T(8,128)(2,1)} %slice.156), channel_id=1, source_target_pairs={{0,16},{16,0},{1,17},{17,1},{2,18},{18,2},{3,19},{19,3},{4,20},{20... | collective-permute-start | bytes 3145736 | tf_op jit(solution)/shard_map/ppermute | solution.py:484
  406.2 24.4 %collective-permute-start.18 = (bf16[2,2,2,2,16,2176]{5,4,3,2,1,0:T(8,128)(2,1)}, bf16[2,2,2,2,16,2176]{5,4,3,2,1,0:T(8,128)(2,1)}, u32[]{:S(2)}, u32[]{:S(2)}) collective-permute-start(bf16[2,2,2,2,16,2176]{5,4,3,2,1,0:T(8,128)(2,1)} %dynamic-slice_bitcast_fusion), channel_id=1, source_target_pairs={{0,8},{8,0},{1,9},{9,1},{2,10},{10,2},{3,11},{11,3},{4,12},{12,4},... | collective-permute-start | bytes 3342344 | tf_op jit(solution)/shard_map/ppermute | solution.py:484
  410.2 23.9 %collective-permute-start.33 = (bf16[2,512,512]{2,1,0:T(8,128)(2,1)}, bf16[2,512,512]{2,1,0:T(8,128)(2,1)}, u32[]{:S(2)}, u32[]{:S(2)}) collective-permute-start(bf16[2,512,512]{2,1,0:T(8,128)(2,1)} %add_convert_fusion), channel_id=1, source_target_pairs={{8,12},{12,8},{9,13},{13,9},{10,14},{14,10},{11,15},{15,11},{24,28... | collective-permute-start | bytes 3145736 | tf_op jit(solution)/shard_map/ppermute | solution.py:490
  423.8 28.3 %collective-permute-start.27 = (bf16[2,512,512]{2,1,0:T(8,128)(2,1)}, bf16[2,512,512]{2,1,0:T(8,128)(2,1)}, u32[]{:S(2)}, u32[]{:S(2)}) collective-permute-start(bf16[2,512,512]{2,1,0:T(8,128)(2,1)} %add_convert_fusion.2), channel_id=1, source_target_pairs={{8,12},{12,8},{9,13},{13,9},{10,14},{14,10},{11,15},{15,11},{24,28... | collective-permute-start | bytes 3145736 | tf_op jit(solution)/shard_map/ppermute | solution.py:490
  425.4 46.1 %all-to-all-start.6 = ((bf16[8,208,512]{2,1,0:T(8,128)(2,1)}), bf16[8,208,512]{2,1,0:T(8,128)(2,1)S(1)}, u32[]{:S(2)}, u32[]{:S(2)}) async-start(bf16[8,208,512]{2,1,0:T(8,128)(2,1)} %bitcast.279), calls=%async_computation.6 | async-start | bytes 3407872 | tf_op jit(solution)/shard_map/all_to_all | solution.py:633
  432.6 30.7 %collective-permute-start.19 = (bf16[2,2,2,16,2176]{4,3,2,1,0:T(8,128)(2,1)S(1)}, bf16[2,2,2,16,2176]{4,3,2,1,0:T(8,128)(2,1)S(1)}, u32[]{:S(2)}, u32[]{:S(2)}) collective-permute-start(bf16[2,2,2,16,2176]{4,3,2,1,0:T(8,128)(2,1)S(1)} %dynamic-slice_bitcast_fusion.6), channel_id=1, source_target_pairs={{0,16},{16,0},{1,17},{17,1},{2,18},{18,2},{3,19},{19,3},{4,20},{20... | collective-permute-start | bytes 1671176 | tf_op jit(solution)/shard_map/ppermute | solution.py:484
  436.4 55.6 %collective-permute-start.34 = (bf16[512,512]{1,0:T(8,128)(2,1)}, bf16[512,512]{1,0:T(8,128)(2,1)}, u32[]{:S(2)}, u32[]{:S(2)}) collective-permute-start(bf16[512,512]{1,0:T(8,128)(2,1)} %dynamic-slice_bitcast_fusion.8), channel_id=1, source_target_pairs={{0,8},{8,0},{1,9},{9,1},{2,10},{10,2},{3,11},{11,3},{4,12},{12,4},... | collective-permute-start | bytes 1572872 | tf_op jit(solution)/shard_map/ppermute | solution.py:484
  454.3 44.0 %collective-permute-start.28 = (bf16[512,512]{1,0:T(8,128)(2,1)}, bf16[512,512]{1,0:T(8,128)(2,1)}, u32[]{:S(2)}, u32[]{:S(2)}) collective-permute-start(bf16[512,512]{1,0:T(8,128)(2,1)} %dynamic-slice_bitcast_fusion.10), channel_id=1, source_target_pairs={{0,8},{8,0},{1,9},{9,1},{2,10},{10,2},{3,11},{11,3},{4,12},{12,4},... | collective-permute-start | bytes 1572872 | tf_op jit(solution)/shard_map/ppermute | solution.py:484
  464.3 30.2 %collective-permute-start.20 = (bf16[2,2,16,2176]{3,2,1,0:T(8,128)(2,1)}, bf16[2,2,16,2176]{3,2,1,0:T(8,128)(2,1)}, u32[]{:S(2)}, u32[]{:S(2)}) collective-permute-start(bf16[2,2,16,2176]{3,2,1,0:T(8,128)(2,1)} %dynamic-slice_bitcast_fusion.12), channel_id=1, source_target_pairs={{0,1},{1,0},{2,3},{3,2},{4,5},{5,4},{6,7},{7,6},{8,9},{9,8},{10,11... | collective-permute-start | bytes 835592 | tf_op jit(solution)/shard_map/ppermute | solution.py:484
  487.7 48.7 %all-to-all-start.7 = ((bf16[8,208,512]{2,1,0:T(8,128)(2,1)}), bf16[8,208,512]{2,1,0:T(8,128)(2,1)}, u32[]{:S(2)}, u32[]{:S(2)}) async-start(bf16[8,208,512]{2,1,0:T(8,128)(2,1)} %bitcast.263), calls=%async_computation.7 | async-start | bytes 3407872 | tf_op jit(solution)/shard_map/all_to_all | solution.py:633
  496.3 20.2 %collective-permute-start.21 = (bf16[2,16,2176]{2,1,0:T(8,128)(2,1)S(1)}, bf16[2,16,2176]{2,1,0:T(8,128)(2,1)}, u32[]{:S(2)}, u32[]{:S(2)}) collective-permute-start(bf16[2,16,2176]{2,1,0:T(8,128)(2,1)S(1)} %dynamic-slice_bitcast_fusion.14), channel_id=1, source_target_pairs={{0,2},{2,0},{1,3},{3,1},{4,6},{6,4},{5,7},{7,5},{8,10},{10,8},{9,1... | collective-permute-start | bytes 417800 | tf_op jit(solution)/shard_map/ppermute | solution.py:484
  518.2 34.1 %collective-permute-start.22 = (bf16[16,2176]{1,0:T(8,128)(2,1)}, bf16[16,2176]{1,0:T(8,128)(2,1)}, u32[]{:S(2)}, u32[]{:S(2)}) collective-permute-start(bf16[16,2176]{1,0:T(8,128)(2,1)} %dynamic-slice_bitcast_fusion.16), channel_id=1, source_target_pairs={{0,4},{4,0},{1,5},{5,1},{2,6},{6,2},{3,7},{7,3},{8,12},{12,8},{9,1... | collective-permute-start | bytes 208904 | tf_op jit(solution)/shard_map/ppermute | solution.py:484
  532.0 26.4 %collective-permute-start.29 = (bf16[2,512,512]{2,1,0:T(8,128)(2,1)}, bf16[2,512,512]{2,1,0:T(8,128)(2,1)}, u32[]{:S(2)}, u32[]{:S(2)}) collective-permute-start(bf16[2,512,512]{2,1,0:T(8,128)(2,1)} %slice.158), channel_id=1, source_target_pairs={{0,16},{16,0},{1,17},{17,1},{2,18},{18,2},{3,19},{19,3},{4,20},{20... | collective-permute-start | bytes 3145736 | tf_op jit(solution)/shard_map/ppermute | solution.py:484
  535.8 43.6 %collective-permute-start.23 = (bf16[2,512,512]{2,1,0:T(8,128)(2,1)}, bf16[2,512,512]{2,1,0:T(8,128)(2,1)}, u32[]{:S(2)}, u32[]{:S(2)}) collective-permute-start(bf16[2,512,512]{2,1,0:T(8,128)(2,1)} %slice.154), channel_id=1, source_target_pairs={{0,16},{16,0},{1,17},{17,1},{2,18},{18,2},{3,19},{19,3},{4,20},{20... | collective-permute-start | bytes 3145736 | tf_op jit(solution)/shard_map/ppermute | solution.py:484
  552.2 27.3 %copy-start.55 = (bf16[4,512,512]{2,1,0:T(8,128)(2,1)S(1)}, bf16[4,512,512]{2,1,0:T(8,128)(2,1)}, u32[]{:S(2)}) copy-start(bf16[4,512,512]{2,1,0:T(8,128)(2,1)} %get-tuple-element.100) | copy-start | bytes 6291460
  552.2 29.7 %collective-permute-start.13 = (bf16[2,2,2,2,16,2176]{5,4,3,2,1,0:T(8,128)(2,1)S(1)}, bf16[2,2,2,2,16,2176]{5,4,3,2,1,0:T(8,128)(2,1)S(1)}, u32[]{:S(2)}, u32[]{:S(2)}) collective-permute-start(bf16[2,2,2,2,16,2176]{5,4,3,2,1,0:T(8,128)(2,1)S(1)} %dynamic-slice_bitcast_fusion.1), channel_id=1, source_target_pairs={{0,8},{8,0},{1,9},{9,1},{2,10},{10,2},{3,11},{11,3},{4,12},{12,4},... | collective-permute-start | bytes 3342344 | tf_op jit(solution)/shard_map/ppermute | solution.py:484
  560.0 23.8 %collective-permute-start.30 = (bf16[2,512,512]{2,1,0:T(8,128)(2,1)S(1)}, bf16[2,512,512]{2,1,0:T(8,128)(2,1)S(1)}, u32[]{:S(2)}, u32[]{:S(2)}) collective-permute-start(bf16[2,512,512]{2,1,0:T(8,128)(2,1)S(1)} %add_convert_fusion.1), channel_id=1, source_target_pairs={{8,12},{12,8},{9,13},{13,9},{10,14},{14,10},{11,15},{15,11},{24,28... | collective-permute-start | bytes 3145736 | tf_op jit(solution)/shard_map/ppermute | solution.py:490
  580.9 4.9 collective-permute-start.24
  582.3 25.3 %collective-permute-start.14 = (bf16[2,2,2,16,2176]{4,3,2,1,0:T(8,128)(2,1)S(1)}, bf16[2,2,2,16,2176]{4,3,2,1,0:T(8,128)(2,1)S(1)}, u32[]{:S(2)}, u32[]{:S(2)}) collective-permute-start(bf16[2,2,2,16,2176]{4,3,2,1,0:T(8,128)(2,1)S(1)} %dynamic-slice_bitcast_fusion.7), channel_id=1, source_target_pairs={{0,16},{16,0},{1,17},{17,1},{2,18},{18,2},{3,19},{19,3},{4,20},{20... | collective-permute-start | bytes 1671176 | tf_op jit(solution)/shard_map/ppermute | solution.py:484
  584.0 25.4 %collective-permute-start.31 = (bf16[512,512]{1,0:T(8,128)(2,1)S(1)}, bf16[512,512]{1,0:T(8,128)(2,1)S(1)}, u32[]{:S(2)}, u32[]{:S(2)}) collective-permute-start(bf16[512,512]{1,0:T(8,128)(2,1)S(1)} %dynamic-slice_bitcast_fusion.9), channel_id=1, source_target_pairs={{0,8},{8,0},{1,9},{9,1},{2,10},{10,2},{3,11},{11,3},{4,12},{12,4},... | collective-permute-start | bytes 1572872 | tf_op jit(solution)/shard_map/ppermute | solution.py:484
  586.0 23.6 %collective-permute-start.25 = (bf16[512,512]{1,0:T(8,128)(2,1)S(1)}, bf16[512,512]{1,0:T(8,128)(2,1)S(1)}, u32[]{:S(2)}, u32[]{:S(2)}) collective-permute-start(bf16[512,512]{1,0:T(8,128)(2,1)S(1)} %dynamic-slice_bitcast_fusion.11), channel_id=1, source_target_pairs={{0,8},{8,0},{1,9},{9,1},{2,10},{10,2},{3,11},{11,3},{4,12},{12,4},... | collective-permute-start | bytes 1572872 | tf_op jit(solution)/shard_map/ppermute | solution.py:484
  607.8 8.7 %collective-permute-start.15 = (bf16[2,2,16,2176]{3,2,1,0:T(8,128)(2,1)S(1)}, bf16[2,2,16,2176]{3,2,1,0:T(8,128)(2,1)S(1)}, u32[]{:S(2)}, u32[]{:S(2)}) collective-permute-start(bf16[2,2,16,2176]{3,2,1,0:T(8,128)(2,1)S(1)} %dynamic-slice_bitcast_fusion.13), channel_id=1, source_target_pairs={{0,1},{1,0},{2,3},{3,2},{4,5},{5,4},{6,7},{7,6},{8,9},{9,8},{10,11... | collective-permute-start | bytes 835592 | tf_op jit(solution)/shard_map/ppermute | solution.py:484
  616.6 5.1 collective-permute-start.16
  621.7 6.0 collective-permute-start.17
  (59 other events, 296.6 us)
Sparse Core Ops, SparseCore 0:
  95.1 67.1 all-gather.1

commit v2 on v1

--- a/solution.py
+++ b/solution.py
@@ -19,7 +19,8 @@
 F32 = jnp.float32
 LANES = 128
 PIECES = 4
-VMEM = 50 * 1024 * 1024
+VMEM = 56 * 1024 * 1024
+MOVED = (False, True)
 
 
 def up16(size):
@@ -64,7 +65,7 @@
     return dot_last(picks, tail)
 
 
-def places_kernel(experts, capacity, cols_ref, rows_ref, *out_refs):
+def places_kernel(experts, capacity, cols_ref, rows_ref, cot_ref, *out_refs):
     tokens = cols_ref.shape[1]
     slots = experts * capacity
     square_row = lax.broadcasted_iota(jnp.int32, (tokens, tokens), 0)
@@ -96,21 +97,47 @@
             rank = jnp.sum(jnp.where(which == chosen, before, 0.0), axis=0, keepdims=True)
             slot = chosen * capacity + rank.astype(jnp.int32)
             out_ref[...] = jnp.where(slot_row == slot, 1.0, 0.0).astype(BF)
-
-
-def call(kernel, out_shapes, args, flops, scratch=()):
+    for at, out_ref in enumerate(out_refs[4 * LAYERS :]):
+        columns = out_ref.shape[1]
+        cot = cot_ref[:, at * columns : (at + 1) * columns]
+        out_ref[...] = (dot(to_slots[0][...], cot) + dot(to_slots[1][...], cot)).astype(BF)
+
+
+def two_parts(values):
+    high = values.astype(BF)
+    return high, (values - high.astype(F32)).astype(BF)
+
+
+def two_lanes(values):
+    high, low = two_parts(values)
+    lane = lane_of(values.shape[0])
+    high, low = high.astype(F32), low.astype(F32)
+    return jnp.where(lane == 0, high, jnp.where(lane == 1, low, 0.0)).astype(BF)
+
+
+def from_lanes(parts):
+    return parts[:, 0:1] + parts[:, 1:2]
+
+
+def behind(kernel, operands, *refs):
+    return kernel(*refs[operands:])
+
+
+def call(kernel, out_shapes, args, flops, scratch=(), after=()):
     moved = sum(a.size * a.dtype.itemsize for a in args) + sum(
         int(np.prod(o.shape)) * o.dtype.itemsize for o in out_shapes
     )
+    whole = pl.BlockSpec(memory_space=pltpu.VMEM)
     return pl.pallas_call(
-        kernel,
+        functools.partial(behind, kernel, len(after)),
+        in_specs=[pl.BlockSpec(memory_space=pl.ANY)] * len(after) + [whole] * len(args),
         out_shape=out_shapes,
         scratch_shapes=list(scratch),
         compiler_params=pltpu.CompilerParams(vmem_limit_bytes=VMEM),
         cost_estimate=pl.CostEstimate(
             flops=int(flops), bytes_accessed=int(moved), transcendentals=0
         ),
-    )(*args)
+    )(*after, *args)
 
 
 def shape(dims, dtype):
@@ -132,15 +159,13 @@
     if combine:
         back_ref, take_first, take_second, gates_before = take(), take(), take(), take()
     full_ref, to_first, to_second, cols_ref = take(), take(), take(), take()
-    if last:
-        cot_ref = take()
     if combine:
         x_out, first_out, second_out = take(), take(), take()
     x1_out, qkv_out, mixed_out, lse_out, probs_out, gates_out, send_out, top_out = (
         take() for _ in range(8)
     )
     if last:
-        send_grad_out = take()
+        send_gates_out = take()
     tokens, width = x_ref.shape
     rows_of = tokens // images
     x = x_ref[...]
@@ -214,132 +239,135 @@
     gates_out[...] = packed
     send_out[...] = (dot(to_first[...], n2) + dot(to_second[...], n2)).astype(BF)
     if last:
-        cot = cot_ref[...]
-        send_grad_out[...] = (
-            dot(to_first[...], (gates[0] * cot).astype(BF))
-            + dot(to_second[...], (gates[1] * cot).astype(BF))
+        send_gates_out[...] = (
+            dot(to_first[...], two_lanes(gates[0])) + dot(to_second[...], two_lanes(gates[1]))
         ).astype(BF)
 
 
-def expert_forward_kernel(rows_ref, win_ref, wout_ref, active_out, slope_out, out_ref, sums):
-    at = pl.program_id(0)
-    chunk = rows_ref.shape[0] // 4
+def expert_forward_kernel(last, *refs):
+    refs = list(refs)
+    if last:
+        grad_refs, inner_out = (refs.pop(0), refs.pop(0)), refs.pop()
+    rows_ref, win_ref, wout_ref, active_out, slope_out, out_ref = refs
+    units = win_ref.shape[1] // 2
     factor = (2.0 / np.pi) ** 0.5
-
-    @pl.loop(0, 4)
-    def _(step):
-        rows = pl.ds(pl.multiple_of(step * chunk, 16), chunk)
-        hidden = dot(rows_ref[rows, :], win_ref[...])
+    rows = rows_ref[...]
+    hidden = dot(rows, win_ref[:, :units])
+    total = before = None
+    for piece in range(2):
+        at = slice(piece * units, (piece + 1) * units)
+        later = dot(rows, win_ref[:, units:]) if piece == 0 else None
         square = hidden * hidden
-        bend = jnp.tanh(factor * hidden * (1.0 + 0.044715 * square))
-        half = 0.5 * (1.0 + bend)
-        active = (hidden * half).astype(BF)
-        active_out[rows, :] = active
-        slope_out[rows, :] = (
-            half
-            + (0.5 * factor)
-            * hidden
-            * (1.0 - bend * bend)
-            * (1.0 + (3 * 0.044715) * square)
-        ).astype(BF)
-        part = dot(active, wout_ref[...])
-
-        @pl.when(at == 0)
-        def _():
-            sums[rows, :] = part
-
-        @pl.when(at > 0)
-        def _():
-            sums[rows, :] += part
-
-        @pl.when(at == PIECES - 1)
-        def _():
-            out_ref[rows, :] = sums[rows, :].astype(BF)
-
-
-def expert_forward(rows_in, weight_in, weight_out):
+        gate = 0.5 + 0.5 * jnp.tanh(hidden * (factor + (0.044715 * factor) * square))
+        active = hidden * gate
+        slope = active * (2 * factor + (6 * 0.044715 * factor) * square)
+        slope_out[:, at] = (gate + slope * (1.0 - gate)).astype(BF)
+        active = active.astype(BF)
+        active_out[:, at] = active
+        if piece == 1:
+            total = dot(before, wout_ref[:units, :]) + dot(active, wout_ref[units:, :])
+        before, hidden = active, later
+    total = total.astype(BF)
+    out_ref[...] = total
+    if last:
+        half = total.shape[1] // 2
+        inner_out[...] = two_lanes(
+            jnp.sum(
+                total[:, :half].astype(F32) * grad_refs[0][...].astype(F32)
+                + total[:, half:].astype(F32) * grad_refs[1][...].astype(F32),
+                axis=1,
+                keepdims=True,
+            )
+        )
+
+
+def weight_spec(weight, layer_at):
+    if weight.ndim == 4:
+        return pl.BlockSpec((None, None) + weight.shape[2:], lambda i: (layer_at, 0, 0, 0))
+    return pl.BlockSpec(weight.shape, lambda i: (0, 0))
+
+
+def expert_forward(layer_at, grads, rows_in, weight_in, weight_out, after=()):
+    last = len(grads) > 0
     slots, width = rows_in.shape
-    hidden_units = weight_in.shape[1]
-    block = hidden_units // PIECES
+    hidden_units = weight_in.shape[-1]
+    chunk = slots // 4
     return pl.pallas_call(
-        expert_forward_kernel,
-        grid=(PIECES,),
-        in_specs=[
-            pl.BlockSpec((slots, width), lambda i: (0, 0)),
-            pl.BlockSpec((width, block), lambda i: (0, i)),
-            pl.BlockSpec((block, width), lambda i: (i, 0)),
+        functools.partial(behind, functools.partial(expert_forward_kernel, last), len(after)),
+        grid=(4,),
+        in_specs=[pl.BlockSpec(memory_space=pl.ANY)] * len(after)
+        + [pl.BlockSpec((chunk, width // 2), lambda i: (i, 0))] * len(grads)
+        + [
+            pl.BlockSpec((chunk, width), lambda i: (i, 0)),
+            weight_spec(weight_in, layer_at),
+            weight_spec(weight_out, layer_at),
         ],
         out_specs=[
-            pl.BlockSpec((slots, block), lambda i: (0, i)),
-            pl.BlockSpec((slots, block), lambda i: (0, i)),
-            pl.BlockSpec((slots, width), lambda i: (0, 0)),
-        ],
+            pl.BlockSpec((chunk, hidden_units), lambda i: (i, 0)),
+            pl.BlockSpec((chunk, hidden_units), lambda i: (i, 0)),
+            pl.BlockSpec((chunk, width), lambda i: (i, 0)),
+        ]
+        + [pl.BlockSpec((chunk, LANES), lambda i: (i, 0))] * last,
         out_shape=[
             shape((slots, hidden_units), BF),
             shape((slots, hidden_units), BF),
             shape((slots, width), BF),
-        ],
-        scratch_shapes=[pltpu.VMEM((slots, width), F32)],
+        ]
+        + [shape((slots, LANES), BF)] * last,
         compiler_params=pltpu.CompilerParams(vmem_limit_bytes=VMEM),
         cost_estimate=pl.CostEstimate(
             flops=4 * slots * width * hidden_units,
             bytes_accessed=slots * (hidden_units * 4 + width * 4) + 4 * width * hidden_units,
             transcendentals=slots * hidden_units,
         ),
-    )(rows_in, weight_in, weight_out)
-
-
-def expert_backward_kernel(grad_ref, slope_ref, win_ref, wout_ref, hidden_out, out_ref, sums):
-    at = pl.program_id(0)
-    chunk = grad_ref.shape[0] // 4
-
-    @pl.loop(0, 4)
-    def _(step):
-        rows = pl.ds(pl.multiple_of(step * chunk, 16), chunk)
-        grad_active = dot_last(grad_ref[rows, :], wout_ref[...])
-        grad_hidden = (grad_active * slope_ref[rows, :].astype(F32)).astype(BF)
-        hidden_out[rows, :] = grad_hidden
-        part = dot_last(grad_hidden, win_ref[...])
-
-        @pl.when(at == 0)
-        def _():
-            sums[rows, :] = part
-
-        @pl.when(at > 0)
-        def _():
-            sums[rows, :] += part
-
-        @pl.when(at == PIECES - 1)
-        def _():
-            out_ref[rows, :] = sums[rows, :].astype(BF)
-
-
-def expert_backward(grad_rows, slope, weight_in, weight_out):
-    slots, width = grad_rows.shape
-    hidden_units = weight_in.shape[1]
-    block = hidden_units // PIECES
+    )(*after, *grads, rows_in, weight_in, weight_out)
+
+
+def expert_backward_kernel(gated, *refs):
+    refs = list(refs)
+    grad_ref = refs.pop(0)
+    if gated:
+        second_ref, gates_ref, scaled = refs.pop(0), refs.pop(0), refs.pop()
+        gates = from_lanes(gates_ref[...].astype(F32))
+        half = grad_ref.shape[1]
+        scaled[:, :half] = (gates * grad_ref[...].astype(F32)).astype(BF)
+        scaled[:, half:] = (gates * second_ref[...].astype(F32)).astype(BF)
+        grad_ref = scaled
+    slope_ref, win_ref, wout_ref, hidden_out, out_ref = refs
+    units = win_ref.shape[1] // PIECES
+    for piece in range(PIECES):
+        at = slice(piece * units, (piece + 1) * units)
+        grad_active = dot_last(grad_ref[...], wout_ref[at, :])
+        hidden_out[:, at] = (grad_active * slope_ref[:, at].astype(F32)).astype(BF)
+    out_ref[...] = dot_last(hidden_out[...], win_ref[...]).astype(BF)
+
+
+def expert_backward(layer_at, grads, gates, slope, weight_in, weight_out):
+    slots, width = grads[0].shape[0], weight_in.shape[-2]
+    hidden_units = weight_in.shape[-1]
+    chunk = slots // 4
+    gated = len(gates)
+    rows_spec = lambda lanes: pl.BlockSpec((chunk, lanes), lambda i: (i, 0))
     return pl.pallas_call(
-        expert_backward_kernel,
-        grid=(PIECES,),
-        in_specs=[
-            pl.BlockSpec((slots, width), lambda i: (0, 0)),
-            pl.BlockSpec((slots, block), lambda i: (0, i)),
-            pl.BlockSpec((width, block), lambda i: (0, i)),
-            pl.BlockSpec((block, width), lambda i: (i, 0)),
+        functools.partial(expert_backward_kernel, gated),
+        grid=(4,),
+        in_specs=[rows_spec(one.shape[1]) for one in grads]
+        + [rows_spec(LANES)] * gated
+        + [
+            rows_spec(hidden_units),
+            weight_spec(weight_in, layer_at),
+            weight_spec(weight_out, layer_at),
         ],
-        out_specs=[
-            pl.BlockSpec((slots, block), lambda i: (0, i)),
-            pl.BlockSpec((slots, width), lambda i: (0, 0)),
-        ],
-        out_shape=[shape((slots, hidden_units), BF), shape((slots, width), BF)],
-        scratch_shapes=[pltpu.VMEM((slots, width), F32)],
+        out_specs=[rows_spec(hidden_units), rows_spec(width)] + [rows_spec(width)] * gated,
+        out_shape=[shape((slots, hidden_units), BF), shape((slots, width), BF)]
+        + [shape((slots, width), BF)] * gated,
         compiler_params=pltpu.CompilerParams(vmem_limit_bytes=VMEM),
         cost_estimate=pl.CostEstimate(
             flops=4 * slots * width * hidden_units,
             bytes_accessed=slots * (hidden_units * 4 + width * 4) + 4 * width * hidden_units,
             transcendentals=0,
         ),
-    )(grad_rows, slope, weight_in, weight_out)
+    )(*grads, *gates, slope, weight_in, weight_out)
 
 
 def expert_weights_kernel(rows_ref, hidden_ref, active_ref, grad_ref, in_out, out_out):
@@ -379,7 +407,7 @@
     take = lambda: refs.pop(0)
     g_ref, rows_ref, take_first, take_second = take(), take(), take(), take()
     if last:
-        out_rows_ref = take()
+        inner_ref = take()
     else:
         first_ref, second_ref = take(), take()
     probs_ref, gates_ref, cols_ref, x_ref, x1_ref = (take() for _ in range(5))
@@ -389,8 +417,6 @@
     g_out, weights_out = take(), take()
     if not first_layer:
         send_out = take()
-    if last:
-        act_out = take()
     grad_qkv = take()
     tokens, width = g_ref.shape
     rows_of = tokens // images
@@ -398,14 +424,13 @@
     gates = gates_ref[...]
     x1 = x1_ref[...]
     if last:
-        out_rows = out_rows_ref[...]
-        first = dot(take_first[...], out_rows)
-        second = dot(take_second[...], out_rows)
-        act_out[...] = x1 + (gates[:, 0:1] * first + gates[:, 1:2] * second)
+        inner = inner_ref[...]
+        grad_gates = [from_lanes(dot(one[...], inner)) for one in (take_first, take_second)]
     else:
-        first = first_ref[...].astype(F32)
-        second = second_ref[...].astype(F32)
-    grad_gates = [jnp.sum(g * one, axis=1, keepdims=True) for one in (first, second)]
+        grad_gates = [
+            jnp.sum(g * one[...].astype(F32), axis=1, keepdims=True)
+            for one in (first_ref, second_ref)
+        ]
     weighted = grad_gates[0] * gates[:, 0:1] + grad_gates[1] * gates[:, 1:2]
     amounts = [
         (grad_gates[at] - weighted) / gates[:, 2:3] * gates[:, 3 + at : 4 + at]
@@ -480,6 +505,53 @@
     ).astype(BF)
 
 
+def combine_kernel(images, x1_ref, gates_ref, take_first, take_second, back_ref, out_ref):
+    back = back_ref[...]
+    gates = gates_ref[...]
+    out = x1_ref[...] + (
+        gates[:, 0:1] * dot(take_first[...], back) + gates[:, 1:2] * dot(take_second[...], back)
+    )
+    out_ref[...] = out
+
+
+def pack_kernel(experts, qkv_ref, o_ref, router_ref, gains_ref, biases_ref, *out_refs):
+    width = o_ref.shape[2]
+    router_lanes = (lane_of(experts) == row_of(experts)).astype(F32).astype(BF)
+    gains_lanes = (lane_of(2) == row_of(2) + experts).astype(F32).astype(BF)
+    biases_lanes = (lane_of(2) == row_of(2) + experts + 2).astype(F32).astype(BF)
+    for at, out_ref in enumerate(out_refs):
+        out_ref[:, : 3 * width] = qkv_ref[at]
+        out_ref[:, 3 * width : 4 * width] = o_ref[at]
+        out_ref[:, 4 * width :] = (
+            dot(router_ref[at], router_lanes)
+            + dot_first(gains_ref[at], gains_lanes)
+            + dot_first(biases_ref[at], biases_lanes)
+        ).astype(BF)
+
+
+def finish_kernel(experts, *refs):
+    sums, outs = refs[:8], refs[8:]
+    keep_ref, more_ref = sums[:2]
+    qkv_out, o_out, router_out, gains_out, biases_out, second_out, in_out, wout_out = outs
+    width = o_out.shape[2]
+    picks = jnp.where(lane_of(8) == row_of(8) + experts, 1.0, 0.0)
+    for at in range(LAYERS):
+        dense = keep_ref[at].astype(F32) + more_ref[at].astype(F32)
+        qkv_out[at] = dense[:, : 3 * width]
+        o_out[at] = dense[:, 3 * width : 4 * width]
+        tail = dense[:, 4 * width :]
+        router_out[at] = tail[:, :experts]
+        norms = lax.dot_general(
+            picks, tail, (((1,), (1,)), ((), ())), precision=lax.Precision.HIGHEST
+        )
+        gains_out[at] = norms[0:2]
+        biases_out[at] = norms[2:4]
+        second_out[at : at + 1] = norms[3:4]
+    for whole, keep, more, out_ref in zip(sums[2:4], sums[4:6], sums[6:8], (in_out, wout_out)):
+        out_ref[0, 0] = whole[...].astype(F32)
+        out_ref[1, 0] = keep[...].astype(F32) + more[...].astype(F32)
+
+
 def other(values, axis):
     return lax.ppermute(values, axis, [(0, 1), (1, 0)])
 
@@ -490,68 +562,88 @@
     return lax.ppermute(values, (core_axis, axis), [(2, 3), (3, 2)])
 
 
-def expert_moved(weight, split_at, dp_axes, ex_axes):
-    row_axes, core_axis = dp_axes[:-1], dp_axes[-1]
-    count = 2 ** len(row_axes)
-    size = weight.shape[split_at] // count
+def expert_sent(weight, split_at, dp_axes, ex_axes):
+    row_axes = dp_axes[:-1]
+    size = weight.shape[split_at] // 2 ** len(row_axes)
     place = lax.axis_index(row_axes) if row_axes else 0
-    own = [
-        lax.dynamic_slice_in_dim(weight, (place ^ p) * size, size, split_at)
-        for p in range(count)
-    ]
-    first = lax.axis_index(core_axis) == 0
-    got = [across(own[0], core_axis, ex_axes[0])]
-    for axis in row_axes[::-1]:
-        got = got + [across(one, core_axis, axis) for one in got]
-    return jnp.concatenate(
-        [jnp.where(first, a, b) for a, b in zip(own, got)], axis=split_at
-    )
-
-
-def expert_returned(pieces, dp_axes, ex_axes):
-    row_axes, core_axis = dp_axes[:-1], dp_axes[-1]
-    pieces = pieces.reshape((2,) * len(row_axes) + (2,) + pieces.shape[1:])
-    for axis in row_axes:
-        pieces = add_low(pieces[0], other(pieces[1], axis))
-    moved = across(pieces, core_axis, ex_axes[0])
+    own = lax.dynamic_slice_in_dim(weight, place * size, size, split_at)
+    return across(own, dp_axes[-1], ex_axes[0])
+
+
+def expert_others(got, dp_axes):
+    got = [got]
+    for axis in dp_axes[:-1][::-1]:
+        got = got + [across(one, dp_axes[-1], axis) for one in got]
+    return got
+
+
+def expert_joined(weight, got, split_at, dp_axes):
+    row_axes = dp_axes[:-1]
+    place = lax.axis_index(row_axes) if row_axes else 0
+    first = lax.axis_index(dp_axes[-1]) == 0
+    size = weight.shape[split_at] // len(got)
+    blocks = []
+    for at in range(len(got)):
+        theirs = got[at]
+        for p, one in enumerate(got):
+            theirs = jnp.where(place == at ^ p, one, theirs)
+        own = lax.slice_in_dim(weight, at * size, (at + 1) * size, axis=split_at)
+        blocks.append(jnp.where(first, own, theirs))
+    return jnp.concatenate(blocks, axis=split_at)
+
+
+def returned_rows(pieces, dp_axes):
+    row_axes = dp_axes[:-1]
+    pieces = pieces.reshape((-1,) + pieces.shape[2:])
+    pieces = lax.psum_scatter(pieces, row_axes, scatter_dimension=0, tiled=True)
+    return pieces.reshape((2, -1) + pieces.shape[1:])
+
+
+def returned_home(pieces, moved, core_axis):
     core = lax.axis_index(core_axis)
     mine = jnp.where(core == 0, pieces, moved)
     keep = lax.dynamic_index_in_dim(mine, core, 0, keepdims=False)
     send = lax.dynamic_index_in_dim(mine, 1 - core, 0, keepdims=False)
-    return keep.astype(F32) + other(send, core_axis).astype(F32)
+    return keep, other(send, core_axis)
 
 
 def add_low(a, b):
     return (a.astype(F32) + b.astype(F32)).astype(BF)
 
 
-def gather_all(shard, axes, order):
-    whole = shard[None]
-    for axis in order:
-        theirs = other(whole, axis)
-        mine_first = lax.axis_index(axis) == 0
-        whole = jnp.stack(
-            [jnp.where(mine_first, whole, theirs), jnp.where(mine_first, theirs, whole)]
-        )
-    whole = whole.reshape((2,) * len(axes) + shard.shape)
+def gather_step(whole, axis, milestone=None):
+    theirs = other(whole, axis)
+    if milestone is not None:
+        theirs = tie(theirs, milestone)
+    mine_first = lax.axis_index(axis) == 0
+    return jnp.stack([jnp.where(mine_first, whole, theirs), jnp.where(mine_first, theirs, whole)])
+
+
+def gathered(whole, axes, order):
+    rows, columns = whole.shape[-2:]
+    whole = whole.reshape((2,) * len(axes) + (rows, columns))
     places = tuple(order[::-1].index(axis) for axis in axes)
-    whole = whole.transpose(places + tuple(range(len(axes), whole.ndim)))
-    return whole.reshape((-1,) + shard.shape[1:])
-
-
-def scatter_sum(values, axes, order):
-    left = list(axes)
-    values = values.reshape((2,) * len(axes) + (-1,) + values.shape[1:])
-    for axis in order:
-        at = left.index(axis)
-        mine = lax.axis_index(axis)
-        keep = lax.dynamic_index_in_dim(values, mine, at, keepdims=False)
-        send = lax.dynamic_index_in_dim(values, 1 - mine, at, keepdims=False)
-        values = keep.astype(F32) + other(send, axis).astype(F32)
-        left.remove(axis)
-        if left:
-            values = values.astype(BF)
-    return values
+    whole = whole.transpose(places + (len(axes), len(axes) + 1))
+    return whole.reshape(-1, columns)
+
+
+def tie(values, milestone):
+    return lax.optimization_barrier((values, milestone))[0]
+
+
+def halves(values, left, axis, milestone=None):
+    at = left.index(axis)
+    mine = lax.axis_index(axis)
+    keep = lax.dynamic_index_in_dim(values, mine, at, keepdims=False)
+    theirs = other(lax.dynamic_index_in_dim(values, 1 - mine, at, keepdims=False), axis)
+    if milestone is not None:
+        theirs = tie(theirs, milestone)
+    left.remove(axis)
+    return keep, theirs
+
+
+def halve(values, left, axis, milestone=None):
+    return add_low(*halves(values, left, axis, milestone))
 
 
 def body(
@@ -572,7 +664,7 @@
     axes = dp_axes + ex_axes
     group = dp_axes[-1:] + ex_axes[1:]
     order_out = ex_axes[::-1][1:] + ex_axes[-1:] + dp_axes
-    order_in = dp_axes[::-1] + ex_axes[::-1]
+    order_in = dp_axes[-1:] + ex_axes[1:][::-1] + dp_axes[:-1][::-1] + ex_axes[:1]
     experts = 2 ** len(ex_axes)
     parts = 2 ** len(dp_axes)
     tokens, width = x_in.shape
@@ -592,45 +684,47 @@
     def unpad(values):
         return values.reshape(images, padded, -1)[:, :SEQ].reshape(tokens, -1)
 
-    shards = [
-        jnp.concatenate(
-            [
-                w_qkv[at],
-                w_o[at],
-                w_router[at],
-                norm_gains[at].T,
-                norm_biases[at].T,
-                jnp.zeros((w_o.shape[1], LANES - experts - 4), BF),
-            ],
-            axis=1,
-        )
-        for at in range(LAYERS)
-    ]
-    full = [gather_all(shards[0], axes, order_out)] + [
-        lax.all_gather(shards[at], axes, axis=0, tiled=True) for at in range(1, LAYERS)
-    ]
+    shards = call(
+        functools.partial(pack_kernel, experts),
+        [shape((w_o.shape[1], 4 * width + LANES), BF)] * LAYERS,
+        (w_qkv, w_o, w_router, norm_gains, norm_biases),
+        1000,
+    )
+    def exchange(rows, at):
+        over = group if MOVED[at] else ex_axes
+        return lax.all_to_all(rows, over, split_axis=0, concat_axis=0, tiled=True)
+
     cols = [pad(routes[at], -1) for at in range(LAYERS)]
-    shift = lax.axis_index(ex_axes[0]) * (experts // 2)
+    half_away = lax.axis_index(ex_axes[0]) * (experts // 2)
     route_cols = jnp.stack(
-        [pad((routes[at] + shift) % experts, -1) for at in range(LAYERS)]
-    )
-    weights_in, weights_out = [], []
-    for at in range(LAYERS):
-        weights_in.append(expert_moved(w_in[at, 0], 1, dp_axes, ex_axes))
-        weights_out.append(expert_moved(w_out[at, 0], 0, dp_axes, ex_axes))
+        [
+            pad((routes[at] + half_away) % experts if MOVED[at] else routes[at], -1)
+            for at in range(LAYERS)
+        ]
+    )
     to_and_from = call(
         functools.partial(places_kernel, experts, capacity),
-        [shape(s, BF) for s in ((total, slots),) * 2 + ((slots, total),) * 2] * LAYERS,
-        (route_cols, route_cols.transpose(0, 2, 1)),
+        [shape(s, BF) for s in ((total, slots),) * 2 + ((slots, total),) * 2] * LAYERS
+        + [shape((slots, width // 2), BF)] * 2,
+        (route_cols, route_cols.transpose(0, 2, 1), pad(cotangent)),
         LAYERS * 4 * total * total * LANES,
     )
     collect = [to_and_from[4 * at : 4 * at + 2] for at in range(LAYERS)]
     spread = [to_and_from[4 * at + 2 : 4 * at + 4] for at in range(LAYERS)]
+    moved_at = LAYERS - 1
+    whole = shards[0][None]
+    for step, axis in enumerate(order_out):
+        milestone = None if step < 2 else {2: (to_and_from, sent[0]), 3: sent[1]}.get(step)
+        whole = gather_step(whole, axis, milestone)
+        if step == 1:
+            sent = [
+                expert_sent(tie(one[moved_at, 0], whole), split_at, dp_axes, ex_axes)
+                for one, split_at in ((w_in, 1), (w_out, 0))
+            ]
+    full = [gathered(whole, axes, order_out)]
+    weights = [(w_in, w_out)] * LAYERS
     cot = pad(cotangent.astype(F32))
     current = pad(x_in.astype(F32))
-
-    def exchange(rows):
-        return lax.all_to_all(rows, group, split_axis=0, concat_axis=0, tiled=True)
 
     dense_flops = 2 * total * width * (4 * width) + 6 * total * slots * width
     kept = []
@@ -644,8 +738,6 @@
             args += [back, *collect[at - 1], gates]
             outs += [shape((total, width), F32), shape((total, width), BF), shape((total, width), BF)]
         args += [full[at], *spread[at], cols[at]]
-        if last:
-            args.append(cot)
         outs += [
             shape((total, width), F32),
             shape((total, 3 * width), BF),
@@ -657,7 +749,7 @@
             shape((8, LANES), F32),
         ]
         if last:
-            outs.append(shape((slots, width), BF))
+            outs.append(shape((slots, LANES), BF))
         made = list(
             call(
                 functools.partial(dense_forward_kernel, experts, images, combine, last),
@@ -672,11 +764,29 @@
             kept[-1]["routed"] = (first, second)
         x1, qkv, mixed, lse, probs, gates, send, top = made[:8]
         tops.append(top[0, :HEADS])
-        rows = exchange(send)
+        rows = exchange(send if at == 0 else tie(send, cot_rows[1]), at)
+        if at == 0:
+            others = [expert_others(tie(one, send), dp_axes) for one in sent]
+            ahead = [one for got in others for one in got]
+            whole = tie(shards[1], whole)[None]
+            for axis in order_out[:-1]:
+                whole = gather_step(whole, axis)
+            ahead.append(whole)
         if last:
-            grad_rows = exchange(made[8])
-        active, slope, out_rows = expert_forward(rows, weights_in[at], weights_out[at])
-        back = exchange(out_rows)
+            gate_rows = exchange(tie(made[8], rows), at)
+            active, slope, out_rows, inner = expert_forward(at, cot_rows, rows, *weights[at])
+        else:
+            active, slope, out_rows = expert_forward(at, [], rows, *weights[at], ahead)
+            cot_rows = [exchange(tie(to_and_from[-2], rows), LAYERS - 1)]
+            back = exchange(tie(out_rows, cot_rows[0]), at)
+            cot_rows.append(exchange(tie(to_and_from[-1], back), LAYERS - 1))
+            full.append(
+                gathered(gather_step(tie(whole, out_rows), order_out[-1]), axes, order_out)
+            )
+            weights[moved_at] = [
+                expert_joined(one[moved_at, 0], tie(got, out_rows), split_at, dp_axes)
+                for one, got, split_at in zip((w_in, w_out), others, (1, 0))
+            ]
         kept.append(
             dict(
                 x=current,
@@ -693,30 +803,41 @@
         )
         current = x1
     tops = jnp.pad(jnp.concatenate(tops), (0, LANES - LAYERS * HEADS))
-    everyone = 2 ** len(axes)
-    tops = lax.all_to_all(
-        jnp.broadcast_to(tops, (everyone, LANES)), axes, split_axis=0, concat_axis=0, tiled=True
-    )
-    head_max = jnp.max(tops, axis=0)[: LAYERS * HEADS].reshape(LAYERS, HEADS)
     upstream = cot
     expert_grads = [None] * LAYERS
     dense_grads = [None] * LAYERS
     for at in reversed(range(LAYERS)):
         own = kept[at]
         last, first_layer = at == LAYERS - 1, at == 0
-        grad_hidden, grad_back = expert_backward(
-            grad_rows, own["slope"], weights_in[at], weights_out[at]
-        )
-        grad_back = exchange(grad_back)
-        expert_grads[at] = [
-            expert_returned(one, dp_axes, ex_axes)
-            for one in expert_weights(
-                own["rows"], grad_hidden, own["active"], grad_rows, parts
+        if last:
+            inner = exchange(inner, at)
+            grad_hidden, grad_back, grad_rows = expert_backward(
+                at, cot_rows, [gate_rows], own["slope"], *weights[at]
             )
-        ]
+            grad_back = tie(grad_back, inner)
+        else:
+            grad_hidden, grad_back = expert_backward(
+                at, [grad_rows], [], own["slope"], *weights[at]
+            )
+            grad_back = tie(grad_back, head_max)
+        grad_back = exchange(grad_back, at)
+        pieces = expert_weights(own["rows"], grad_hidden, own["active"], grad_rows, parts)
+        if MOVED[at]:
+            moved_pieces = [returned_rows(one, dp_axes) for one in pieces]
+            out_rows = tie(out_rows, (grad_back, pieces))
+        else:
+            expert_grads[at] = [
+                lax.psum_scatter(
+                    one.reshape((-1,) + one.shape[2:]), dp_axes, scatter_dimension=0, tiled=True
+                )
+                for one in pieces
+            ]
+        if first_layer:
+            moved_pieces = [tie(one, (grad_back, pieces)) for one in moved_pieces]
+            crossed = [across(one, dp_axes[-1], ex_axes[0]) for one in moved_pieces]
         args = [upstream, grad_back, *collect[at]]
         if last:
-            args.append(back)
+            args.append(inner)
         else:
             args += own["routed"]
         args += [own["probs"], own["gates"], cols[at], own["x"], own["x1"]]
@@ -725,8 +846,6 @@
         if not first_layer:
             args += [*spread[at - 1], kept[at - 1]["gates"]]
             outs.append(shape((slots, width), BF))
-        if last:
-            outs.append(shape((total, width), F32))
         made = list(
             call(
                 functools.partial(dense_backward_kernel, experts, images, last, first_layer),
@@ -734,21 +853,67 @@
                 args,
                 2 * dense_flops,
                 [pltpu.VMEM((total, 3 * width), BF)],
+                pieces,
             )
         )
         upstream, weight_grads = made[:2]
         if not first_layer:
-            grad_rows = exchange(made[2])
-        if last:
-            out_act = made[-1]
-        dense_grads[at] = scatter_sum(weight_grads, axes, order_in)
-    dense = jnp.stack(dense_grads)
-    tail = dense[:, :, 4 * width :]
-    grad_norm_gains = tail[:, :, experts : experts + 2].transpose(0, 2, 1)
-    grad_norm_biases = tail[:, :, experts + 2 : experts + 4].transpose(0, 2, 1)
-    grad_in, grad_out = (
-        jnp.stack([expert_grads[at][which] for at in range(LAYERS)])[:, None] for which in range(2)
-    )
+            back = exchange(out_rows, at)
+            grad_rows = exchange(tie(made[2], back), at - 1)
+        weight_grads = weight_grads.reshape((2,) * len(axes) + (-1,) + weight_grads.shape[1:])
+        if first_layer:
+            first_left = list(axes)
+            weight_grads = tie(weight_grads, crossed[0])
+            weight_grads = halve(weight_grads, first_left, order_in[0])
+            weight_grads = halve(weight_grads, first_left, order_in[1])
+            both = jnp.stack([weight_grads, sums], axis=-3)
+            both = tie(halve(both, first_left, order_in[2]), crossed[1])
+            for axis in order_in[3:-1]:
+                both = halve(both, first_left, axis)
+            dense = [
+                one.reshape(LAYERS, -1, one.shape[-1])
+                for one in halves(both, first_left, order_in[-1])
+            ]
+        else:
+            left = list(axes)
+            sums = halve(weight_grads, left, order_in[0])
+            sums = halve(sums, left, order_in[1], grad_rows)
+            [out_act] = call(
+                functools.partial(combine_kernel, images),
+                [shape((total, width), F32)],
+                [own["x1"], own["gates"], *collect[at], back],
+                4 * total * slots * width,
+            )
+            grad_rows = tie(grad_rows, (out_act, sums))
+            everyone = 2 ** len(axes)
+            tops = lax.all_to_all(
+                jnp.broadcast_to(tie(tops, grad_rows), (everyone, LANES)),
+                axes,
+                split_axis=0,
+                concat_axis=0,
+                tiled=True,
+            )
+            head_max = jnp.max(tops, axis=0)[: LAYERS * HEADS].reshape(LAYERS, HEADS)
+    home = [
+        returned_home(one, tie(moved, both), dp_axes[-1])
+        for one, moved in zip(moved_pieces, crossed)
+    ]
+    rows = w_o.shape[1]
+    finished = call(
+        functools.partial(finish_kernel, experts),
+        [
+            shape((LAYERS, rows, 3 * width), F32),
+            shape((LAYERS, rows, width), F32),
+            shape((LAYERS, rows, experts), F32),
+            shape((LAYERS, 2, rows), F32),
+            shape((LAYERS, 2, rows), F32),
+            shape((LAYERS, rows), F32),
+        ]
+        + [shape((LAYERS, 1) + one.shape, F32) for one, _ in home],
+        [*dense, *expert_grads[0], home[0][0], home[1][0], home[0][1], home[1][1]],
+        1000,
+    )
+    grad_qkv, grad_o, grad_router, grad_gains, grad_biases, second, grad_in, grad_out = finished
     factor = jnp.sqrt(threshold / jnp.maximum(head_max, threshold))
     columns = jnp.repeat(factor, HEAD_DIM, axis=1)
     clipped_qk = (
@@ -758,16 +923,16 @@
     return (
         unpad(out_act),
         unpad(upstream),
-        grad_norm_gains,
-        grad_norm_biases,
-        dense[:, :, : 3 * width],
-        dense[:, :, 3 * width : 4 * width],
-        tail[:, :, :experts],
+        grad_gains,
+        grad_biases,
+        grad_qkv,
+        grad_o,
+        grad_router,
         grad_in,
         grad_out,
         head_max,
         clipped_qk,
-        grad_norm_biases[:, 1],
+        second,
     )
 
 

time: 651 us -> 570 us (0.88)
  starting transfers between devices: 176 us -> 124 us
  waiting for transfers between devices: 154 us -> 199 us
  local copies, waits for them, and re-layouts: 62.6 us -> 35.7 us
  blocking collectives: 26 us -> 0 us
  other arithmetic: 43 us -> 31.8 us
    all_to_all x1 -> x0, blocking collectives: 26 us -> none  [exchange(): return lax.all_to_all(rows, group, split_axis=0, concat_axis=0, tiled=True)]
    ppermute x23 -> x19, waiting for transfers between devices: 79.2 us -> 105 us  [other(): return lax.ppermute(values, axis, [(0, 1), (1, 0)])]
    all_to_all x8 -> x12, starting transfers between devices: 75 us -> 56.4 us  [the longest x11 52.6 us: exchange(): return lax.all_to_all(rows, over, split_axis=0, concat_axis=0, tiled=True)]
    all_to_all x8 -> x12, waiting for transfers between devices: 75.2 us -> 93.3 us  [the longest x11 93.3 us: exchange(): return lax.all_to_all(rows, over, split_axis=0, concat_axis=0, tiled=True)]
    unnamed x130 -> x56, local copies, waits for them, and re-layouts: 24.3 us -> 9.55 us
    slice x8 -> x1, local copies, waits for them, and re-layouts: 14.4 us -> 0.01 us  [body(): routes[at]]
    ppermute x4 -> x2, starting transfers between devices: 17.1 us -> 3.24 us  [across(): return lax.ppermute(values, (axis, core_axis), [(1, 3), (3, 1)])]
    ppermute x23 -> x19, starting transfers between devices: 71.4 us -> 58.1 us  [other(): return lax.ppermute(values, axis, [(0, 1), (1, 0)])]
  transfers between devices with their start and end apart: 44 -> 41, of which waited for: 16 -> 18; matrix products, arithmetic and copies ran while one was open for 11% -> 10% of each run, Pallas kernels for 23% -> 27%
where the time goes in v2:
time: 570 us; the launch traced here: 563 us
  waiting for transfers between devices  199 us (35%)
  Pallas kernels  158 us (28%)
  starting transfers between devices  124 us (22%)
  local copies, waits for them, and re-layouts  35.7 us (6%)
  other arithmetic  31.8 us (6%)
  between operations  14.7 us (3%)
    ppermute x19, waiting for transfers between devices, other(): return lax.ppermute(values, axis, [(0, 1), (1, 0)])  105 us
    all_to_all x11, waiting for transfers between devices, exchange(): return lax.all_to_all(rows, over, split_axis=0, concat_axis=0, tiled=True)  93.3 us
    pallas_call x8, Pallas kernels, call(): pl.pallas_call(functools.partial(behind, kernel, len(after)), in_specs=[p...  77.8 us
    ppermute x19, starting transfers between devices, other(): return lax.ppermute(values, axis, [(0, 1), (1, 0)])  58.1 us
    all_to_all x11, starting transfers between devices, exchange(): return lax.all_to_all(rows, over, split_axis=0, concat_axis=0, tiled=True)  52.6 us
    pallas_call x2, Pallas kernels, expert_forward(): pl.pallas_call(functools.partial(behind, functools.partial(expert_forward...  30.7 us
    pallas_call x2, Pallas kernels, expert_weights(): pl.pallas_call(expert_weights_kernel, grid=(pieces,), in_specs=[pl.BlockS...  25 us
    pallas_call x2, Pallas kernels, expert_backward(): pl.pallas_call(functools.partial(expert_backward_kernel, gated), grid=(4,...  24.2 us
  transfers between devices with their start and end apart: 41, of which 18 were waited for; matrix products, arithmetic and copies ran while one was open for 10% of the time, Pallas kernels for 27%

profile of v2, /device:TPU:0, one launch (start us, length us, event | category | flops | bytes accessed | tf_op | source)
XLA Modules:
  0.0 562.7 jit_solution(2913220233229529768)
XLA Ops:
  10.3 3.0 collective-permute-start
  16.8 3.1 collective-permute-start.1
  21.6 3.8 collective-permute-done.1
  29.0 3.1 slice_bitcast_fusion
  36.6 8.9 %shard_map.203 = (bf16[416,1664]{1,0:T(8,128)(2,1)}, bf16[416,1664]{1,0:T(8,128)(2,1)}, bf16[1664,416]{1,0:T(8,128)(2,1)}, bf16[1664,416]{1,0:T(8,128)(2,1)}, bf...) custom-call(s32[2,416,2]{2,1,0:T(8,128)} %copy.113.refs_0_, ...), custom_call_target="tpu_custom_call" | custom-call | flops 177209344 | bytes 13218816 | tf_op jit(solution)/shard_map/pallas_call | solution.py:131
  53.9 11.4 %collective-permute-done.4 = bf16[2,2,2,1,16,2176]{5,4,2,1,0,3:T(8,128)(2,1)} collective-permute-done((bf16[2,2,2,1,16,2176]{5,4,2,1,0,3:T(8,128)(2,1)}, bf16[2,2,2,1,16,2176]{5,4,2,1,0,3:T(8,128)(2,1)}, u32[]{:S(2)}, u32[]{:S(2)}) %collective-permute-start.4) | collective-permute-done | bytes 557088 | tf_op jit(solution)/shard_map/ppermute | solution.py:556
  67.7 9.8 %collective-permute-start.6 = (bf16[2,2,2,2,1,16,2176]{6,5,3,2,1,0,4:T(8,128)(2,1)}, bf16[2,2,2,2,1,16,2176]{6,5,3,2,1,0,4:T(8,128)(2,1)}, u32[]{:S(2)}, u32[]{:S(2)}) collective-permute-start(bf16[2,2,2,2,1,16,2176]{6,5,3,2,1,0,4:T(8,128)(2,1)} %pad_maximum_fusion.3), channel_id=1, source_target_pairs={{0,8},{8,0},{1,9},{9,1},{2,10},{10,2},{3,11},{11,3},{4,12},{12,4},... | collective-permute-start | bytes 3342344 | tf_op jit(solution)/shard_map/ppermute | solution.py:556
  83.5 9.7 %shard_map.204 = (f32[416,512]{1,0:T(8,128)}, bf16[416,1536]{1,0:T(8,128)(2,1)}, bf16[416,512]{1,0:T(8,128)(2,1)}, f32[416,128]{1,0:T(8,128)}, f32[416,128]{1,0:...) custom-call(f32[416,512]{1,0:T(8,128)} %bitcast_convert_fusion.refs_0_.refs_11_, ...), custom_call_target="tpu_custom_call" | custom-call | flops 2998927360 | bytes 10755328 | tf_op jit(solution)/shard_map/pallas_call | solution.py:131
  93.2 5.2 all-to-all-start
  100.6 19.8 %collective-permute-done.11 = bf16[2,2,1,16,2176]{4,3,1,0,2:T(8,128)(2,1)S(1)} collective-permute-done((bf16[2,2,1,16,2176]{4,3,1,0,2:T(8,128)(2,1)S(1)}, bf16[2,2,1,16,2176]{4,3,1,0,2:T(8,128)(2,1)S(1)}, u32[]{:S(2)}, u32[]{:S(2)}) %collective-permute-start.11) | collective-permute-done | bytes 278560 | tf_op jit(solution)/shard_map/ppermute | solution.py:556
  126.1 12.2 %all-to-all-done = bf16[8,208,512]{2,1,0:T(8,128)(2,1)} async-done(((bf16[8,208,512]{2,1,0:T(8,128)(2,1)}), bf16[8,208,512]{2,1,0:T(8,128)(2,1)}, u32[]{:S(2)}, u32[]{:S(2)}) %all-to-all-start) | async-done | bytes 1703968 | tf_op jit(solution)/shard_map/all_to_all | solution.py:695
  138.2 3.5 all-to-all-start.1
  144.1 15.0 %shard_map.205 = (bf16[1664,2048]{1,0:T(8,128)(2,1)}, bf16[1664,2048]{1,0:T(8,128)(2,1)}, bf16[1664,512]{1,0:T(8,128)(2,1)}) custom-call(bf16[512,1024]{1,0:T(8,128)(2,1)} %collective-permute-done.3.refs_0_, bf16[512,1024]{1,0:T(8,128)(2,1)} %collective-permute-done.7.refs_1_, bf16[1024,512]{1,0:T(8,128)(2,1)} %collective-permute-done.5.refs_2_, ...), custom_call_target="tpu_custom_call" | custom-call | flops 6979321856 | bytes 21233664 | tf_op jit(solution)/shard_map/pallas_call | solution.py:295
  160.1 4.6 all-to-all-start.2
  164.7 14.0 %collective-permute-start.13 = (bf16[2,2,2,2,1,16,2176]{6,5,3,2,1,0,4:T(8,128)(2,1)S(1)}, bf16[2,2,2,2,1,16,2176]{6,5,3,2,1,0,4:T(8,128)(2,1)}, u32[]{:S(2)}, u32[]{:S(2)}) collective-permute-start(bf16[2,2,2,2,1,16,2176]{6,5,3,2,1,0,4:T(8,128)(2,1)S(1)} %bitcast.200), channel_id=1, source_target_pairs={{0,8},{8,0},{1,9},{9,1},{2,10},{10,2},{3,11},{11,3},{4,12},{12,4},... | collective-permute-start | bytes 3342344 | tf_op jit(solution)/shard_map/ppermute | solution.py:556
  179.5 21.4 %all-to-all-done.2 = bf16[8,208,512]{2,1,0:T(8,128)(2,1)} async-done(((bf16[8,208,512]{2,1,0:T(8,128)(2,1)}), bf16[8,208,512]{2,1,0:T(8,128)(2,1)}, u32[]{:S(2)}, u32[]{:S(2)}) %all-to-all-start.2) | async-done | bytes 1703968 | tf_op jit(solution)/shard_map/all_to_all | solution.py:695
  200.9 7.8 %all-to-all-start.3 = ((bf16[8,208,256]{2,1,0:T(8,128)(2,1)}), bf16[8,208,256]{2,1,0:T(8,128)(2,1)}, u32[]{:S(2)}, u32[]{:S(2)}) async-start(bf16[8,208,256]{2,1,0:T(8,128)(2,1)} %bitcast.232), calls=%async_computation.3 | async-start | bytes 1703936 | tf_op jit(solution)/shard_map/all_to_all | solution.py:695
  212.0 13.7 %shard_map.206 = (f32[416,512]{1,0:T(8,128)}, bf16[416,512]{1,0:T(8,128)(2,1)}, bf16[416,512]{1,0:T(8,128)(2,1)}, f32[416,512]{1,0:T(8,128)}, bf16[416,1536]{1,0...) custom-call(f32[416,512]{1,0:T(8,128)} %get-tuple-element.118.refs_0, ...), custom_call_target="tpu_custom_call" | custom-call | flops 2998927360 | bytes 17571072 | tf_op jit(solution)/shard_map/pallas_call | solution.py:131
  225.7 5.4 all-to-all-start.4
  237.7 15.7 %all-to-all-done.4 = bf16[8,208,512]{2,1,0:T(8,128)(2,1)} async-done(((bf16[8,208,512]{2,1,0:T(8,128)(2,1)}), bf16[8,208,512]{2,1,0:T(8,128)(2,1)}, u32[]{:S(2)}, u32[]{:S(2)}) %all-to-all-start.4) | async-done | bytes 1703968 | tf_op jit(solution)/shard_map/all_to_all | solution.py:695
  253.4 3.5 all-to-all-start.5
  256.8 2.8 pad_maximum_fusion.1.refs_3_.refs_4_
  259.6 15.7 %shard_map.207 = (bf16[1664,2048]{1,0:T(8,128)(2,1)}, bf16[1664,2048]{1,0:T(8,128)(2,1)}, bf16[1664,512]{1,0:T(8,128)(2,1)}, bf16[1664,128]{1,0:T(8,128)(2,1)}) custom-call(bf16[1664,256]{1,0:T(8,128)(2,1)} %bitcast.233, bf16[1664,256]{1,0:T(8,128)(2,1)} %bitcast.58.refs_1_, bf16[1664,512]{1,0:T(8,128)(2,1)} %bitcast.60.refs_2_.rows_ref, ...), custom_call_target="tpu_custom_call" | custom-call | flops 6979321856 | bytes 21233664 | tf_op jit(solution)/shard_map/pallas_call | solution.py:295
  275.3 4.3 all-to-all-start.6
  279.6 12.6 %shard_map.208 = (bf16[1664,2048]{1,0:T(8,128)(2,1)}, bf16[1664,512]{1,0:T(8,128)(2,1)}, bf16[1664,512]{1,0:T(8,128)(2,1)}) custom-call(bf16[1664,256]{1,0:T(8,128)(2,1)} %bitcast.234, bf16[1664,256]{1,0:T(8,128)(2,1)} %bitcast.58.refs_1_, bf16[1664,128]{1,0:T(8,128)(2,1)} %bitcast.240, bf16[1664,2048]{1,0:T(8,128)(2,1)} %get-tuple-element.141.refs_3_, ...), custom_call_target="tpu_custom_call" | custom-call | flops 6979321856 | bytes 21233664 | tf_op jit(solution)/shard_map/pallas_call | solution.py:351
  293.0 4.2 all-to-all-start.7
  297.2 12.5 %shard_map.209 = (bf16[4,512,512]{2,1,0:T(8,128)(2,1)}, bf16[4,512,512]{2,1,0:T(8,128)(2,1)}) custom-call(bf16[1664,512]{1,0:T(8,128)(2,1)} %bitcast.60.refs_2_.rows_ref, bf16[1664,2048]{1,0:T(8,128)(2,1)} %get-tuple-element.145.hidden_ref, bf16[1664,2048]{1,0:T(8,128)(2,1)} %get-tuple-element.146.active_ref, bf16[1664,512]{1,0:T(8,128)(2,1)} %get-tuple-element.147.grad_ref), custom_call_target="tpu_custom_call" | custom-call | flops 6979321856 | bytes 21233664 | tf_op jit(solution)/shard_map/pallas_call | solution.py:382
  309.7 9.4 %all-to-all-done.7 = bf16[8,208,512]{2,1,0:T(8,128)(2,1)S(1)} async-done(((bf16[8,208,512]{2,1,0:T(8,128)(2,1)}), bf16[8,208,512]{2,1,0:T(8,128)(2,1)S(1)}, u32[]{:S(2)}, u32[]{:S(2)}) %all-to-all-start.7) | async-done | bytes 1703968 | tf_op jit(solution)/shard_map/all_to_all | solution.py:695
  320.3 3.6 all-to-all-start.8
  325.9 19.1 %shard_map.211 = (f32[416,512]{1,0:T(8,128)}, bf16[512,2176]{1,0:T(8,128)(2,1)}, bf16[1664,512]{1,0:T(8,128)(2,1)}) custom-call(bf16[4,512,512]{2,1,0:T(8,128)(2,1)} %get-tuple-element.148.refs_0_, bf16[4,512,512]{2,1,0:T(8,128)(2,1)} %get-tuple-element.149.refs_1_, f32[416,512]{1,0:T(8,128)} %bitcast_convert_fusion.1.refs_2_, bf16[1664,512]{1,0:T(8,128)(2,1)} %bitcast.218, ...), custom_call_target="tpu_custom_call" | custom-call | flops 5997854720 | bytes 19795200 | tf_op jit(solution)/shard_map/pallas_call | solution.py:131
  346.9 4.7 all-to-all-start.9
  354.7 3.0 collective-permute-done.14
  363.8 5.3 shard_map.210
  369.1 16.2 %collective-permute-done.15 = bf16[2,2,2,16,2176]{4,3,1,0,2:T(8,128)(2,1)S(1)} collective-permute-done((bf16[2,2,2,16,2176]{4,3,1,0,2:T(8,128)(2,1)S(1)}, bf16[2,2,2,16,2176]{4,3,1,0,2:T(8,128)(2,1)S(1)}, u32[]{:S(2)}, u32[]{:S(2)}) %collective-permute-start.15) | collective-permute-done | bytes 557088 | tf_op jit(solution)/shard_map/ppermute | solution.py:556
  385.3 6.5 %all-to-all-done.9 = bf16[8,208,512]{2,1,0:T(8,128)(2,1)} async-done(((bf16[8,208,512]{2,1,0:T(8,128)(2,1)}), bf16[8,208,512]{2,1,0:T(8,128)(2,1)}, u32[]{:S(2)}, u32[]{:S(2)}) %all-to-all-start.9) | async-done | bytes 1703968 | tf_op jit(solution)/shard_map/all_to_all | solution.py:695
  392.5 3.8 all-to-all-start.10
  396.3 11.6 %shard_map.212 = (bf16[1664,2048]{1,0:T(8,128)(2,1)}, bf16[1664,512]{1,0:T(8,128)(2,1)}) custom-call(bf16[1664,512]{1,0:T(8,128)(2,1)} %bitcast.73.refs_0_.grad_ref, bf16[1664,2048]{1,0:T(8,128)(2,1)} %get-tuple-element.161.refs_1_, bf16[2,1,512,2048]{3,2,1,0:T(8,128)(2,1)} %refs_2_.2, bf16[2,1,2048,512]{3,2,1,0:T(8,128)(2,1)} %refs_3_.3), custom_call_target="tpu_custom_call" | custom-call | flops 6979321856 | bytes 21233664 | tf_op jit(solution)/shard_map/pallas_call | solution.py:351
  408.0 5.8 %all-to-all-start.11 = ((bf16[8,208,512]{2,1,0:T(8,128)(2,1)}), bf16[8,208,512]{2,1,0:T(8,128)(2,1)S(1)}, u32[]{:S(2)}, u32[]{:S(2)}) async-start(bf16[8,208,512]{2,1,0:T(8,128)(2,1)} %bitcast.222), calls=%async_computation.11 | async-start | bytes 3407872 | tf_op jit(solution)/shard_map/all_to_all | solution.py:695
  413.9 12.5 %shard_map.213 = (bf16[4,512,512]{2,1,0:T(8,128)(2,1)}, bf16[4,512,512]{2,1,0:T(8,128)(2,1)}) custom-call(bf16[1664,512]{1,0:T(8,128)(2,1)} %bitcast.43.refs_5_.rows_ref, bf16[1664,2048]{1,0:T(8,128)(2,1)} %get-tuple-element.162.hidden_ref, bf16[1664,2048]{1,0:T(8,128)(2,1)} %get-tuple-element.163.active_ref, bf16[1664,512]{1,0:T(8,128)(2,1)} %bitcast.73.refs_0_.grad_ref), custom_call_target="tpu_custom_call" | custom-call | flops 6979321856 | bytes 21233664 | tf_op jit(solution)/shard_map/pallas_call | solution.py:382
  426.4 27.6 %all-to-all-done.11 = bf16[8,208,512]{2,1,0:T(8,128)(2,1)S(1)} async-done(((bf16[8,208,512]{2,1,0:T(8,128)(2,1)}), bf16[8,208,512]{2,1,0:T(8,128)(2,1)S(1)}, u32[]{:S(2)}, u32[]{:S(2)}) %all-to-all-start.11) | async-done | bytes 1703968 | tf_op jit(solution)/shard_map/all_to_all | solution.py:695
  455.2 15.0 %shard_map.214 = (f32[416,512]{1,0:T(8,128)}, bf16[512,2176]{1,0:T(8,128)(2,1)}) custom-call(bf16[4,512,512]{2,1,0:T(8,128)(2,1)} %get-tuple-element.164.refs_0_, bf16[4,512,512]{2,1,0:T(8,128)(2,1)} %get-tuple-element.165.refs_1_, f32[416,512]{1,0:T(8,128)} %get-tuple-element.166.refs_2_, bf16[1664,512]{1,0:T(8,128)(2,1)} %bitcast.219, ...), custom_call_target="tpu_custom_call" | custom-call | flops 5997854720 | bytes 15535360 | tf_op jit(solution)/shard_map/pallas_call | solution.py:131
  471.9 10.7 %collective-permute-start.17 = (bf16[2,2,2,2,16,2176]{5,4,1,0,2,3:T(8,128)(2,1)S(1)}, bf16[2,2,2,2,16,2176]{5,4,1,0,2,3:T(8,128)(2,1)S(1)}, u32[]{:S(2)}, u32[]{:S(2)}) collective-permute-start(bf16[2,2,2,2,16,2176]{5,4,1,0,2,3:T(8,128)(2,1)S(1)} %copy_bitcast_fusion.1), channel_id=1, source_target_pairs={{0,8},{8,0},{1,9},{9,1},{2,10},{10,2},{3,11},{11,3},{4,12},{12,4},... | collective-permute-start | bytes 3342344 | tf_op jit(solution)/shard_map/ppermute | solution.py:556
  486.8 13.7 %collective-permute-done.18 = bf16[2,2,2,16,2176]{4,3,1,0,2:T(8,128)(2,1)} collective-permute-done((bf16[2,2,2,16,2176]{4,3,1,0,2:T(8,128)(2,1)S(1)}, bf16[2,2,2,16,2176]{4,3,1,0,2:T(8,128)(2,1)}, u32[]{:S(2)}, u32[]{:S(2)}) %collective-permute-start.18) | collective-permute-done | bytes 557088 | tf_op jit(solution)/shard_map/ppermute | solution.py:556
  504.5 19.9 %collective-permute-done.19 = bf16[2,2,2,16,2176]{4,3,2,1,0:T(8,128)(2,1)} collective-permute-done((bf16[2,2,2,16,2176]{4,3,2,1,0:T(8,128)(2,1)S(1)}, bf16[2,2,2,16,2176]{4,3,2,1,0:T(8,128)(2,1)}, u32[]{:S(2)}, u32[]{:S(2)}) %collective-permute-start.19) | collective-permute-done | bytes 557088 | tf_op jit(solution)/shard_map/ppermute | solution.py:556
  527.4 4.9 collective-permute-done.21
  533.5 4.0 collective-permute-start.24
  542.0 7.1 %collective-permute-done.22.refs_1_ = bf16[2,16,2176]{2,1,0:T(8,128)(2,1)S(1)} collective-permute-done((bf16[2,16,2176]{2,1,0:T(8,128)(2,1)S(1)}, bf16[2,16,2176]{2,1,0:T(8,128)(2,1)S(1)}, u32[]{:S(2)}, u32[]{:S(2)}) %collective-permute-start.22) | collective-permute-done | bytes 139296 | tf_op jit(solution)/shard_map/ppermute | solution.py:556
  550.2 4.2 shard_map.215
  (191 shorter events, 92.8 us)
Async XLA Ops:
  10.3 5.5 collective-permute-start
  16.8 8.6 %collective-permute-start.1 = (bf16[2,1,16,2176]{3,2,0,1:T(8,128)(2,1)S(1)}, bf16[2,1,16,2176]{3,2,0,1:T(8,128)(2,1)S(1)}, u32[]{:S(2)}, u32[]{:S(2)}) collective-permute-start(bf16[2,1,16,2176]{3,2,0,1:T(8,128)(2,1)S(1)} %pad_maximum_fusion.9), channel_id=1, source_target_pairs={{0,4},{4,0},{1,5},{5,1},{2,6},{6,2},{3,7},{7,3},{8,12},{12,8},{9,1... | collective-permute-start | bytes 417800 | tf_op jit(solution)/shard_map/ppermute | solution.py:556
  27.2 22.4 %collective-permute-start.3 = (bf16[512,1024]{1,0:T(8,128)(2,1)}, bf16[512,1024]{1,0:T(8,128)(2,1)}, u32[]{:S(2)}, u32[]{:S(2)}) collective-permute-start(bf16[512,1024]{1,0:T(8,128)(2,1)} %constant_dynamic-slice_fusion.4), channel_id=1, source_target_pairs={{8,12},{12,8},{9,13},{13,9},{10,14},{14,10},{11,15},{15,11},{24,28... | collective-permute-start | bytes 3145736 | tf_op jit(solution)/shard_map/ppermute | solution.py:562
  32.1 17.6 %collective-permute-start.2 = (bf16[2,2,1,16,2176]{4,3,1,0,2:T(8,128)(2,1)}, bf16[2,2,1,16,2176]{4,3,1,0,2:T(8,128)(2,1)}, u32[]{:S(2)}, u32[]{:S(2)}) collective-permute-start(bf16[2,2,1,16,2176]{4,3,1,0,2:T(8,128)(2,1)} %pad_maximum_fusion.7), channel_id=1, source_target_pairs={{0,1},{1,0},{2,3},{3,2},{4,5},{5,4},{6,7},{7,6},{8,9},{9,8},{10,11... | collective-permute-start | bytes 835592 | tf_op jit(solution)/shard_map/ppermute | solution.py:556
  45.5 8.3 %copy-start.21 = (bf16[394,512]{1,0:T(8,128)(2,1)S(1)}, bf16[394,512]{1,0:T(8,128)(2,1)}, u32[]{:S(2)}) copy-start(bf16[394,512]{1,0:T(8,128)(2,1)} %param.11) | copy-start | bytes 1210372
  47.8 6.1 %collective-permute-start.5 = (bf16[1024,512]{1,0:T(8,128)(2,1)}, bf16[1024,512]{1,0:T(8,128)(2,1)}, u32[]{:S(2)}, u32[]{:S(2)}) collective-permute-start(bf16[1024,512]{1,0:T(8,128)(2,1)} %constant_dynamic-slice_fusion.3), channel_id=1, source_target_pairs={{8,12},{12,8},{9,13},{13,9},{10,14},{14,10},{11,15},{15,11},{24,28... | collective-permute-start | bytes 3145736 | tf_op jit(solution)/shard_map/ppermute | solution.py:562
  51.6 13.8 %collective-permute-start.4 = (bf16[2,2,2,1,16,2176]{5,4,2,1,0,3:T(8,128)(2,1)}, bf16[2,2,2,1,16,2176]{5,4,2,1,0,3:T(8,128)(2,1)}, u32[]{:S(2)}, u32[]{:S(2)}) collective-permute-start(bf16[2,2,2,1,16,2176]{5,4,2,1,0,3:T(8,128)(2,1)} %pad_maximum_fusion.5), channel_id=1, source_target_pairs={{0,16},{16,0},{1,17},{17,1},{2,18},{18,2},{3,19},{19,3},{4,20},{20... | collective-permute-start | bytes 1671176 | tf_op jit(solution)/shard_map/ppermute | solution.py:556
  53.1 25.4 %collective-permute-start.9 = (bf16[1,16,2176]{2,1,0:T(8,128)(2,1)}, bf16[1,16,2176]{2,1,0:T(8,128)(2,1)}, u32[]{:S(2)}, u32[]{:S(2)}) collective-permute-start(bf16[1,16,2176]{2,1,0:T(8,128)(2,1)} %bitcast.27), channel_id=1, source_target_pairs={{0,2},{2,0},{1,3},{3,1},{4,6},{6,4},{5,7},{7,5},{8,10},{10,8},{9,1... | collective-permute-start | bytes 208904 | tf_op jit(solution)/shard_map/ppermute | solution.py:556
  67.7 12.5 %collective-permute-start.6 = (bf16[2,2,2,2,1,16,2176]{6,5,3,2,1,0,4:T(8,128)(2,1)}, bf16[2,2,2,2,1,16,2176]{6,5,3,2,1,0,4:T(8,128)(2,1)}, u32[]{:S(2)}, u32[]{:S(2)}) collective-permute-start(bf16[2,2,2,2,1,16,2176]{6,5,3,2,1,0,4:T(8,128)(2,1)} %pad_maximum_fusion.3), channel_id=1, source_target_pairs={{0,8},{8,0},{1,9},{9,1},{2,10},{10,2},{3,11},{11,3},{4,12},{12,4},... | collective-permute-start | bytes 3342344 | tf_op jit(solution)/shard_map/ppermute | solution.py:556
  80.1 18.3 %collective-permute-start.10 = (bf16[2,1,16,2176]{3,2,0,1:T(8,128)(2,1)}, bf16[2,1,16,2176]{3,2,0,1:T(8,128)(2,1)S(1)}, u32[]{:S(2)}, u32[]{:S(2)}) collective-permute-start(bf16[2,1,16,2176]{3,2,0,1:T(8,128)(2,1)} %pad_maximum_fusion.10), channel_id=1, source_target_pairs={{0,4},{4,0},{1,5},{5,1},{2,6},{6,2},{3,7},{7,3},{8,12},{12,8},{9,1... | collective-permute-start | bytes 417800 | tf_op jit(solution)/shard_map/ppermute | solution.py:556
  93.2 45.0 %all-to-all-start = ((bf16[8,208,512]{2,1,0:T(8,128)(2,1)}), bf16[8,208,512]{2,1,0:T(8,128)(2,1)}, u32[]{:S(2)}, u32[]{:S(2)}) async-start(bf16[8,208,512]{2,1,0:T(8,128)(2,1)} %bitcast.220), calls=%async_computation | async-start | bytes 3407872 | tf_op jit(solution)/shard_map/all_to_all | solution.py:695
  98.5 21.9 %collective-permute-start.11 = (bf16[2,2,1,16,2176]{4,3,1,0,2:T(8,128)(2,1)S(1)}, bf16[2,2,1,16,2176]{4,3,1,0,2:T(8,128)(2,1)S(1)}, u32[]{:S(2)}, u32[]{:S(2)}) collective-permute-start(bf16[2,2,1,16,2176]{4,3,1,0,2:T(8,128)(2,1)S(1)} %pad_maximum_fusion.8), channel_id=1, source_target_pairs={{0,1},{1,0},{2,3},{3,2},{4,5},{5,4},{6,7},{7,6},{8,9},{9,8},{10,11... | collective-permute-start | bytes 835592 | tf_op jit(solution)/shard_map/ppermute | solution.py:556
  121.4 20.4 %collective-permute-start.12 = (bf16[2,2,2,1,16,2176]{5,4,2,1,0,3:T(8,128)(2,1)}, bf16[2,2,2,1,16,2176]{5,4,2,1,0,3:T(8,128)(2,1)}, u32[]{:S(2)}, u32[]{:S(2)}) collective-permute-start(bf16[2,2,2,1,16,2176]{5,4,2,1,0,3:T(8,128)(2,1)} %pad_maximum_fusion.6), channel_id=1, source_target_pairs={{0,16},{16,0},{1,17},{17,1},{2,18},{18,2},{3,19},{19,3},{4,20},{20... | collective-permute-start | bytes 1671176 | tf_op jit(solution)/shard_map/ppermute | solution.py:556
  122.8 21.3 %collective-permute-start.8 = (bf16[1024,512]{1,0:T(8,128)(2,1)}, bf16[1024,512]{1,0:T(8,128)(2,1)}, u32[]{:S(2)}, u32[]{:S(2)}) collective-permute-start(bf16[1024,512]{1,0:T(8,128)(2,1)} %collective-permute-done.5.refs_2_), channel_id=1, source_target_pairs={{8,24},{24,8},{9,25},{25,9},{10,26},{26,10},{11,27},{27,11},{12,28... | collective-permute-start | bytes 3145736 | tf_op jit(solution)/shard_map/ppermute | solution.py:561
  124.4 19.7 %collective-permute-start.7 = (bf16[512,1024]{1,0:T(8,128)(2,1)}, bf16[512,1024]{1,0:T(8,128)(2,1)}, u32[]{:S(2)}, u32[]{:S(2)}) collective-permute-start(bf16[512,1024]{1,0:T(8,128)(2,1)} %collective-permute-done.3.refs_0_), channel_id=1, source_target_pairs={{8,24},{24,8},{9,25},{25,9},{10,26},{26,10},{11,27},{27,11},{12,28... | collective-permute-start | bytes 3145736 | tf_op jit(solution)/shard_map/ppermute | solution.py:561
  138.2 20.9 %all-to-all-start.1 = ((bf16[8,208,256]{2,1,0:T(8,128)(2,1)}), bf16[8,208,256]{2,1,0:T(8,128)(2,1)S(1)}, u32[]{:S(2)}, u32[]{:S(2)}) async-start(bf16[8,208,256]{2,1,0:T(8,128)(2,1)} %bitcast.44), calls=%async_computation.1 | async-start | bytes 1703936 | tf_op jit(solution)/shard_map/all_to_all | solution.py:695
  160.1 40.8 %all-to-all-start.2 = ((bf16[8,208,512]{2,1,0:T(8,128)(2,1)}), bf16[8,208,512]{2,1,0:T(8,128)(2,1)}, u32[]{:S(2)}, u32[]{:S(2)}) async-start(bf16[8,208,512]{2,1,0:T(8,128)(2,1)} %bitcast.224), calls=%async_computation.2 | async-start | bytes 3407872 | tf_op jit(solution)/shard_map/all_to_all | solution.py:695
  164.7 44.0 %collective-permute-start.13 = (bf16[2,2,2,2,1,16,2176]{6,5,3,2,1,0,4:T(8,128)(2,1)S(1)}, bf16[2,2,2,2,1,16,2176]{6,5,3,2,1,0,4:T(8,128)(2,1)}, u32[]{:S(2)}, u32[]{:S(2)}) collective-permute-start(bf16[2,2,2,2,1,16,2176]{6,5,3,2,1,0,4:T(8,128)(2,1)S(1)} %bitcast.200), channel_id=1, source_target_pairs={{0,8},{8,0},{1,9},{9,1},{2,10},{10,2},{3,11},{11,3},{4,12},{12,4},... | collective-permute-start | bytes 3342344 | tf_op jit(solution)/shard_map/ppermute | solution.py:556
  200.9 24.8 %all-to-all-start.3 = ((bf16[8,208,256]{2,1,0:T(8,128)(2,1)}), bf16[8,208,256]{2,1,0:T(8,128)(2,1)}, u32[]{:S(2)}, u32[]{:S(2)}) async-start(bf16[8,208,256]{2,1,0:T(8,128)(2,1)} %bitcast.232), calls=%async_computation.3 | async-start | bytes 1703936 | tf_op jit(solution)/shard_map/all_to_all | solution.py:695
  225.7 27.6 %all-to-all-start.4 = ((bf16[8,208,512]{2,1,0:T(8,128)(2,1)}), bf16[8,208,512]{2,1,0:T(8,128)(2,1)}, u32[]{:S(2)}, u32[]{:S(2)}) async-start(bf16[8,208,512]{2,1,0:T(8,128)(2,1)} %bitcast.221), calls=%async_computation.4 | async-start | bytes 3407872 | tf_op jit(solution)/shard_map/all_to_all | solution.py:695
  253.4 21.9 %all-to-all-start.5 = ((bf16[8,208,128]{2,1,0:T(8,128)(2,1)}), bf16[8,208,128]{2,1,0:T(8,128)(2,1)S(1)}, u32[]{:S(2)}, u32[]{:S(2)}) async-start(bf16[8,208,128]{2,1,0:T(8,128)(2,1)} %bitcast.239), calls=%async_computation.5 | async-start | bytes 851968 | tf_op jit(solution)/shard_map/all_to_all | solution.py:695
  275.3 16.9 %all-to-all-start.6 = ((bf16[8,208,128]{2,1,0:T(8,128)(2,1)}), bf16[8,208,128]{2,1,0:T(8,128)(2,1)S(1)}, u32[]{:S(2)}, u32[]{:S(2)}) async-start(bf16[8,208,128]{2,1,0:T(8,128)(2,1)} %bitcast.241), calls=%async_computation.6 | async-start | bytes 851968 | tf_op jit(solution)/shard_map/all_to_all | solution.py:695
  293.0 26.1 %all-to-all-start.7 = ((bf16[8,208,512]{2,1,0:T(8,128)(2,1)}), bf16[8,208,512]{2,1,0:T(8,128)(2,1)S(1)}, u32[]{:S(2)}, u32[]{:S(2)}) async-start(bf16[8,208,512]{2,1,0:T(8,128)(2,1)} %bitcast.223), calls=%async_computation.7 | async-start | bytes 3407872 | tf_op jit(solution)/shard_map/all_to_all | solution.py:695
  320.3 25.4 %all-to-all-start.8 = ((bf16[8,208,512]{2,1,0:T(8,128)(2,1)}), bf16[8,208,512]{2,1,0:T(8,128)(2,1)S(1)}, u32[]{:S(2)}, u32[]{:S(2)}) async-start(bf16[8,208,512]{2,1,0:T(8,128)(2,1)} %bitcast.69), calls=%async_computation.8 | async-start | bytes 3407872 | tf_op jit(solution)/shard_map/all_to_all | solution.py:695
  323.9 102.5 %reduce-scatter.5.cloned.1.call-start = ((), (), s32[]{:S(2)}) async-start(), calls=%async_computation.16 | async-start | bytes 3145728 | tf_op jit(solution)/shard_map/reduce_scatter | solution.py:598
  346.9 44.9 %all-to-all-start.9 = ((bf16[8,208,512]{2,1,0:T(8,128)(2,1)}), bf16[8,208,512]{2,1,0:T(8,128)(2,1)}, u32[]{:S(2)}, u32[]{:S(2)}) async-start(bf16[8,208,512]{2,1,0:T(8,128)(2,1)} %bitcast.217), calls=%async_computation.9 | async-start | bytes 3407872 | tf_op jit(solution)/shard_map/all_to_all | solution.py:695
  351.6 150.3 %reduce-scatter.7.cloned.1.call-start = ((), (), s32[]{:S(2)}) async-start(), calls=%async_computation.17 | async-start | bytes 3145728 | tf_op jit(solution)/shard_map/reduce_scatter | solution.py:598
  354.7 3.0 collective-permute-start.14
  360.3 25.0 %collective-permute-start.15 = (bf16[2,2,2,16,2176]{4,3,1,0,2:T(8,128)(2,1)S(1)}, bf16[2,2,2,16,2176]{4,3,1,0,2:T(8,128)(2,1)S(1)}, u32[]{:S(2)}, u32[]{:S(2)}) collective-permute-start(bf16[2,2,2,16,2176]{4,3,1,0,2:T(8,128)(2,1)S(1)} %dynamic-slice_bitcast_fusion.1), channel_id=1, source_target_pairs={{0,1},{1,0},{2,3},{3,2},{4,5},{5,4},{6,7},{7,6},{8,9},{9,8},{10,11... | collective-permute-start | bytes 1671176 | tf_op jit(solution)/shard_map/ppermute | solution.py:556
  392.5 15.4 %all-to-all-start.10 = ((f32[32,1,128]{2,1,0:T(1,128)}), f32[32,1,128]{2,1,0:T(1,128)S(1)}, u32[]{:S(2)}, u32[]{:S(2)}) async-start(f32[32,1,128]{2,1,0:T(1,128)} %broadcast_in_dim.15), calls=%async_computation.10 | async-start | bytes 32768 | tf_op jit(solution)/shard_map/all_to_all | solution.py:889
  408.0 119.2 %copy-start.26 = (f32[2,8]{1,0:T(2,128)}, f32[2,8]{1,0:T(2,128)S(1)}, u32[]{:S(2)}) copy-start(f32[2,8]{1,0:T(2,128)S(1)} %reshape.172) | copy-start | bytes 196
  408.0 45.9 %all-to-all-start.11 = ((bf16[8,208,512]{2,1,0:T(8,128)(2,1)}), bf16[8,208,512]{2,1,0:T(8,128)(2,1)S(1)}, u32[]{:S(2)}, u32[]{:S(2)}) async-start(bf16[8,208,512]{2,1,0:T(8,128)(2,1)} %bitcast.222), calls=%async_computation.11 | async-start | bytes 3407872 | tf_op jit(solution)/shard_map/all_to_all | solution.py:695
  413.8 128.2 %reduce-scatter.11.cloned.1.call-start = ((), (), s32[]{:S(2)}) async-start(), calls=%async_computation.19 | async-start | bytes 2621440 | tf_op jit(solution)/shard_map/reduce_scatter | solution.py:830
  454.0 16.2 %collective-permute-start.16 = (bf16[2,512,512]{2,1,0:T(8,128)(2,1)}, bf16[2,512,512]{2,1,0:T(8,128)(2,1)S(1)}, u32[]{:S(2)}, u32[]{:S(2)}) collective-permute-start(bf16[2,512,512]{2,1,0:T(8,128)(2,1)} %bitcast.225), channel_id=1, source_target_pairs={{8,12},{12,8},{9,13},{13,9},{10,14},{14,10},{11,15},{15,11},{24,28... | collective-permute-start | bytes 3145736 | tf_op jit(solution)/shard_map/ppermute | solution.py:562
  454.7 87.3 %reduce-scatter.9.cloned.1.call-start = ((), (), s32[]{:S(2)}) async-start(), calls=%async_computation.18 | async-start | bytes 2621440 | tf_op jit(solution)/shard_map/reduce_scatter | solution.py:830
  470.1 14.9 %copy-start.5 = (bf16[512,2176]{1,0:T(8,128)(2,1)S(1)}, bf16[512,2176]{1,0:T(8,128)(2,1)}, u32[]{:S(2)}) copy-start(bf16[512,2176]{1,0:T(8,128)(2,1)} %get-tuple-element.179) | copy-start | bytes 6684676
  470.2 12.5 %copy-start.11 = (bf16[2,512,512]{2,1,0:T(8,128)(2,1)}, bf16[2,512,512]{2,1,0:T(8,128)(2,1)S(1)}, u32[]{:S(2)}) copy-start(bf16[2,512,512]{2,1,0:T(8,128)(2,1)S(1)} %collective-permute-done.16) | copy-start | bytes 3145732
  471.9 13.1 %collective-permute-start.17 = (bf16[2,2,2,2,16,2176]{5,4,1,0,2,3:T(8,128)(2,1)S(1)}, bf16[2,2,2,2,16,2176]{5,4,1,0,2,3:T(8,128)(2,1)S(1)}, u32[]{:S(2)}, u32[]{:S(2)}) collective-permute-start(bf16[2,2,2,2,16,2176]{5,4,1,0,2,3:T(8,128)(2,1)S(1)} %copy_bitcast_fusion.1), channel_id=1, source_target_pairs={{0,8},{8,0},{1,9},{9,1},{2,10},{10,2},{3,11},{11,3},{4,12},{12,4},... | collective-permute-start | bytes 3342344 | tf_op jit(solution)/shard_map/ppermute | solution.py:556
  485.4 15.1 %collective-permute-start.18 = (bf16[2,2,2,16,2176]{4,3,1,0,2:T(8,128)(2,1)S(1)}, bf16[2,2,2,16,2176]{4,3,1,0,2:T(8,128)(2,1)}, u32[]{:S(2)}, u32[]{:S(2)}) collective-permute-start(bf16[2,2,2,16,2176]{4,3,1,0,2:T(8,128)(2,1)S(1)} %dynamic-slice_bitcast_fusion), channel_id=1, source_target_pairs={{0,1},{1,0},{2,3},{3,2},{4,5},{5,4},{6,7},{7,6},{8,9},{9,8},{10,11... | collective-permute-start | bytes 1671176 | tf_op jit(solution)/shard_map/ppermute | solution.py:556
  486.8 16.7 %copy-start.3 = (f32[416,512]{1,0:T(8,128)S(1)}, f32[416,512]{1,0:T(8,128)}, u32[]{:S(2)}) copy-start(f32[416,512]{1,0:T(8,128)} %shard_map.210) | copy-start | bytes 2555908
  501.8 22.7 %collective-permute-start.19 = (bf16[2,2,2,16,2176]{4,3,2,1,0:T(8,128)(2,1)S(1)}, bf16[2,2,2,16,2176]{4,3,2,1,0:T(8,128)(2,1)}, u32[]{:S(2)}, u32[]{:S(2)}) collective-permute-start(bf16[2,2,2,16,2176]{4,3,2,1,0:T(8,128)(2,1)S(1)} %fusion.10), channel_id=1, source_target_pairs={{0,2},{2,0},{1,3},{3,1},{4,6},{6,4},{5,7},{7,5},{8,10},{10,8},{9,1... | collective-permute-start | bytes 1671176 | tf_op jit(solution)/shard_map/ppermute | solution.py:556
  501.9 23.8 %collective-permute-start.20 = (bf16[2,512,512]{2,1,0:T(8,128)(2,1)}, bf16[2,512,512]{2,1,0:T(8,128)(2,1)}, u32[]{:S(2)}, u32[]{:S(2)}) collective-permute-start(bf16[2,512,512]{2,1,0:T(8,128)(2,1)} %bitcast.227), channel_id=1, source_target_pairs={{8,12},{12,8},{9,13},{13,9},{10,14},{14,10},{11,15},{15,11},{24,28... | collective-permute-start | bytes 3145736 | tf_op jit(solution)/shard_map/ppermute | solution.py:562
  504.5 22.7 %copy-start.25 = (f32[2,8]{1,0:T(2,128)S(1)}, f32[2,8]{1,0:T(2,128)}, u32[]{:S(2)}) copy-start(f32[2,8]{1,0:T(2,128)} %param.20) | copy-start | bytes 196
  504.5 27.9 %copy-start.10 = (bf16[1024,512]{1,0:T(8,128)(2,1)S(1)}, bf16[1024,512]{1,0:T(8,128)(2,1)}, u32[]{:S(2)}) copy-start(bf16[1024,512]{1,0:T(8,128)(2,1)} %reduce-scatter.7.cloned.1.call-done) | copy-start | bytes 3145732
  525.7 6.7 %collective-permute-start.21 = (bf16[2,2,16,2176]{3,2,1,0:T(8,128)(2,1)S(1)}, bf16[2,2,16,2176]{3,2,1,0:T(8,128)(2,1)S(1)}, u32[]{:S(2)}, u32[]{:S(2)}) collective-permute-start(bf16[2,2,16,2176]{3,2,1,0:T(8,128)(2,1)S(1)} %dynamic-slice_bitcast_fusion.6), channel_id=1, source_target_pairs={{0,16},{16,0},{1,17},{17,1},{2,18},{18,2},{3,19},{19,3},{4,20},{20... | collective-permute-start | bytes 835592 | tf_op jit(solution)/shard_map/ppermute | solution.py:556
  533.5 15.7 %collective-permute-start.24 = (bf16[512,512]{1,0:T(8,128)(2,1)S(1)}, bf16[512,512]{1,0:T(8,128)(2,1)S(1)}, u32[]{:S(2)}, u32[]{:S(2)}) collective-permute-start(bf16[512,512]{1,0:T(8,128)(2,1)S(1)} %get-tuple-element.254), channel_id=1, source_target_pairs={{0,8},{8,0},{1,9},{9,1},{2,10},{10,2},{3,11},{11,3},{4,12},{12,4},... | collective-permute-start | bytes 1572872 | tf_op jit(solution)/shard_map/ppermute | solution.py:556
  538.4 10.7 %collective-permute-start.23 = (bf16[512,512]{1,0:T(8,128)(2,1)S(1)}, bf16[512,512]{1,0:T(8,128)(2,1)S(1)}, u32[]{:S(2)}, u32[]{:S(2)}) collective-permute-start(bf16[512,512]{1,0:T(8,128)(2,1)S(1)} %get-tuple-element.256), channel_id=1, source_target_pairs={{0,8},{8,0},{1,9},{9,1},{2,10},{10,2},{3,11},{11,3},{4,12},{12,4},... | collective-permute-start | bytes 1572872 | tf_op jit(solution)/shard_map/ppermute | solution.py:556
  539.9 9.2 %collective-permute-start.22 = (bf16[2,16,2176]{2,1,0:T(8,128)(2,1)S(1)}, bf16[2,16,2176]{2,1,0:T(8,128)(2,1)S(1)}, u32[]{:S(2)}, u32[]{:S(2)}) collective-permute-start(bf16[2,16,2176]{2,1,0:T(8,128)(2,1)S(1)} %get-tuple-element.262), channel_id=1, source_target_pairs={{0,4},{4,0},{1,5},{5,1},{2,6},{6,2},{3,7},{7,3},{8,12},{12,8},{9,1... | collective-permute-start | bytes 417800 | tf_op jit(solution)/shard_map/ppermute | solution.py:556
  (20 other events, 52.6 us)
Sparse Core Ops, SparseCore 0:
  327.5 32.6 reduce-scatter.4
  363.9 31.8 reduce-scatter.6
  454.8 31.6 reduce-scatter.10
  489.0 31.4 reduce-scatter.8

commit v3 on v2

--- a/solution.py
+++ b/solution.py
@@ -237,7 +237,7 @@
     for at, column in enumerate((gates[0], gates[1], total, picked[0], picked[1])):
         packed = jnp.where(lane == at, column, packed)
     gates_out[...] = packed
-    send_out[...] = (dot(to_first[...], n2) + dot(to_second[...], n2)).astype(BF)
+    send_out[...] = dot(to_first[...] + to_second[...], n2).astype(BF)
     if last:
         send_gates_out[...] = (
             dot(to_first[...], two_lanes(gates[0])) + dot(to_second[...], two_lanes(gates[1]))
@@ -444,9 +444,7 @@
     tail = full_ref[:, 4 * width :]
     norms = norm_rows(tail, experts)
     rows = rows_ref[...]
-    grad_n2 = (
-        dot(take_first[...], rows) + dot(take_second[...], rows) + dot_last(grad_logits, tail)
-    )
+    grad_n2 = dot(take_first[...] + take_second[...], rows) + dot_last(grad_logits, tail)
     unit2, inverse2 = normalize(x1)
     n2 = (unit2 * norms[1:2] + norms[3:4]).astype(BF)
     grad_x1 = g + norm_backward(grad_n2, unit2, inverse2, norms[1:2])
@@ -670,7 +668,7 @@
     tokens, width = x_in.shape
     images = tokens // SEQ
     padded = up16(SEQ)
-    capacity = up16(4 * tokens // experts)
+    capacity = -(-(4 * tokens // experts) // 8) * 8
     slots = experts * capacity
     total = images * padded
 
@@ -756,6 +754,7 @@
                 outs,
                 args,
                 dense_flops,
+                after=weights[moved_at] if last else [],
             )
         )
         if combine:

time: 570 us -> 558 us (0.979)
  waiting for transfers between devices: 199 us -> 161 us
  blocking collectives: 0 us -> 25.9 us
    all_to_all x11 -> x10, waiting for transfers between devices: 93.3 us -> 53.7 us  [exchange(): return lax.all_to_all(rows, over, split_axis=0, concat_axis=0, tiled=True)]
    all_to_all x0 -> x1, blocking collectives: none -> 25.9 us  [exchange(): return lax.all_to_all(rows, over, split_axis=0, concat_axis=0, tiled=True)]
    all_to_all x11 -> x10, starting transfers between devices: 52.6 us -> 55.8 us  [exchange(): return lax.all_to_all(rows, over, split_axis=0, concat_axis=0, tiled=True)]
  transfers between devices with their start and end apart: 41 -> 40, of which waited for: 18 -> 15; matrix products, arithmetic and copies ran while one was open for 10% -> 10% of each run, Pallas kernels for 27% -> 27%
where the time goes in v3:
time: 558 us; the launch traced here: 551 us
  waiting for transfers between devices  161 us (29%)
  Pallas kernels  154 us (28%)
  starting transfers between devices  129 us (23%)
  local copies, waits for them, and re-layouts  36.7 us (7%)
  other arithmetic  29.7 us (5%)
  blocking collectives  25.9 us (5%)
  between operations  14.6 us (3%)
    ppermute x19, waiting for transfers between devices, other(): return lax.ppermute(values, axis, [(0, 1), (1, 0)])  106 us
    pallas_call x8, Pallas kernels, call(): pl.pallas_call(functools.partial(behind, kernel, len(after)), in_specs=[p...  76 us
    ppermute x19, starting transfers between devices, other(): return lax.ppermute(values, axis, [(0, 1), (1, 0)])  59.9 us
    all_to_all x10, starting transfers between devices, exchange(): return lax.all_to_all(rows, over, split_axis=0, concat_axis=0, tiled=True)  55.8 us
    all_to_all x10, waiting for transfers between devices, exchange(): return lax.all_to_all(rows, over, split_axis=0, concat_axis=0, tiled=True)  53.7 us
    pallas_call x2, Pallas kernels, expert_forward(): pl.pallas_call(functools.partial(behind, functools.partial(expert_forward...  29.7 us
    all_to_all x1, blocking collectives, exchange(): return lax.all_to_all(rows, over, split_axis=0, concat_axis=0, tiled=True)  25.9 us
    pallas_call x2, Pallas kernels, expert_weights(): pl.pallas_call(expert_weights_kernel, grid=(pieces,), in_specs=[pl.BlockS...  24.6 us
  transfers between devices with their start and end apart: 40, of which 15 were waited for; matrix products, arithmetic and copies ran while one was open for 10% of the time, Pallas kernels for 27%

profile of v3, /device:TPU:0, one launch (start us, length us, event | category | flops | bytes accessed | tf_op | source)
XLA Modules:
  0.0 550.7 jit_solution(2261462815166146559)
XLA Ops:
  10.3 3.0 collective-permute-start
  13.3 2.5 collective-permute-done
  16.8 3.1 collective-permute-start.1
  21.6 3.8 collective-permute-done.1
  28.9 3.1 slice_bitcast_fusion
  36.6 8.8 %shard_map.203 = (bf16[416,1600]{1,0:T(8,128)(2,1)}, bf16[416,1600]{1,0:T(8,128)(2,1)}, bf16[1600,416]{1,0:T(8,128)(2,1)}, bf16[1600,416]{1,0:T(8,128)(2,1)}, bf...) custom-call(s32[2,416,2]{2,1,0:T(8,128)} %copy.113.refs_0_, ...), custom_call_target="tpu_custom_call" | custom-call | flops 177209344 | bytes 12727296 | tf_op jit(solution)/shard_map/pallas_call | solution.py:131
  45.4 2.3 constant_dynamic-slice_fusion.3
  54.2 11.7 %collective-permute-done.4 = bf16[2,2,2,1,16,2176]{5,4,2,1,0,3:T(8,128)(2,1)} collective-permute-done((bf16[2,2,2,1,16,2176]{5,4,2,1,0,3:T(8,128)(2,1)}, bf16[2,2,2,1,16,2176]{5,4,2,1,0,3:T(8,128)(2,1)}, u32[]{:S(2)}, u32[]{:S(2)}) %collective-permute-start.4) | collective-permute-done | bytes 557088 | tf_op jit(solution)/shard_map/ppermute | solution.py:554
  68.3 9.1 %collective-permute-start.6 = (bf16[2,2,2,2,1,16,2176]{6,5,3,2,1,0,4:T(8,128)(2,1)}, bf16[2,2,2,2,1,16,2176]{6,5,3,2,1,0,4:T(8,128)(2,1)}, u32[]{:S(2)}, u32[]{:S(2)}) collective-permute-start(bf16[2,2,2,2,1,16,2176]{6,5,3,2,1,0,4:T(8,128)(2,1)} %pad_maximum_fusion.3), channel_id=1, source_target_pairs={{0,8},{8,0},{1,9},{9,1},{2,10},{10,2},{3,11},{11,3},{4,12},{12,4},... | collective-permute-start | bytes 3342344 | tf_op jit(solution)/shard_map/ppermute | solution.py:554
  83.4 8.7 %shard_map.204 = (f32[416,512]{1,0:T(8,128)}, bf16[416,1536]{1,0:T(8,128)(2,1)}, bf16[416,512]{1,0:T(8,128)(2,1)}, f32[416,128]{1,0:T(8,128)}, f32[416,128]{1,0:...) custom-call(f32[416,512]{1,0:T(8,128)} %bitcast_convert_fusion.refs_0_.refs_11_, ...), custom_call_target="tpu_custom_call" | custom-call | flops 2917138432 | bytes 10583296 | tf_op jit(solution)/shard_map/pallas_call | solution.py:131
  92.1 5.2 all-to-all-start
  99.5 19.5 %collective-permute-done.11 = bf16[2,2,1,16,2176]{4,3,1,0,2:T(8,128)(2,1)S(1)} collective-permute-done((bf16[2,2,1,16,2176]{4,3,1,0,2:T(8,128)(2,1)S(1)}, bf16[2,2,1,16,2176]{4,3,1,0,2:T(8,128)(2,1)S(1)}, u32[]{:S(2)}, u32[]{:S(2)}) %collective-permute-start.11) | collective-permute-done | bytes 278560 | tf_op jit(solution)/shard_map/ppermute | solution.py:554
  124.6 11.1 %all-to-all-done = bf16[8,200,512]{2,1,0:T(8,128)(2,1)} async-done(((bf16[8,200,512]{2,1,0:T(8,128)(2,1)}), bf16[8,200,512]{2,1,0:T(8,128)(2,1)}, u32[]{:S(2)}, u32[]{:S(2)}) %all-to-all-start) | async-done | bytes 1638432 | tf_op jit(solution)/shard_map/all_to_all | solution.py:693
  135.7 3.5 all-to-all-start.1
  141.6 14.5 %shard_map.205 = (bf16[1600,2048]{1,0:T(8,128)(2,1)}, bf16[1600,2048]{1,0:T(8,128)(2,1)}, bf16[1600,512]{1,0:T(8,128)(2,1)}) custom-call(bf16[512,1024]{1,0:T(8,128)(2,1)} %collective-permute-done.2.refs_0_, bf16[512,1024]{1,0:T(8,128)(2,1)} %collective-permute-done.7.refs_1_, bf16[1024,512]{1,0:T(8,128)(2,1)} %collective-permute-done.5.refs_2_, ...), custom_call_target="tpu_custom_call" | custom-call | flops 6710886400 | bytes 20578304 | tf_op jit(solution)/shard_map/pallas_call | solution.py:295
  157.0 5.3 all-to-all-start.2
  163.1 17.2 %collective-permute-start.13 = (bf16[2,2,2,2,1,16,2176]{6,5,3,2,1,0,4:T(8,128)(2,1)S(1)}, bf16[2,2,2,2,1,16,2176]{6,5,3,2,1,0,4:T(8,128)(2,1)S(1)}, u32[]{:S(2)}, u32[]{:S(2)}) collective-permute-start(bf16[2,2,2,2,1,16,2176]{6,5,3,2,1,0,4:T(8,128)(2,1)S(1)} %bitcast.200), channel_id=1, source_target_pairs={{0,8},{8,0},{1,9},{9,1},{2,10},{10,2},{3,11},{11,3},{4,12},{12,4},... | collective-permute-start | bytes 3342344 | tf_op jit(solution)/shard_map/ppermute | solution.py:554
  180.3 2.4 bitcast_select_fusion.1
  189.3 15.4 %all-to-all-start.3 = ((bf16[8,200,256]{2,1,0:T(8,128)(2,1)}), bf16[8,200,256]{2,1,0:T(8,128)(2,1)S(1)}, u32[]{:S(2)}, u32[]{:S(2)}) async-start(bf16[8,200,256]{2,1,0:T(8,128)(2,1)} %bitcast.59), calls=%async_computation.3 | async-start | bytes 1638400 | tf_op jit(solution)/shard_map/all_to_all | solution.py:693
  207.9 12.7 %shard_map.206 = (f32[416,512]{1,0:T(8,128)}, bf16[416,512]{1,0:T(8,128)(2,1)}, bf16[416,512]{1,0:T(8,128)(2,1)}, f32[416,512]{1,0:T(8,128)}, bf16[416,1536]{1,0...) custom-call(bf16[512,2048]{1,0:T(8,128)(2,1)} %pad_maximum_fusion.1., ...), custom_call_target="tpu_custom_call" | custom-call | flops 2917138432 | bytes 17210624 | tf_op jit(solution)/shard_map/pallas_call | solution.py:131
  220.6 25.9 %all_to_all.128 = bf16[8,200,512]{2,1,0:T(8,128)(2,1)} all-to-all(bf16[8,200,512]{2,1,0:T(8,128)(2,1)} %bitcast.226), channel_id=1, replica_groups=mesh['d0'=2,'d1'=2,'e0'=2,'e1'=2,'e2'=2] {'d1','e1','e2'}, dimensions={0} | all-to-all | bytes 3276800 | tf_op jit(solution)/shard_map/all_to_all | solution.py:693
  246.5 3.5 all-to-all-start.5
  250.0 15.2 %shard_map.207 = (bf16[1600,2048]{1,0:T(8,128)(2,1)}, bf16[1600,2048]{1,0:T(8,128)(2,1)}, bf16[1600,512]{1,0:T(8,128)(2,1)}, bf16[1600,128]{1,0:T(8,128)(2,1)}) custom-call(bf16[1600,256]{1,0:T(8,128)(2,1)} %bitcast.236, bf16[1600,256]{1,0:T(8,128)(2,1)} %bitcast.238, bf16[1600,512]{1,0:T(8,128)(2,1)} %bitcast.222, ...), custom_call_target="tpu_custom_call" | custom-call | flops 6710886400 | bytes 20578304 | tf_op jit(solution)/shard_map/pallas_call | solution.py:295
  265.2 4.1 all-to-all-start.6
  269.3 12.3 %shard_map.208 = (bf16[1600,2048]{1,0:T(8,128)(2,1)}, bf16[1600,512]{1,0:T(8,128)(2,1)}, bf16[1600,512]{1,0:T(8,128)(2,1)}) custom-call(bf16[1600,256]{1,0:T(8,128)(2,1)} %bitcast.237, bf16[1600,256]{1,0:T(8,128)(2,1)} %bitcast.239, bf16[1600,128]{1,0:T(8,128)(2,1)} %bitcast.242, bf16[1600,2048]{1,0:T(8,128)(2,1)} %get-tuple-element.141.refs_3_, ...), custom_call_target="tpu_custom_call" | custom-call | flops 6710886400 | bytes 20578304 | tf_op jit(solution)/shard_map/pallas_call | solution.py:351
  282.4 4.6 all-to-all-start.7
  287.0 12.3 %shard_map.209 = (bf16[4,512,512]{2,1,0:T(8,128)(2,1)}, bf16[4,512,512]{2,1,0:T(8,128)(2,1)}) custom-call(bf16[1600,512]{1,0:T(8,128)(2,1)} %bitcast.223, bf16[1600,2048]{1,0:T(8,128)(2,1)} %get-tuple-element.145.hidden_ref, bf16[1600,2048]{1,0:T(8,128)(2,1)} %get-tuple-element.146.active_ref, bf16[1600,512]{1,0:T(8,128)(2,1)} %get-tuple-element.147.grad_ref), custom_call_target="tpu_custom_call" | custom-call | flops 6710886400 | bytes 20578304 | tf_op jit(solution)/shard_map/pallas_call | solution.py:382
  299.3 8.9 %all-to-all-done.7 = bf16[8,200,512]{2,1,0:T(8,128)(2,1)S(1)} async-done(((bf16[8,200,512]{2,1,0:T(8,128)(2,1)}), bf16[8,200,512]{2,1,0:T(8,128)(2,1)S(1)}, u32[]{:S(2)}, u32[]{:S(2)}) %all-to-all-start.7) | async-done | bytes 1638432 | tf_op jit(solution)/shard_map/all_to_all | solution.py:693
  309.4 3.6 all-to-all-start.8
  315.1 18.5 %shard_map.211 = (f32[416,512]{1,0:T(8,128)}, bf16[512,2176]{1,0:T(8,128)(2,1)}, bf16[1600,512]{1,0:T(8,128)(2,1)}) custom-call(bf16[4,512,512]{2,1,0:T(8,128)(2,1)} %get-tuple-element.148.refs_0_, bf16[4,512,512]{2,1,0:T(8,128)(2,1)} %get-tuple-element.149.refs_1_, f32[416,512]{1,0:T(8,128)} %bitcast_convert_fusion.1.refs_2_, bf16[1600,512]{1,0:T(8,128)(2,1)} %bitcast.218, ...), custom_call_target="tpu_custom_call" | custom-call | flops 5834276864 | bytes 19434752 | tf_op jit(solution)/shard_map/pallas_call | solution.py:131
  338.0 4.8 all-to-all-start.9
  349.1 5.3 shard_map.210
  354.4 20.7 %collective-permute-done.15 = bf16[2,2,2,16,2176]{4,3,1,0,2:T(8,128)(2,1)S(1)} collective-permute-done((bf16[2,2,2,16,2176]{4,3,1,0,2:T(8,128)(2,1)S(1)}, bf16[2,2,2,16,2176]{4,3,1,0,2:T(8,128)(2,1)S(1)}, u32[]{:S(2)}, u32[]{:S(2)}) %collective-permute-start.15) | collective-permute-done | bytes 557088 | tf_op jit(solution)/shard_map/ppermute | solution.py:554
  375.1 6.7 %all-to-all-done.9 = bf16[8,200,512]{2,1,0:T(8,128)(2,1)} async-done(((bf16[8,200,512]{2,1,0:T(8,128)(2,1)}), bf16[8,200,512]{2,1,0:T(8,128)(2,1)}, u32[]{:S(2)}, u32[]{:S(2)}) %all-to-all-start.9) | async-done | bytes 1638432 | tf_op jit(solution)/shard_map/all_to_all | solution.py:693
  382.5 3.7 all-to-all-start.10
  386.3 11.3 %shard_map.212 = (bf16[1600,2048]{1,0:T(8,128)(2,1)}, bf16[1600,512]{1,0:T(8,128)(2,1)}) custom-call(bf16[1600,512]{1,0:T(8,128)(2,1)} %bitcast.73.refs_0_.grad_ref, bf16[1600,2048]{1,0:T(8,128)(2,1)} %get-tuple-element.161.refs_1_, bf16[2,1,512,2048]{3,2,1,0:T(8,128)(2,1)} %refs_2_.2, bf16[2,1,2048,512]{3,2,1,0:T(8,128)(2,1)} %refs_3_.3), custom_call_target="tpu_custom_call" | custom-call | flops 6710886400 | bytes 20578304 | tf_op jit(solution)/shard_map/pallas_call | solution.py:351
  397.7 5.8 %all-to-all-start.11 = ((bf16[8,200,512]{2,1,0:T(8,128)(2,1)}), bf16[8,200,512]{2,1,0:T(8,128)(2,1)S(1)}, u32[]{:S(2)}, u32[]{:S(2)}) async-start(bf16[8,200,512]{2,1,0:T(8,128)(2,1)} %bitcast.224), calls=%async_computation.11 | async-start | bytes 3276800 | tf_op jit(solution)/shard_map/all_to_all | solution.py:693
  403.5 12.3 %shard_map.213 = (bf16[4,512,512]{2,1,0:T(8,128)(2,1)}, bf16[4,512,512]{2,1,0:T(8,128)(2,1)}) custom-call(bf16[1600,512]{1,0:T(8,128)(2,1)} %bitcast.43.refs_5_.rows_ref, bf16[1600,2048]{1,0:T(8,128)(2,1)} %get-tuple-element.162.hidden_ref, bf16[1600,2048]{1,0:T(8,128)(2,1)} %get-tuple-element.163.active_ref, bf16[1600,512]{1,0:T(8,128)(2,1)} %bitcast.73.refs_0_.grad_ref), custom_call_target="tpu_custom_call" | custom-call | flops 6710886400 | bytes 20578304 | tf_op jit(solution)/shard_map/pallas_call | solution.py:382
  415.8 26.4 %all-to-all-done.11 = bf16[8,200,512]{2,1,0:T(8,128)(2,1)S(1)} async-done(((bf16[8,200,512]{2,1,0:T(8,128)(2,1)}), bf16[8,200,512]{2,1,0:T(8,128)(2,1)S(1)}, u32[]{:S(2)}, u32[]{:S(2)}) %all-to-all-start.11) | async-done | bytes 1638432 | tf_op jit(solution)/shard_map/all_to_all | solution.py:693
  443.4 15.9 %shard_map.214 = (f32[416,512]{1,0:T(8,128)}, bf16[512,2176]{1,0:T(8,128)(2,1)}) custom-call(bf16[4,512,512]{2,1,0:T(8,128)(2,1)} %get-tuple-element.164.refs_0_, bf16[4,512,512]{2,1,0:T(8,128)(2,1)} %get-tuple-element.165.refs_1_, f32[416,512]{1,0:T(8,128)} %get-tuple-element.166.refs_2_, bf16[1600,512]{1,0:T(8,128)(2,1)} %bitcast.219, ...), custom_call_target="tpu_custom_call" | custom-call | flops 5834276864 | bytes 15363328 | tf_op jit(solution)/shard_map/pallas_call | solution.py:131
  461.2 9.7 %collective-permute-start.17 = (bf16[2,2,2,2,16,2176]{5,4,1,0,2,3:T(8,128)(2,1)S(1)}, bf16[2,2,2,2,16,2176]{5,4,1,0,2,3:T(8,128)(2,1)S(1)}, u32[]{:S(2)}, u32[]{:S(2)}) collective-permute-start(bf16[2,2,2,2,16,2176]{5,4,1,0,2,3:T(8,128)(2,1)S(1)} %copy_bitcast_fusion.1), channel_id=1, source_target_pairs={{0,8},{8,0},{1,9},{9,1},{2,10},{10,2},{3,11},{11,3},{4,12},{12,4},... | collective-permute-start | bytes 3342344 | tf_op jit(solution)/shard_map/ppermute | solution.py:554
  470.9 2.4 collective-permute-done.17
  475.0 13.7 %collective-permute-done.18 = bf16[2,2,2,16,2176]{4,3,1,0,2:T(8,128)(2,1)} collective-permute-done((bf16[2,2,2,16,2176]{4,3,1,0,2:T(8,128)(2,1)S(1)}, bf16[2,2,2,16,2176]{4,3,1,0,2:T(8,128)(2,1)}, u32[]{:S(2)}, u32[]{:S(2)}) %collective-permute-start.18) | collective-permute-done | bytes 557088 | tf_op jit(solution)/shard_map/ppermute | solution.py:554
  492.8 19.9 %collective-permute-done.19 = bf16[2,2,2,16,2176]{4,3,2,1,0:T(8,128)(2,1)} collective-permute-done((bf16[2,2,2,16,2176]{4,3,2,1,0:T(8,128)(2,1)S(1)}, bf16[2,2,2,16,2176]{4,3,2,1,0:T(8,128)(2,1)}, u32[]{:S(2)}, u32[]{:S(2)}) %collective-permute-start.19) | collective-permute-done | bytes 557088 | tf_op jit(solution)/shard_map/ppermute | solution.py:554
  515.7 4.9 collective-permute-done.21
  521.7 4.0 collective-permute-start.24
  530.3 7.1 %collective-permute-done.22.refs_1_ = bf16[2,16,2176]{2,1,0:T(8,128)(2,1)S(1)} collective-permute-done((bf16[2,16,2176]{2,1,0:T(8,128)(2,1)S(1)}, bf16[2,16,2176]{2,1,0:T(8,128)(2,1)S(1)}, u32[]{:S(2)}, u32[]{:S(2)}) %collective-permute-start.22) | collective-permute-done | bytes 139296 | tf_op jit(solution)/shard_map/ppermute | solution.py:554
  538.4 4.2 shard_map.215
  (196 shorter events, 85.6 us)
Async XLA Ops:
  10.3 5.5 %collective-permute-start = (bf16[1,16,2176]{2,1,0:T(8,128)(2,1)}, bf16[1,16,2176]{2,1,0:T(8,128)(2,1)S(1)}, u32[]{:S(2)}, u32[]{:S(2)}) collective-permute-start(bf16[1,16,2176]{2,1,0:T(8,128)(2,1)} %bitcast.244), channel_id=1, source_target_pairs={{0,2},{2,0},{1,3},{3,1},{4,6},{6,4},{5,7},{7,5},{8,10},{10,8},{9,1... | collective-permute-start | bytes 208904 | tf_op jit(solution)/shard_map/ppermute | solution.py:554
  16.8 8.6 %collective-permute-start.1 = (bf16[2,1,16,2176]{3,2,0,1:T(8,128)(2,1)S(1)}, bf16[2,1,16,2176]{3,2,0,1:T(8,128)(2,1)S(1)}, u32[]{:S(2)}, u32[]{:S(2)}) collective-permute-start(bf16[2,1,16,2176]{3,2,0,1:T(8,128)(2,1)S(1)} %pad_maximum_fusion.9), channel_id=1, source_target_pairs={{0,4},{4,0},{1,5},{5,1},{2,6},{6,2},{3,7},{7,3},{8,12},{12,8},{9,1... | collective-permute-start | bytes 417800 | tf_op jit(solution)/shard_map/ppermute | solution.py:554
  27.2 22.7 %collective-permute-start.2 = (bf16[512,1024]{1,0:T(8,128)(2,1)}, bf16[512,1024]{1,0:T(8,128)(2,1)}, u32[]{:S(2)}, u32[]{:S(2)}) collective-permute-start(bf16[512,1024]{1,0:T(8,128)(2,1)} %constant_dynamic-slice_fusion.4), channel_id=1, source_target_pairs={{8,12},{12,8},{9,13},{13,9},{10,14},{14,10},{11,15},{15,11},{24,28... | collective-permute-start | bytes 3145736 | tf_op jit(solution)/shard_map/ppermute | solution.py:560
  32.0 17.9 %collective-permute-start.3 = (bf16[2,2,1,16,2176]{4,3,1,0,2:T(8,128)(2,1)}, bf16[2,2,1,16,2176]{4,3,1,0,2:T(8,128)(2,1)}, u32[]{:S(2)}, u32[]{:S(2)}) collective-permute-start(bf16[2,2,1,16,2176]{4,3,1,0,2:T(8,128)(2,1)} %pad_maximum_fusion.7), channel_id=1, source_target_pairs={{0,1},{1,0},{2,3},{3,2},{4,5},{5,4},{6,7},{7,6},{8,9},{9,8},{10,11... | collective-permute-start | bytes 835592 | tf_op jit(solution)/shard_map/ppermute | solution.py:554
  47.7 6.5 %collective-permute-start.5 = (bf16[1024,512]{1,0:T(8,128)(2,1)}, bf16[1024,512]{1,0:T(8,128)(2,1)}, u32[]{:S(2)}, u32[]{:S(2)}) collective-permute-start(bf16[1024,512]{1,0:T(8,128)(2,1)} %constant_dynamic-slice_fusion.3), channel_id=1, source_target_pairs={{8,12},{12,8},{9,13},{13,9},{10,14},{14,10},{11,15},{15,11},{24,28... | collective-permute-start | bytes 3145736 | tf_op jit(solution)/shard_map/ppermute | solution.py:560
  51.9 14.1 %collective-permute-start.4 = (bf16[2,2,2,1,16,2176]{5,4,2,1,0,3:T(8,128)(2,1)}, bf16[2,2,2,1,16,2176]{5,4,2,1,0,3:T(8,128)(2,1)}, u32[]{:S(2)}, u32[]{:S(2)}) collective-permute-start(bf16[2,2,2,1,16,2176]{5,4,2,1,0,3:T(8,128)(2,1)} %pad_maximum_fusion.5), channel_id=1, source_target_pairs={{0,16},{16,0},{1,17},{17,1},{2,18},{18,2},{3,19},{19,3},{4,20},{20... | collective-permute-start | bytes 1671176 | tf_op jit(solution)/shard_map/ppermute | solution.py:554
  53.4 25.1 %collective-permute-start.9 = (bf16[1,16,2176]{2,1,0:T(8,128)(2,1)}, bf16[1,16,2176]{2,1,0:T(8,128)(2,1)}, u32[]{:S(2)}, u32[]{:S(2)}) collective-permute-start(bf16[1,16,2176]{2,1,0:T(8,128)(2,1)} %bitcast.27), channel_id=1, source_target_pairs={{0,2},{2,0},{1,3},{3,1},{4,6},{6,4},{5,7},{7,5},{8,10},{10,8},{9,1... | collective-permute-start | bytes 208904 | tf_op jit(solution)/shard_map/ppermute | solution.py:554
  68.3 11.8 %collective-permute-start.6 = (bf16[2,2,2,2,1,16,2176]{6,5,3,2,1,0,4:T(8,128)(2,1)}, bf16[2,2,2,2,1,16,2176]{6,5,3,2,1,0,4:T(8,128)(2,1)}, u32[]{:S(2)}, u32[]{:S(2)}) collective-permute-start(bf16[2,2,2,2,1,16,2176]{6,5,3,2,1,0,4:T(8,128)(2,1)} %pad_maximum_fusion.3), channel_id=1, source_target_pairs={{0,8},{8,0},{1,9},{9,1},{2,10},{10,2},{3,11},{11,3},{4,12},{12,4},... | collective-permute-start | bytes 3342344 | tf_op jit(solution)/shard_map/ppermute | solution.py:554
  80.1 17.2 %collective-permute-start.10 = (bf16[2,1,16,2176]{3,2,0,1:T(8,128)(2,1)}, bf16[2,1,16,2176]{3,2,0,1:T(8,128)(2,1)S(1)}, u32[]{:S(2)}, u32[]{:S(2)}) collective-permute-start(bf16[2,1,16,2176]{3,2,0,1:T(8,128)(2,1)} %pad_maximum_fusion.10), channel_id=1, source_target_pairs={{0,4},{4,0},{1,5},{5,1},{2,6},{6,2},{3,7},{7,3},{8,12},{12,8},{9,1... | collective-permute-start | bytes 417800 | tf_op jit(solution)/shard_map/ppermute | solution.py:554
  92.1 43.6 %all-to-all-start = ((bf16[8,200,512]{2,1,0:T(8,128)(2,1)}), bf16[8,200,512]{2,1,0:T(8,128)(2,1)}, u32[]{:S(2)}, u32[]{:S(2)}) async-start(bf16[8,200,512]{2,1,0:T(8,128)(2,1)} %bitcast.220), calls=%async_computation | async-start | bytes 3276800 | tf_op jit(solution)/shard_map/all_to_all | solution.py:693
  97.4 21.6 %collective-permute-start.11 = (bf16[2,2,1,16,2176]{4,3,1,0,2:T(8,128)(2,1)S(1)}, bf16[2,2,1,16,2176]{4,3,1,0,2:T(8,128)(2,1)S(1)}, u32[]{:S(2)}, u32[]{:S(2)}) collective-permute-start(bf16[2,2,1,16,2176]{4,3,1,0,2:T(8,128)(2,1)S(1)} %pad_maximum_fusion.8), channel_id=1, source_target_pairs={{0,1},{1,0},{2,3},{3,2},{4,5},{5,4},{6,7},{7,6},{8,9},{9,8},{10,11... | collective-permute-start | bytes 835592 | tf_op jit(solution)/shard_map/ppermute | solution.py:554
  119.9 19.4 %collective-permute-start.12 = (bf16[2,2,2,1,16,2176]{5,4,2,1,0,3:T(8,128)(2,1)}, bf16[2,2,2,1,16,2176]{5,4,2,1,0,3:T(8,128)(2,1)}, u32[]{:S(2)}, u32[]{:S(2)}) collective-permute-start(bf16[2,2,2,1,16,2176]{5,4,2,1,0,3:T(8,128)(2,1)} %pad_maximum_fusion.6), channel_id=1, source_target_pairs={{0,16},{16,0},{1,17},{17,1},{2,18},{18,2},{3,19},{19,3},{4,20},{20... | collective-permute-start | bytes 1671176 | tf_op jit(solution)/shard_map/ppermute | solution.py:554
  121.3 20.2 %collective-permute-start.8 = (bf16[1024,512]{1,0:T(8,128)(2,1)}, bf16[1024,512]{1,0:T(8,128)(2,1)}, u32[]{:S(2)}, u32[]{:S(2)}) collective-permute-start(bf16[1024,512]{1,0:T(8,128)(2,1)} %collective-permute-done.5.refs_2_), channel_id=1, source_target_pairs={{8,24},{24,8},{9,25},{25,9},{10,26},{26,10},{11,27},{27,11},{12,28... | collective-permute-start | bytes 3145736 | tf_op jit(solution)/shard_map/ppermute | solution.py:559
  123.0 18.6 %collective-permute-start.7 = (bf16[512,1024]{1,0:T(8,128)(2,1)}, bf16[512,1024]{1,0:T(8,128)(2,1)}, u32[]{:S(2)}, u32[]{:S(2)}) collective-permute-start(bf16[512,1024]{1,0:T(8,128)(2,1)} %collective-permute-done.2.refs_0_), channel_id=1, source_target_pairs={{8,24},{24,8},{9,25},{25,9},{10,26},{26,10},{11,27},{27,11},{12,28... | collective-permute-start | bytes 3145736 | tf_op jit(solution)/shard_map/ppermute | solution.py:559
  135.7 20.4 %all-to-all-start.1 = ((bf16[8,200,256]{2,1,0:T(8,128)(2,1)}), bf16[8,200,256]{2,1,0:T(8,128)(2,1)S(1)}, u32[]{:S(2)}, u32[]{:S(2)}) async-start(bf16[8,200,256]{2,1,0:T(8,128)(2,1)} %bitcast.46), calls=%async_computation.1 | async-start | bytes 1638400 | tf_op jit(solution)/shard_map/all_to_all | solution.py:693
  157.0 32.3 %all-to-all-start.2 = ((bf16[8,200,512]{2,1,0:T(8,128)(2,1)}), bf16[8,200,512]{2,1,0:T(8,128)(2,1)}, u32[]{:S(2)}, u32[]{:S(2)}) async-start(bf16[8,200,512]{2,1,0:T(8,128)(2,1)} %bitcast.221), calls=%async_computation.2 | async-start | bytes 3276800 | tf_op jit(solution)/shard_map/all_to_all | solution.py:693
  163.1 24.3 %collective-permute-start.13 = (bf16[2,2,2,2,1,16,2176]{6,5,3,2,1,0,4:T(8,128)(2,1)S(1)}, bf16[2,2,2,2,1,16,2176]{6,5,3,2,1,0,4:T(8,128)(2,1)S(1)}, u32[]{:S(2)}, u32[]{:S(2)}) collective-permute-start(bf16[2,2,2,2,1,16,2176]{6,5,3,2,1,0,4:T(8,128)(2,1)S(1)} %bitcast.200), channel_id=1, source_target_pairs={{0,8},{8,0},{1,9},{9,1},{2,10},{10,2},{3,11},{11,3},{4,12},{12,4},... | collective-permute-start | bytes 3342344 | tf_op jit(solution)/shard_map/ppermute | solution.py:554
  189.3 31.3 %all-to-all-start.3 = ((bf16[8,200,256]{2,1,0:T(8,128)(2,1)}), bf16[8,200,256]{2,1,0:T(8,128)(2,1)S(1)}, u32[]{:S(2)}, u32[]{:S(2)}) async-start(bf16[8,200,256]{2,1,0:T(8,128)(2,1)} %bitcast.59), calls=%async_computation.3 | async-start | bytes 1638400 | tf_op jit(solution)/shard_map/all_to_all | solution.py:693
  220.6 25.9 %copy-start.17 = (bf16[8,200,256]{2,1,0:T(8,128)(2,1)}, bf16[8,200,256]{2,1,0:T(8,128)(2,1)S(1)}, u32[]{:S(2)}) copy-start(bf16[8,200,256]{2,1,0:T(8,128)(2,1)S(1)} %all-to-all-done.3) | copy-start | bytes 2457604
  246.5 18.7 %all-to-all-start.5 = ((bf16[8,200,128]{2,1,0:T(8,128)(2,1)}), bf16[8,200,128]{2,1,0:T(8,128)(2,1)S(1)}, u32[]{:S(2)}, u32[]{:S(2)}) async-start(bf16[8,200,128]{2,1,0:T(8,128)(2,1)} %bitcast.63), calls=%async_computation.5 | async-start | bytes 819200 | tf_op jit(solution)/shard_map/all_to_all | solution.py:693
  265.2 16.4 %all-to-all-start.6 = ((bf16[8,200,128]{2,1,0:T(8,128)(2,1)}), bf16[8,200,128]{2,1,0:T(8,128)(2,1)S(1)}, u32[]{:S(2)}, u32[]{:S(2)}) async-start(bf16[8,200,128]{2,1,0:T(8,128)(2,1)} %bitcast.243), calls=%async_computation.6 | async-start | bytes 819200 | tf_op jit(solution)/shard_map/all_to_all | solution.py:693
  282.4 25.8 %all-to-all-start.7 = ((bf16[8,200,512]{2,1,0:T(8,128)(2,1)}), bf16[8,200,512]{2,1,0:T(8,128)(2,1)S(1)}, u32[]{:S(2)}, u32[]{:S(2)}) async-start(bf16[8,200,512]{2,1,0:T(8,128)(2,1)} %bitcast.225), calls=%async_computation.7 | async-start | bytes 3276800 | tf_op jit(solution)/shard_map/all_to_all | solution.py:693
  309.4 27.4 %all-to-all-start.8 = ((bf16[8,200,512]{2,1,0:T(8,128)(2,1)}), bf16[8,200,512]{2,1,0:T(8,128)(2,1)S(1)}, u32[]{:S(2)}, u32[]{:S(2)}) async-start(bf16[8,200,512]{2,1,0:T(8,128)(2,1)} %bitcast.69), calls=%async_computation.8 | async-start | bytes 3276800 | tf_op jit(solution)/shard_map/all_to_all | solution.py:693
  313.0 102.9 %reduce-scatter.5.cloned.1.call-start = ((), (), s32[]{:S(2)}) async-start(), calls=%async_computation.16 | async-start | bytes 3145728 | tf_op jit(solution)/shard_map/reduce_scatter | solution.py:596
  336.4 6.5 %collective-permute-start.14 = (bf16[2,2,2,2,16,2176]{5,4,1,0,2,3:T(8,128)(2,1)}, bf16[2,2,2,2,16,2176]{5,4,1,0,2,3:T(8,128)(2,1)}, u32[]{:S(2)}, u32[]{:S(2)}) collective-permute-start(bf16[2,2,2,2,16,2176]{5,4,1,0,2,3:T(8,128)(2,1)} %bitcast.198), channel_id=1, source_target_pairs={{0,8},{8,0},{1,9},{9,1},{2,10},{10,2},{3,11},{11,3},{4,12},{12,4},... | collective-permute-start | bytes 3342344 | tf_op jit(solution)/shard_map/ppermute | solution.py:554
  338.0 43.8 %all-to-all-start.9 = ((bf16[8,200,512]{2,1,0:T(8,128)(2,1)}), bf16[8,200,512]{2,1,0:T(8,128)(2,1)}, u32[]{:S(2)}, u32[]{:S(2)}) async-start(bf16[8,200,512]{2,1,0:T(8,128)(2,1)} %bitcast.217), calls=%async_computation.9 | async-start | bytes 3276800 | tf_op jit(solution)/shard_map/all_to_all | solution.py:693
  342.7 147.4 %reduce-scatter.7.cloned.1.call-start = ((), (), s32[]{:S(2)}) async-start(), calls=%async_computation.17 | async-start | bytes 3145728 | tf_op jit(solution)/shard_map/reduce_scatter | solution.py:596
  345.6 29.5 %collective-permute-start.15 = (bf16[2,2,2,16,2176]{4,3,1,0,2:T(8,128)(2,1)S(1)}, bf16[2,2,2,16,2176]{4,3,1,0,2:T(8,128)(2,1)S(1)}, u32[]{:S(2)}, u32[]{:S(2)}) collective-permute-start(bf16[2,2,2,16,2176]{4,3,1,0,2:T(8,128)(2,1)S(1)} %dynamic-slice_bitcast_fusion.1), channel_id=1, source_target_pairs={{0,1},{1,0},{2,3},{3,2},{4,5},{5,4},{6,7},{7,6},{8,9},{9,8},{10,11... | collective-permute-start | bytes 1671176 | tf_op jit(solution)/shard_map/ppermute | solution.py:554
  349.1 32.7 %copy-start.3 = (bf16[2,2,2,2,16,2176]{5,4,1,0,2,3:T(8,128)(2,1)S(1)}, bf16[2,2,2,2,16,2176]{5,4,1,0,2,3:T(8,128)(2,1)}, u32[]{:S(2)}) copy-start(bf16[2,2,2,2,16,2176]{5,4,1,0,2,3:T(8,128)(2,1)} %copy-done.2) | copy-start | bytes 3342340
  382.5 15.0 %all-to-all-start.10 = ((f32[32,1,128]{2,1,0:T(1,128)}), f32[32,1,128]{2,1,0:T(1,128)S(1)}, u32[]{:S(2)}, u32[]{:S(2)}) async-start(f32[32,1,128]{2,1,0:T(1,128)} %broadcast_in_dim.15), calls=%async_computation.10 | async-start | bytes 32768 | tf_op jit(solution)/shard_map/all_to_all | solution.py:888
  397.7 117.8 %copy-start.29 = (f32[2,8]{1,0:T(2,128)}, f32[2,8]{1,0:T(2,128)S(1)}, u32[]{:S(2)}) copy-start(f32[2,8]{1,0:T(2,128)S(1)} %reshape.172) | copy-start | bytes 196
  397.7 44.5 %all-to-all-start.11 = ((bf16[8,200,512]{2,1,0:T(8,128)(2,1)}), bf16[8,200,512]{2,1,0:T(8,128)(2,1)S(1)}, u32[]{:S(2)}, u32[]{:S(2)}) async-start(bf16[8,200,512]{2,1,0:T(8,128)(2,1)} %bitcast.224), calls=%async_computation.11 | async-start | bytes 3276800 | tf_op jit(solution)/shard_map/all_to_all | solution.py:693
  403.5 126.8 %reduce-scatter.11.cloned.1.call-start = ((), (), s32[]{:S(2)}) async-start(), calls=%async_computation.19 | async-start | bytes 2621440 | tf_op jit(solution)/shard_map/reduce_scatter | solution.py:829
  442.2 17.1 %collective-permute-start.16 = (bf16[2,512,512]{2,1,0:T(8,128)(2,1)}, bf16[2,512,512]{2,1,0:T(8,128)(2,1)S(1)}, u32[]{:S(2)}, u32[]{:S(2)}) collective-permute-start(bf16[2,512,512]{2,1,0:T(8,128)(2,1)} %bitcast.227), channel_id=1, source_target_pairs={{8,12},{12,8},{9,13},{13,9},{10,14},{14,10},{11,15},{15,11},{24,28... | collective-permute-start | bytes 3145736 | tf_op jit(solution)/shard_map/ppermute | solution.py:560
  443.0 87.3 %reduce-scatter.9.cloned.1.call-start = ((), (), s32[]{:S(2)}) async-start(), calls=%async_computation.18 | async-start | bytes 2621440 | tf_op jit(solution)/shard_map/reduce_scatter | solution.py:829
  459.3 14.0 %copy-start.8 = (bf16[512,2176]{1,0:T(8,128)(2,1)S(1)}, bf16[512,2176]{1,0:T(8,128)(2,1)}, u32[]{:S(2)}) copy-start(bf16[512,2176]{1,0:T(8,128)(2,1)} %get-tuple-element.179) | copy-start | bytes 6684676
  459.3 11.6 %copy-start.13 = (bf16[2,512,512]{2,1,0:T(8,128)(2,1)}, bf16[2,512,512]{2,1,0:T(8,128)(2,1)S(1)}, u32[]{:S(2)}) copy-start(bf16[2,512,512]{2,1,0:T(8,128)(2,1)S(1)} %collective-permute-done.16) | copy-start | bytes 3145732
  461.2 12.1 %collective-permute-start.17 = (bf16[2,2,2,2,16,2176]{5,4,1,0,2,3:T(8,128)(2,1)S(1)}, bf16[2,2,2,2,16,2176]{5,4,1,0,2,3:T(8,128)(2,1)S(1)}, u32[]{:S(2)}, u32[]{:S(2)}) collective-permute-start(bf16[2,2,2,2,16,2176]{5,4,1,0,2,3:T(8,128)(2,1)S(1)} %copy_bitcast_fusion.1), channel_id=1, source_target_pairs={{0,8},{8,0},{1,9},{9,1},{2,10},{10,2},{3,11},{11,3},{4,12},{12,4},... | collective-permute-start | bytes 3342344 | tf_op jit(solution)/shard_map/ppermute | solution.py:554
  473.7 15.1 %collective-permute-start.18 = (bf16[2,2,2,16,2176]{4,3,1,0,2:T(8,128)(2,1)S(1)}, bf16[2,2,2,16,2176]{4,3,1,0,2:T(8,128)(2,1)}, u32[]{:S(2)}, u32[]{:S(2)}) collective-permute-start(bf16[2,2,2,16,2176]{4,3,1,0,2:T(8,128)(2,1)S(1)} %dynamic-slice_bitcast_fusion), channel_id=1, source_target_pairs={{0,1},{1,0},{2,3},{3,2},{4,5},{5,4},{6,7},{7,6},{8,9},{9,8},{10,11... | collective-permute-start | bytes 1671176 | tf_op jit(solution)/shard_map/ppermute | solution.py:554
  475.0 16.8 %copy-start.6 = (f32[416,512]{1,0:T(8,128)S(1)}, f32[416,512]{1,0:T(8,128)}, u32[]{:S(2)}) copy-start(f32[416,512]{1,0:T(8,128)} %shard_map.210) | copy-start | bytes 2555908
  490.0 22.7 %collective-permute-start.19 = (bf16[2,2,2,16,2176]{4,3,2,1,0:T(8,128)(2,1)S(1)}, bf16[2,2,2,16,2176]{4,3,2,1,0:T(8,128)(2,1)}, u32[]{:S(2)}, u32[]{:S(2)}) collective-permute-start(bf16[2,2,2,16,2176]{4,3,2,1,0:T(8,128)(2,1)S(1)} %fusion.10), channel_id=1, source_target_pairs={{0,2},{2,0},{1,3},{3,1},{4,6},{6,4},{5,7},{7,5},{8,10},{10,8},{9,1... | collective-permute-start | bytes 1671176 | tf_op jit(solution)/shard_map/ppermute | solution.py:554
  490.1 23.8 %collective-permute-start.20 = (bf16[2,512,512]{2,1,0:T(8,128)(2,1)}, bf16[2,512,512]{2,1,0:T(8,128)(2,1)}, u32[]{:S(2)}, u32[]{:S(2)}) collective-permute-start(bf16[2,512,512]{2,1,0:T(8,128)(2,1)} %bitcast.229), channel_id=1, source_target_pairs={{8,12},{12,8},{9,13},{13,9},{10,14},{14,10},{11,15},{15,11},{24,28... | collective-permute-start | bytes 3145736 | tf_op jit(solution)/shard_map/ppermute | solution.py:560
  492.8 22.7 %copy-start.28 = (f32[2,8]{1,0:T(2,128)S(1)}, f32[2,8]{1,0:T(2,128)}, u32[]{:S(2)}) copy-start(f32[2,8]{1,0:T(2,128)} %param.20) | copy-start | bytes 196
  492.8 27.8 %copy-start.12 = (bf16[1024,512]{1,0:T(8,128)(2,1)S(1)}, bf16[1024,512]{1,0:T(8,128)(2,1)}, u32[]{:S(2)}) copy-start(bf16[1024,512]{1,0:T(8,128)(2,1)} %reduce-scatter.7.cloned.1.call-done) | copy-start | bytes 3145732
  513.9 6.7 %collective-permute-start.21 = (bf16[2,2,16,2176]{3,2,1,0:T(8,128)(2,1)S(1)}, bf16[2,2,16,2176]{3,2,1,0:T(8,128)(2,1)S(1)}, u32[]{:S(2)}, u32[]{:S(2)}) collective-permute-start(bf16[2,2,16,2176]{3,2,1,0:T(8,128)(2,1)S(1)} %dynamic-slice_bitcast_fusion.6), channel_id=1, source_target_pairs={{0,16},{16,0},{1,17},{17,1},{2,18},{18,2},{3,19},{19,3},{4,20},{20... | collective-permute-start | bytes 835592 | tf_op jit(solution)/shard_map/ppermute | solution.py:554
  521.7 15.7 %collective-permute-start.24 = (bf16[512,512]{1,0:T(8,128)(2,1)S(1)}, bf16[512,512]{1,0:T(8,128)(2,1)S(1)}, u32[]{:S(2)}, u32[]{:S(2)}) collective-permute-start(bf16[512,512]{1,0:T(8,128)(2,1)S(1)} %get-tuple-element.254), channel_id=1, source_target_pairs={{0,8},{8,0},{1,9},{9,1},{2,10},{10,2},{3,11},{11,3},{4,12},{12,4},... | collective-permute-start | bytes 1572872 | tf_op jit(solution)/shard_map/ppermute | solution.py:554
  526.7 10.7 %collective-permute-start.23 = (bf16[512,512]{1,0:T(8,128)(2,1)S(1)}, bf16[512,512]{1,0:T(8,128)(2,1)S(1)}, u32[]{:S(2)}, u32[]{:S(2)}) collective-permute-start(bf16[512,512]{1,0:T(8,128)(2,1)S(1)} %get-tuple-element.256), channel_id=1, source_target_pairs={{0,8},{8,0},{1,9},{9,1},{2,10},{10,2},{3,11},{11,3},{4,12},{12,4},... | collective-permute-start | bytes 1572872 | tf_op jit(solution)/shard_map/ppermute | solution.py:554
  528.2 9.2 %collective-permute-start.22 = (bf16[2,16,2176]{2,1,0:T(8,128)(2,1)S(1)}, bf16[2,16,2176]{2,1,0:T(8,128)(2,1)S(1)}, u32[]{:S(2)}, u32[]{:S(2)}) collective-permute-start(bf16[2,16,2176]{2,1,0:T(8,128)(2,1)S(1)} %get-tuple-element.262), channel_id=1, source_target_pairs={{0,4},{4,0},{1,5},{5,1},{2,6},{6,2},{3,7},{7,3},{8,12},{12,8},{9,1... | collective-permute-start | bytes 417800 | tf_op jit(solution)/shard_map/ppermute | solution.py:554
  (22 other events, 61.2 us)
Sparse Core Ops, SparseCore 0:
  316.6 32.2 reduce-scatter.4
  351.8 31.8 reduce-scatter.6
  443.1 31.6 reduce-scatter.10
  477.3 31.4 reduce-scatter.8

commit v4 on v3

--- a/solution.py
+++ b/solution.py
@@ -521,14 +521,14 @@
         out_ref[:, : 3 * width] = qkv_ref[at]
         out_ref[:, 3 * width : 4 * width] = o_ref[at]
         out_ref[:, 4 * width :] = (
-            dot(router_ref[at], router_lanes)
+            dot_first(router_ref[at], router_lanes)
             + dot_first(gains_ref[at], gains_lanes)
             + dot_first(biases_ref[at], biases_lanes)
         ).astype(BF)
 
 
 def finish_kernel(experts, *refs):
-    sums, outs = refs[:8], refs[8:]
+    sums, outs = refs[:12], refs[12:]
     keep_ref, more_ref = sums[:2]
     qkv_out, o_out, router_out, gains_out, biases_out, second_out, in_out, wout_out = outs
     width = o_out.shape[2]
@@ -545,9 +545,13 @@
         gains_out[at] = norms[0:2]
         biases_out[at] = norms[2:4]
         second_out[at : at + 1] = norms[3:4]
-    for whole, keep, more, out_ref in zip(sums[2:4], sums[4:6], sums[6:8], (in_out, wout_out)):
-        out_ref[0, 0] = whole[...].astype(F32)
-        out_ref[1, 0] = keep[...].astype(F32) + more[...].astype(F32)
+    for number, out_ref in enumerate((in_out, wout_out)):
+        out_ref[0, 0] = sums[2 + number][...].astype(F32)
+        for half in range(2):
+            keep_ref, more_ref = sums[4 + 4 * number + 2 * half :][:2]
+            rows = keep_ref.shape[0]
+            at = slice(half * rows, (half + 1) * rows)
+            out_ref[1, 0, at] = keep_ref[...].astype(F32) + more_ref[...].astype(F32)
 
 
 def other(values, axis):
@@ -685,7 +689,7 @@
     shards = call(
         functools.partial(pack_kernel, experts),
         [shape((w_o.shape[1], 4 * width + LANES), BF)] * LAYERS,
-        (w_qkv, w_o, w_router, norm_gains, norm_biases),
+        (w_qkv, w_o, w_router.transpose(0, 2, 1), norm_gains, norm_biases),
         1000,
     )
     def exchange(rows, at):
@@ -823,6 +827,7 @@
         pieces = expert_weights(own["rows"], grad_hidden, own["active"], grad_rows, parts)
         if MOVED[at]:
             moved_pieces = [returned_rows(one, dp_axes) for one in pieces]
+            moved_pieces = [half for one in moved_pieces for half in jnp.split(one, 2, axis=1)]
             out_rows = tie(out_rows, (grad_back, pieces))
         else:
             expert_grads[at] = [
@@ -864,10 +869,11 @@
             first_left = list(axes)
             weight_grads = tie(weight_grads, crossed[0])
             weight_grads = halve(weight_grads, first_left, order_in[0])
-            weight_grads = halve(weight_grads, first_left, order_in[1])
+            weight_grads = halve(weight_grads, first_left, order_in[1], crossed[1])
             both = jnp.stack([weight_grads, sums], axis=-3)
-            both = tie(halve(both, first_left, order_in[2]), crossed[1])
-            for axis in order_in[3:-1]:
+            both = halve(both, first_left, order_in[2], crossed[2])
+            both = halve(both, first_left, order_in[3], crossed[3])
+            for axis in order_in[4:-1]:
                 both = halve(both, first_left, axis)
             dense = [
                 one.reshape(LAYERS, -1, one.shape[-1])
@@ -908,8 +914,8 @@
             shape((LAYERS, 2, rows), F32),
             shape((LAYERS, rows), F32),
         ]
-        + [shape((LAYERS, 1) + one.shape, F32) for one, _ in home],
-        [*dense, *expert_grads[0], home[0][0], home[1][0], home[0][1], home[1][1]],
+        + [shape((LAYERS, 1) + one.shape, F32) for one in expert_grads[0]],
+        [*dense, *expert_grads[0], *(one for pair in home for one in pair)],
         1000,
     )
     grad_qkv, grad_o, grad_router, grad_gains, grad_biases, second, grad_in, grad_out = finished

time: 558 us -> 551 us (0.987)
  starting transfers between devices: 129 us -> 113 us
    ppermute x19 -> x21, starting transfers between devices: 59.9 us -> 50 us  [other(): return lax.ppermute(values, axis, [(0, 1), (1, 0)])]
    all_to_all x10, starting transfers between devices: 55.8 us -> 48 us  [exchange(): return lax.all_to_all(rows, over, split_axis=0, concat_axis=0, tiled=True)]
    all_to_all x10, waiting for transfers between devices: 53.7 us -> 59.9 us  [exchange(): return lax.all_to_all(rows, over, split_axis=0, concat_axis=0, tiled=True)]
    ppermute x19 -> x21, waiting for transfers between devices: 106 us -> 101 us  [other(): return lax.ppermute(values, axis, [(0, 1), (1, 0)])]
  transfers between devices with their start and end apart: 40 -> 44, of which waited for: 15 -> 16; matrix products, arithmetic and copies ran while one was open for 10% -> 11% of each run, Pallas kernels for 27% -> 27%
where the time goes in v4:
time: 551 us; the launch traced here: 544 us
  waiting for transfers between devices  163 us (30%)
  Pallas kernels  155 us (28%)
  starting transfers between devices  113 us (21%)
  local copies, waits for them, and re-layouts  40.1 us (7%)
  other arithmetic  33 us (6%)
  blocking collectives  25.9 us (5%)
  between operations  14.6 us (3%)
    ppermute x21, waiting for transfers between devices, other(): return lax.ppermute(values, axis, [(0, 1), (1, 0)])  101 us
    pallas_call x8, Pallas kernels, call(): pl.pallas_call(functools.partial(behind, kernel, len(after)), in_specs=[p...  76 us
    all_to_all x10, waiting for transfers between devices, exchange(): return lax.all_to_all(rows, over, split_axis=0, concat_axis=0, tiled=True)  59.9 us
    ppermute x21, starting transfers between devices, other(): return lax.ppermute(values, axis, [(0, 1), (1, 0)])  50 us
    all_to_all x10, starting transfers between devices, exchange(): return lax.all_to_all(rows, over, split_axis=0, concat_axis=0, tiled=True)  48 us
    pallas_call x2, Pallas kernels, expert_forward(): pl.pallas_call(functools.partial(behind, functools.partial(expert_forward...  29.8 us
    all_to_all x1, blocking collectives, exchange(): return lax.all_to_all(rows, over, split_axis=0, concat_axis=0, tiled=True)  25.9 us
    pallas_call x2, Pallas kernels, expert_weights(): pl.pallas_call(expert_weights_kernel, grid=(pieces,), in_specs=[pl.BlockS...  25.3 us
  transfers between devices with their start and end apart: 44, of which 16 were waited for; matrix products, arithmetic and copies ran while one was open for 11% of the time, Pallas kernels for 27%

profile of v4, /device:TPU:0, one launch (start us, length us, event | category | flops | bytes accessed | tf_op | source)
XLA Modules:
  0.0 544.4 jit_solution(8912427413004980292)
XLA Ops:
  9.0 3.0 collective-permute-start
  12.0 2.5 collective-permute-done
  15.4 3.1 collective-permute-start.1
  20.3 3.8 collective-permute-done.1
  27.6 3.1 slice_bitcast_fusion
  35.2 8.8 %shard_map.203 = (bf16[416,1600]{1,0:T(8,128)(2,1)}, bf16[416,1600]{1,0:T(8,128)(2,1)}, bf16[1600,416]{1,0:T(8,128)(2,1)}, bf16[1600,416]{1,0:T(8,128)(2,1)}, bf...) custom-call(s32[2,416,2]{2,1,0:T(8,128)} %copy.109.refs_0_, ...), custom_call_target="tpu_custom_call" | custom-call | flops 177209344 | bytes 12727296 | tf_op jit(solution)/shard_map/pallas_call | solution.py:131
  44.0 2.2 constant_dynamic-slice_fusion.3
  52.5 11.3 %collective-permute-done.4 = bf16[2,2,2,1,16,2176]{5,4,2,1,0,3:T(8,128)(2,1)} collective-permute-done((bf16[2,2,2,1,16,2176]{5,4,2,1,0,3:T(8,128)(2,1)}, bf16[2,2,2,1,16,2176]{5,4,2,1,0,3:T(8,128)(2,1)}, u32[]{:S(2)}, u32[]{:S(2)}) %collective-permute-start.4) | collective-permute-done | bytes 557088 | tf_op jit(solution)/shard_map/ppermute | solution.py:558
  66.1 9.9 %collective-permute-start.6 = (bf16[2,2,2,2,1,16,2176]{6,5,3,2,1,0,4:T(8,128)(2,1)}, bf16[2,2,2,2,1,16,2176]{6,5,3,2,1,0,4:T(8,128)(2,1)}, u32[]{:S(2)}, u32[]{:S(2)}) collective-permute-start(bf16[2,2,2,2,1,16,2176]{6,5,3,2,1,0,4:T(8,128)(2,1)} %pad_maximum_fusion.3), channel_id=1, source_target_pairs={{0,8},{8,0},{1,9},{9,1},{2,10},{10,2},{3,11},{11,3},{4,12},{12,4},... | collective-permute-start | bytes 3342344 | tf_op jit(solution)/shard_map/ppermute | solution.py:558
  82.0 8.7 %shard_map.204 = (f32[416,512]{1,0:T(8,128)}, bf16[416,1536]{1,0:T(8,128)(2,1)}, bf16[416,512]{1,0:T(8,128)(2,1)}, f32[416,128]{1,0:T(8,128)}, f32[416,128]{1,0:...) custom-call(f32[416,512]{1,0:T(8,128)} %bitcast_convert_fusion.refs_0_.refs_11_, ...), custom_call_target="tpu_custom_call" | custom-call | flops 2917138432 | bytes 10583296 | tf_op jit(solution)/shard_map/pallas_call | solution.py:131
  90.8 5.2 all-to-all-start
  98.1 19.5 %collective-permute-done.11 = bf16[2,2,1,16,2176]{4,3,1,0,2:T(8,128)(2,1)S(1)} collective-permute-done((bf16[2,2,1,16,2176]{4,3,1,0,2:T(8,128)(2,1)S(1)}, bf16[2,2,1,16,2176]{4,3,1,0,2:T(8,128)(2,1)S(1)}, u32[]{:S(2)}, u32[]{:S(2)}) %collective-permute-start.11) | collective-permute-done | bytes 278560 | tf_op jit(solution)/shard_map/ppermute | solution.py:558
  123.4 10.9 %all-to-all-done = bf16[8,200,512]{2,1,0:T(8,128)(2,1)} async-done(((bf16[8,200,512]{2,1,0:T(8,128)(2,1)}), bf16[8,200,512]{2,1,0:T(8,128)(2,1)}, u32[]{:S(2)}, u32[]{:S(2)}) %all-to-all-start) | async-done | bytes 1638432 | tf_op jit(solution)/shard_map/all_to_all | solution.py:697
  134.3 3.5 all-to-all-start.1
  140.2 14.6 %shard_map.205 = (bf16[1600,2048]{1,0:T(8,128)(2,1)}, bf16[1600,2048]{1,0:T(8,128)(2,1)}, bf16[1600,512]{1,0:T(8,128)(2,1)}) custom-call(bf16[512,1024]{1,0:T(8,128)(2,1)} %collective-permute-done.2.refs_0_, bf16[512,1024]{1,0:T(8,128)(2,1)} %collective-permute-done.7.refs_1_, bf16[1024,512]{1,0:T(8,128)(2,1)} %collective-permute-done.5.refs_2_, ...), custom_call_target="tpu_custom_call" | custom-call | flops 6710886400 | bytes 20578304 | tf_op jit(solution)/shard_map/pallas_call | solution.py:295
  155.7 5.3 all-to-all-start.2
  161.8 15.9 %collective-permute-start.13 = (bf16[2,2,2,2,1,16,2176]{6,5,3,2,1,0,4:T(8,128)(2,1)S(1)}, bf16[2,2,2,2,1,16,2176]{6,5,3,2,1,0,4:T(8,128)(2,1)S(1)}, u32[]{:S(2)}, u32[]{:S(2)}) collective-permute-start(bf16[2,2,2,2,1,16,2176]{6,5,3,2,1,0,4:T(8,128)(2,1)S(1)} %bitcast.209), channel_id=1, source_target_pairs={{0,8},{8,0},{1,9},{9,1},{2,10},{10,2},{3,11},{11,3},{4,12},{12,4},... | collective-permute-start | bytes 3342344 | tf_op jit(solution)/shard_map/ppermute | solution.py:558
  177.7 2.4 bitcast_select_fusion.1
  186.0 9.8 %all-to-all-done.2 = bf16[8,200,512]{2,1,0:T(8,128)(2,1)} async-done(((bf16[8,200,512]{2,1,0:T(8,128)(2,1)}), bf16[8,200,512]{2,1,0:T(8,128)(2,1)}, u32[]{:S(2)}, u32[]{:S(2)}) %all-to-all-start.2) | async-done | bytes 1638432 | tf_op jit(solution)/shard_map/all_to_all | solution.py:697
  195.8 7.7 %all-to-all-start.3 = ((bf16[8,200,256]{2,1,0:T(8,128)(2,1)}), bf16[8,200,256]{2,1,0:T(8,128)(2,1)S(1)}, u32[]{:S(2)}, u32[]{:S(2)}) async-start(bf16[8,200,256]{2,1,0:T(8,128)(2,1)} %bitcast.60), calls=%async_computation.3 | async-start | bytes 1638400 | tf_op jit(solution)/shard_map/all_to_all | solution.py:697
  206.7 12.7 %shard_map.206 = (f32[416,512]{1,0:T(8,128)}, bf16[416,512]{1,0:T(8,128)(2,1)}, bf16[416,512]{1,0:T(8,128)(2,1)}, f32[416,512]{1,0:T(8,128)}, bf16[416,1536]{1,0...) custom-call(bf16[512,2048]{1,0:T(8,128)(2,1)} %pad_maximum_fusion.1., ...), custom_call_target="tpu_custom_call" | custom-call | flops 2917138432 | bytes 17210624 | tf_op jit(solution)/shard_map/pallas_call | solution.py:131
  219.5 25.9 %all_to_all.128 = bf16[8,200,512]{2,1,0:T(8,128)(2,1)} all-to-all(bf16[8,200,512]{2,1,0:T(8,128)(2,1)} %bitcast.236), channel_id=1, replica_groups=mesh['d0'=2,'d1'=2,'e0'=2,'e1'=2,'e2'=2] {'d1','e1','e2'}, dimensions={0} | all-to-all | bytes 3276800 | tf_op jit(solution)/shard_map/all_to_all | solution.py:697
  245.4 3.5 all-to-all-start.5
  248.9 15.2 %shard_map.207 = (bf16[1600,2048]{1,0:T(8,128)(2,1)}, bf16[1600,2048]{1,0:T(8,128)(2,1)}, bf16[1600,512]{1,0:T(8,128)(2,1)}, bf16[1600,128]{1,0:T(8,128)(2,1)}) custom-call(bf16[1600,256]{1,0:T(8,128)(2,1)} %bitcast.244, bf16[1600,256]{1,0:T(8,128)(2,1)} %bitcast.246, bf16[1600,512]{1,0:T(8,128)(2,1)} %bitcast.232, ...), custom_call_target="tpu_custom_call" | custom-call | flops 6710886400 | bytes 20578304 | tf_op jit(solution)/shard_map/pallas_call | solution.py:295
  264.1 4.1 all-to-all-start.6
  268.2 12.3 %shard_map.208 = (bf16[1600,2048]{1,0:T(8,128)(2,1)}, bf16[1600,512]{1,0:T(8,128)(2,1)}, bf16[1600,512]{1,0:T(8,128)(2,1)}) custom-call(bf16[1600,256]{1,0:T(8,128)(2,1)} %bitcast.245, bf16[1600,256]{1,0:T(8,128)(2,1)} %bitcast.247, bf16[1600,128]{1,0:T(8,128)(2,1)} %bitcast.250, bf16[1600,2048]{1,0:T(8,128)(2,1)} %get-tuple-element.147.refs_3_, ...), custom_call_target="tpu_custom_call" | custom-call | flops 6710886400 | bytes 20578304 | tf_op jit(solution)/shard_map/pallas_call | solution.py:351
  281.3 4.4 all-to-all-start.7
  285.7 12.3 %shard_map.209 = (bf16[4,512,512]{2,1,0:T(8,128)(2,1)}, bf16[4,512,512]{2,1,0:T(8,128)(2,1)}) custom-call(bf16[1600,512]{1,0:T(8,128)(2,1)} %bitcast.233, bf16[1600,2048]{1,0:T(8,128)(2,1)} %get-tuple-element.151.hidden_ref, bf16[1600,2048]{1,0:T(8,128)(2,1)} %get-tuple-element.152.active_ref, bf16[1600,512]{1,0:T(8,128)(2,1)} %get-tuple-element.153.grad_ref), custom_call_target="tpu_custom_call" | custom-call | flops 6710886400 | bytes 20578304 | tf_op jit(solution)/shard_map/pallas_call | solution.py:382
  297.9 8.9 %all-to-all-done.7 = bf16[8,200,512]{2,1,0:T(8,128)(2,1)S(1)} async-done(((bf16[8,200,512]{2,1,0:T(8,128)(2,1)}), bf16[8,200,512]{2,1,0:T(8,128)(2,1)S(1)}, u32[]{:S(2)}, u32[]{:S(2)}) %all-to-all-start.7) | async-done | bytes 1638432 | tf_op jit(solution)/shard_map/all_to_all | solution.py:697
  308.0 3.7 all-to-all-start.8
  312.8 18.5 %shard_map.211 = (f32[416,512]{1,0:T(8,128)}, bf16[512,2176]{1,0:T(8,128)(2,1)}, bf16[1600,512]{1,0:T(8,128)(2,1)}) custom-call(bf16[4,512,512]{2,1,0:T(8,128)(2,1)} %get-tuple-element.154.refs_0_, bf16[4,512,512]{2,1,0:T(8,128)(2,1)} %get-tuple-element.155.refs_1_, f32[416,512]{1,0:T(8,128)} %bitcast_convert_fusion.1.refs_2_, bf16[1600,512]{1,0:T(8,128)(2,1)} %bitcast.230, ...), custom_call_target="tpu_custom_call" | custom-call | flops 5834276864 | bytes 19434752 | tf_op jit(solution)/shard_map/pallas_call | solution.py:131
  335.7 4.8 all-to-all-start.9
  347.2 5.4 shard_map.210
  352.6 20.2 %collective-permute-done.15 = bf16[2,2,2,16,2176]{4,3,1,0,2:T(8,128)(2,1)S(1)} collective-permute-done((bf16[2,2,2,16,2176]{4,3,1,0,2:T(8,128)(2,1)S(1)}, bf16[2,2,2,16,2176]{4,3,1,0,2:T(8,128)(2,1)S(1)}, u32[]{:S(2)}, u32[]{:S(2)}) %collective-permute-start.15) | collective-permute-done | bytes 557088 | tf_op jit(solution)/shard_map/ppermute | solution.py:558
  372.8 6.7 %all-to-all-done.9 = bf16[8,200,512]{2,1,0:T(8,128)(2,1)} async-done(((bf16[8,200,512]{2,1,0:T(8,128)(2,1)}), bf16[8,200,512]{2,1,0:T(8,128)(2,1)}, u32[]{:S(2)}, u32[]{:S(2)}) %all-to-all-start.9) | async-done | bytes 1638432 | tf_op jit(solution)/shard_map/all_to_all | solution.py:697
  380.2 3.8 all-to-all-start.10
  384.1 11.3 %shard_map.212 = (bf16[1600,2048]{1,0:T(8,128)(2,1)}, bf16[1600,512]{1,0:T(8,128)(2,1)}) custom-call(bf16[1600,512]{1,0:T(8,128)(2,1)} %bitcast.74.refs_0_.grad_ref, bf16[1600,2048]{1,0:T(8,128)(2,1)} %get-tuple-element.167.refs_1_, bf16[2,1,512,2048]{3,2,1,0:T(8,128)(2,1)} %refs_2_.1, bf16[2,1,2048,512]{3,2,1,0:T(8,128)(2,1)} %refs_3_.3), custom_call_target="tpu_custom_call" | custom-call | flops 6710886400 | bytes 20578304 | tf_op jit(solution)/shard_map/pallas_call | solution.py:351
  395.5 5.8 %all-to-all-start.11 = ((bf16[8,200,512]{2,1,0:T(8,128)(2,1)}), bf16[8,200,512]{2,1,0:T(8,128)(2,1)S(1)}, u32[]{:S(2)}, u32[]{:S(2)}) async-start(bf16[8,200,512]{2,1,0:T(8,128)(2,1)} %bitcast.234), calls=%async_computation.11 | async-start | bytes 3276800 | tf_op jit(solution)/shard_map/all_to_all | solution.py:697
  403.4 13.0 %shard_map.213 = (bf16[4,512,512]{2,1,0:T(8,128)(2,1)}, bf16[4,512,512]{2,1,0:T(8,128)(2,1)}) custom-call(bf16[1600,512]{1,0:T(8,128)(2,1)} %bitcast.44.refs_5_.rows_ref, bf16[1600,2048]{1,0:T(8,128)(2,1)} %get-tuple-element.168.hidden_ref, bf16[1600,2048]{1,0:T(8,128)(2,1)} %get-tuple-element.169.active_ref, bf16[1600,512]{1,0:T(8,128)(2,1)} %bitcast.74.refs_0_.grad_ref), custom_call_target="tpu_custom_call" | custom-call | flops 6710886400 | bytes 20578304 | tf_op jit(solution)/shard_map/pallas_call | solution.py:382
  416.4 23.6 %all-to-all-done.11 = bf16[8,200,512]{2,1,0:T(8,128)(2,1)S(1)} async-done(((bf16[8,200,512]{2,1,0:T(8,128)(2,1)}), bf16[8,200,512]{2,1,0:T(8,128)(2,1)S(1)}, u32[]{:S(2)}, u32[]{:S(2)}) %all-to-all-start.11) | async-done | bytes 1638432 | tf_op jit(solution)/shard_map/all_to_all | solution.py:697
  441.2 15.9 %shard_map.214 = (f32[416,512]{1,0:T(8,128)}, bf16[512,2176]{1,0:T(8,128)(2,1)}) custom-call(bf16[4,512,512]{2,1,0:T(8,128)(2,1)} %get-tuple-element.170.refs_0_, bf16[4,512,512]{2,1,0:T(8,128)(2,1)} %get-tuple-element.171.refs_1_, f32[416,512]{1,0:T(8,128)} %get-tuple-element.172.refs_2_, bf16[1600,512]{1,0:T(8,128)(2,1)} %bitcast.228, ...), custom_call_target="tpu_custom_call" | custom-call | flops 5834276864 | bytes 15363328 | tf_op jit(solution)/shard_map/pallas_call | solution.py:131
  458.8 2.8 collective-permute-done.17
  467.2 11.9 %collective-permute-done.18 = bf16[2,2,2,16,2176]{4,3,1,0,2:T(8,128)(2,1)S(1)} collective-permute-done((bf16[2,2,2,16,2176]{4,3,1,0,2:T(8,128)(2,1)}, bf16[2,2,2,16,2176]{4,3,1,0,2:T(8,128)(2,1)S(1)}, u32[]{:S(2)}, u32[]{:S(2)}) %collective-permute-start.18) | collective-permute-done | bytes 557088 | tf_op jit(solution)/shard_map/ppermute | solution.py:558
  480.2 3.5 collective-permute-start.20
  489.2 14.7 %collective-permute-done.20 = bf16[2,2,2,16,2176]{4,3,2,1,0:T(8,128)(2,1)} collective-permute-done((bf16[2,2,2,16,2176]{4,3,2,1,0:T(8,128)(2,1)}, bf16[2,2,2,16,2176]{4,3,2,1,0:T(8,128)(2,1)}, u32[]{:S(2)}, u32[]{:S(2)}) %collective-permute-start.20) | collective-permute-done | bytes 557088 | tf_op jit(solution)/shard_map/ppermute | solution.py:558
  506.9 9.0 %collective-permute-done.22 = bf16[2,2,16,2176]{3,2,1,0:T(8,128)(2,1)S(1)} collective-permute-done((bf16[2,2,16,2176]{3,2,1,0:T(8,128)(2,1)S(1)}, bf16[2,2,16,2176]{3,2,1,0:T(8,128)(2,1)S(1)}, u32[]{:S(2)}, u32[]{:S(2)}) %collective-permute-start.22) | collective-permute-done | bytes 278560 | tf_op jit(solution)/shard_map/ppermute | solution.py:558
  526.4 4.9 collective-permute-done.24.refs_1_
  532.1 4.2 shard_map.215
  (205 shorter events, 95.5 us)
Async XLA Ops:
  9.0 5.5 %collective-permute-start = (bf16[1,16,2176]{2,1,0:T(8,128)(2,1)}, bf16[1,16,2176]{2,1,0:T(8,128)(2,1)S(1)}, u32[]{:S(2)}, u32[]{:S(2)}) collective-permute-start(bf16[1,16,2176]{2,1,0:T(8,128)(2,1)} %bitcast.252), channel_id=1, source_target_pairs={{0,2},{2,0},{1,3},{3,1},{4,6},{6,4},{5,7},{7,5},{8,10},{10,8},{9,1... | collective-permute-start | bytes 208904 | tf_op jit(solution)/shard_map/ppermute | solution.py:558
  15.4 8.6 %collective-permute-start.1 = (bf16[2,1,16,2176]{3,2,0,1:T(8,128)(2,1)S(1)}, bf16[2,1,16,2176]{3,2,0,1:T(8,128)(2,1)S(1)}, u32[]{:S(2)}, u32[]{:S(2)}) collective-permute-start(bf16[2,1,16,2176]{3,2,0,1:T(8,128)(2,1)S(1)} %pad_maximum_fusion.9), channel_id=1, source_target_pairs={{0,4},{4,0},{1,5},{5,1},{2,6},{6,2},{3,7},{7,3},{8,12},{12,8},{9,1... | collective-permute-start | bytes 417800 | tf_op jit(solution)/shard_map/ppermute | solution.py:558
  25.9 22.3 %collective-permute-start.2 = (bf16[512,1024]{1,0:T(8,128)(2,1)}, bf16[512,1024]{1,0:T(8,128)(2,1)}, u32[]{:S(2)}, u32[]{:S(2)}) collective-permute-start(bf16[512,1024]{1,0:T(8,128)(2,1)} %constant_dynamic-slice_fusion.4), channel_id=1, source_target_pairs={{8,12},{12,8},{9,13},{13,9},{10,14},{14,10},{11,15},{15,11},{24,28... | collective-permute-start | bytes 3145736 | tf_op jit(solution)/shard_map/ppermute | solution.py:564
  30.7 17.5 %collective-permute-start.3 = (bf16[2,2,1,16,2176]{4,3,1,0,2:T(8,128)(2,1)}, bf16[2,2,1,16,2176]{4,3,1,0,2:T(8,128)(2,1)}, u32[]{:S(2)}, u32[]{:S(2)}) collective-permute-start(bf16[2,2,1,16,2176]{4,3,1,0,2:T(8,128)(2,1)} %pad_maximum_fusion.7), channel_id=1, source_target_pairs={{0,1},{1,0},{2,3},{3,2},{4,5},{5,4},{6,7},{7,6},{8,9},{9,8},{10,11... | collective-permute-start | bytes 835592 | tf_op jit(solution)/shard_map/ppermute | solution.py:558
  46.3 6.2 %collective-permute-start.5 = (bf16[1024,512]{1,0:T(8,128)(2,1)}, bf16[1024,512]{1,0:T(8,128)(2,1)}, u32[]{:S(2)}, u32[]{:S(2)}) collective-permute-start(bf16[1024,512]{1,0:T(8,128)(2,1)} %constant_dynamic-slice_fusion.3), channel_id=1, source_target_pairs={{8,12},{12,8},{9,13},{13,9},{10,14},{14,10},{11,15},{15,11},{24,28... | collective-permute-start | bytes 3145736 | tf_op jit(solution)/shard_map/ppermute | solution.py:564
  50.1 13.7 %collective-permute-start.4 = (bf16[2,2,2,1,16,2176]{5,4,2,1,0,3:T(8,128)(2,1)}, bf16[2,2,2,1,16,2176]{5,4,2,1,0,3:T(8,128)(2,1)}, u32[]{:S(2)}, u32[]{:S(2)}) collective-permute-start(bf16[2,2,2,1,16,2176]{5,4,2,1,0,3:T(8,128)(2,1)} %pad_maximum_fusion.5), channel_id=1, source_target_pairs={{0,16},{16,0},{1,17},{17,1},{2,18},{18,2},{3,19},{19,3},{4,20},{20... | collective-permute-start | bytes 1671176 | tf_op jit(solution)/shard_map/ppermute | solution.py:558
  51.6 25.5 %collective-permute-start.9 = (bf16[1,16,2176]{2,1,0:T(8,128)(2,1)}, bf16[1,16,2176]{2,1,0:T(8,128)(2,1)}, u32[]{:S(2)}, u32[]{:S(2)}) collective-permute-start(bf16[1,16,2176]{2,1,0:T(8,128)(2,1)} %bitcast.28), channel_id=1, source_target_pairs={{0,2},{2,0},{1,3},{3,1},{4,6},{6,4},{5,7},{7,5},{8,10},{10,8},{9,1... | collective-permute-start | bytes 208904 | tf_op jit(solution)/shard_map/ppermute | solution.py:558
  66.1 12.6 %collective-permute-start.6 = (bf16[2,2,2,2,1,16,2176]{6,5,3,2,1,0,4:T(8,128)(2,1)}, bf16[2,2,2,2,1,16,2176]{6,5,3,2,1,0,4:T(8,128)(2,1)}, u32[]{:S(2)}, u32[]{:S(2)}) collective-permute-start(bf16[2,2,2,2,1,16,2176]{6,5,3,2,1,0,4:T(8,128)(2,1)} %pad_maximum_fusion.3), channel_id=1, source_target_pairs={{0,8},{8,0},{1,9},{9,1},{2,10},{10,2},{3,11},{11,3},{4,12},{12,4},... | collective-permute-start | bytes 3342344 | tf_op jit(solution)/shard_map/ppermute | solution.py:558
  78.7 17.2 %collective-permute-start.10 = (bf16[2,1,16,2176]{3,2,0,1:T(8,128)(2,1)}, bf16[2,1,16,2176]{3,2,0,1:T(8,128)(2,1)S(1)}, u32[]{:S(2)}, u32[]{:S(2)}) collective-permute-start(bf16[2,1,16,2176]{3,2,0,1:T(8,128)(2,1)} %pad_maximum_fusion.10), channel_id=1, source_target_pairs={{0,4},{4,0},{1,5},{5,1},{2,6},{6,2},{3,7},{7,3},{8,12},{12,8},{9,1... | collective-permute-start | bytes 417800 | tf_op jit(solution)/shard_map/ppermute | solution.py:558
  90.8 43.6 %all-to-all-start = ((bf16[8,200,512]{2,1,0:T(8,128)(2,1)}), bf16[8,200,512]{2,1,0:T(8,128)(2,1)}, u32[]{:S(2)}, u32[]{:S(2)}) async-start(bf16[8,200,512]{2,1,0:T(8,128)(2,1)} %bitcast.229), calls=%async_computation | async-start | bytes 3276800 | tf_op jit(solution)/shard_map/all_to_all | solution.py:697
  96.0 21.6 %collective-permute-start.11 = (bf16[2,2,1,16,2176]{4,3,1,0,2:T(8,128)(2,1)S(1)}, bf16[2,2,1,16,2176]{4,3,1,0,2:T(8,128)(2,1)S(1)}, u32[]{:S(2)}, u32[]{:S(2)}) collective-permute-start(bf16[2,2,1,16,2176]{4,3,1,0,2:T(8,128)(2,1)S(1)} %pad_maximum_fusion.8), channel_id=1, source_target_pairs={{0,1},{1,0},{2,3},{3,2},{4,5},{5,4},{6,7},{7,6},{8,9},{9,8},{10,11... | collective-permute-start | bytes 835592 | tf_op jit(solution)/shard_map/ppermute | solution.py:558
  118.5 19.4 %collective-permute-start.12 = (bf16[2,2,2,1,16,2176]{5,4,2,1,0,3:T(8,128)(2,1)}, bf16[2,2,2,1,16,2176]{5,4,2,1,0,3:T(8,128)(2,1)}, u32[]{:S(2)}, u32[]{:S(2)}) collective-permute-start(bf16[2,2,2,1,16,2176]{5,4,2,1,0,3:T(8,128)(2,1)} %pad_maximum_fusion.6), channel_id=1, source_target_pairs={{0,16},{16,0},{1,17},{17,1},{2,18},{18,2},{3,19},{19,3},{4,20},{20... | collective-permute-start | bytes 1671176 | tf_op jit(solution)/shard_map/ppermute | solution.py:558
  120.2 20.0 %collective-permute-start.8 = (bf16[1024,512]{1,0:T(8,128)(2,1)}, bf16[1024,512]{1,0:T(8,128)(2,1)}, u32[]{:S(2)}, u32[]{:S(2)}) collective-permute-start(bf16[1024,512]{1,0:T(8,128)(2,1)} %collective-permute-done.5.refs_2_), channel_id=1, source_target_pairs={{8,24},{24,8},{9,25},{25,9},{10,26},{26,10},{11,27},{27,11},{12,28... | collective-permute-start | bytes 3145736 | tf_op jit(solution)/shard_map/ppermute | solution.py:563
  121.8 18.4 %collective-permute-start.7 = (bf16[512,1024]{1,0:T(8,128)(2,1)}, bf16[512,1024]{1,0:T(8,128)(2,1)}, u32[]{:S(2)}, u32[]{:S(2)}) collective-permute-start(bf16[512,1024]{1,0:T(8,128)(2,1)} %collective-permute-done.2.refs_0_), channel_id=1, source_target_pairs={{8,24},{24,8},{9,25},{25,9},{10,26},{26,10},{11,27},{27,11},{12,28... | collective-permute-start | bytes 3145736 | tf_op jit(solution)/shard_map/ppermute | solution.py:563
  134.3 20.4 %all-to-all-start.1 = ((bf16[8,200,256]{2,1,0:T(8,128)(2,1)}), bf16[8,200,256]{2,1,0:T(8,128)(2,1)S(1)}, u32[]{:S(2)}, u32[]{:S(2)}) async-start(bf16[8,200,256]{2,1,0:T(8,128)(2,1)} %bitcast.47), calls=%async_computation.1 | async-start | bytes 1638400 | tf_op jit(solution)/shard_map/all_to_all | solution.py:697
  155.7 40.1 %all-to-all-start.2 = ((bf16[8,200,512]{2,1,0:T(8,128)(2,1)}), bf16[8,200,512]{2,1,0:T(8,128)(2,1)}, u32[]{:S(2)}, u32[]{:S(2)}) async-start(bf16[8,200,512]{2,1,0:T(8,128)(2,1)} %bitcast.231), calls=%async_computation.2 | async-start | bytes 3276800 | tf_op jit(solution)/shard_map/all_to_all | solution.py:697
  161.8 23.0 %collective-permute-start.13 = (bf16[2,2,2,2,1,16,2176]{6,5,3,2,1,0,4:T(8,128)(2,1)S(1)}, bf16[2,2,2,2,1,16,2176]{6,5,3,2,1,0,4:T(8,128)(2,1)S(1)}, u32[]{:S(2)}, u32[]{:S(2)}) collective-permute-start(bf16[2,2,2,2,1,16,2176]{6,5,3,2,1,0,4:T(8,128)(2,1)S(1)} %bitcast.209), channel_id=1, source_target_pairs={{0,8},{8,0},{1,9},{9,1},{2,10},{10,2},{3,11},{11,3},{4,12},{12,4},... | collective-permute-start | bytes 3342344 | tf_op jit(solution)/shard_map/ppermute | solution.py:558
  195.8 23.7 %all-to-all-start.3 = ((bf16[8,200,256]{2,1,0:T(8,128)(2,1)}), bf16[8,200,256]{2,1,0:T(8,128)(2,1)S(1)}, u32[]{:S(2)}, u32[]{:S(2)}) async-start(bf16[8,200,256]{2,1,0:T(8,128)(2,1)} %bitcast.60), calls=%async_computation.3 | async-start | bytes 1638400 | tf_op jit(solution)/shard_map/all_to_all | solution.py:697
  219.5 25.9 %copy-start.14 = (bf16[8,200,256]{2,1,0:T(8,128)(2,1)}, bf16[8,200,256]{2,1,0:T(8,128)(2,1)S(1)}, u32[]{:S(2)}) copy-start(bf16[8,200,256]{2,1,0:T(8,128)(2,1)S(1)} %all-to-all-done.3) | copy-start | bytes 2457604
  245.4 18.7 %all-to-all-start.5 = ((bf16[8,200,128]{2,1,0:T(8,128)(2,1)}), bf16[8,200,128]{2,1,0:T(8,128)(2,1)S(1)}, u32[]{:S(2)}, u32[]{:S(2)}) async-start(bf16[8,200,128]{2,1,0:T(8,128)(2,1)} %bitcast.64), calls=%async_computation.5 | async-start | bytes 819200 | tf_op jit(solution)/shard_map/all_to_all | solution.py:697
  264.1 16.4 %all-to-all-start.6 = ((bf16[8,200,128]{2,1,0:T(8,128)(2,1)}), bf16[8,200,128]{2,1,0:T(8,128)(2,1)S(1)}, u32[]{:S(2)}, u32[]{:S(2)}) async-start(bf16[8,200,128]{2,1,0:T(8,128)(2,1)} %bitcast.251), calls=%async_computation.6 | async-start | bytes 819200 | tf_op jit(solution)/shard_map/all_to_all | solution.py:697
  281.3 25.6 %all-to-all-start.7 = ((bf16[8,200,512]{2,1,0:T(8,128)(2,1)}), bf16[8,200,512]{2,1,0:T(8,128)(2,1)S(1)}, u32[]{:S(2)}, u32[]{:S(2)}) async-start(bf16[8,200,512]{2,1,0:T(8,128)(2,1)} %bitcast.235), calls=%async_computation.7 | async-start | bytes 3276800 | tf_op jit(solution)/shard_map/all_to_all | solution.py:697
  308.0 26.5 %all-to-all-start.8 = ((bf16[8,200,512]{2,1,0:T(8,128)(2,1)}), bf16[8,200,512]{2,1,0:T(8,128)(2,1)S(1)}, u32[]{:S(2)}, u32[]{:S(2)}) async-start(bf16[8,200,512]{2,1,0:T(8,128)(2,1)} %bitcast.226), calls=%async_computation.8 | async-start | bytes 3276800 | tf_op jit(solution)/shard_map/all_to_all | solution.py:697
  334.1 7.1 %collective-permute-start.14 = (bf16[2,2,2,2,16,2176]{5,4,1,0,2,3:T(8,128)(2,1)}, bf16[2,2,2,2,16,2176]{5,4,1,0,2,3:T(8,128)(2,1)}, u32[]{:S(2)}, u32[]{:S(2)}) collective-permute-start(bf16[2,2,2,2,16,2176]{5,4,1,0,2,3:T(8,128)(2,1)} %bitcast.207), channel_id=1, source_target_pairs={{0,8},{8,0},{1,9},{9,1},{2,10},{10,2},{3,11},{11,3},{4,12},{12,4},... | collective-permute-start | bytes 3342344 | tf_op jit(solution)/shard_map/ppermute | solution.py:558
  335.7 43.8 %all-to-all-start.9 = ((bf16[8,200,512]{2,1,0:T(8,128)(2,1)}), bf16[8,200,512]{2,1,0:T(8,128)(2,1)}, u32[]{:S(2)}, u32[]{:S(2)}) async-start(bf16[8,200,512]{2,1,0:T(8,128)(2,1)} %bitcast.227), calls=%async_computation.9 | async-start | bytes 3276800 | tf_op jit(solution)/shard_map/all_to_all | solution.py:697
  340.4 61.7 %reduce-scatter.5.cloned.1.call-start = ((), (), s32[]{:S(2)}) async-start(), calls=%async_computation.16 | async-start | bytes 3145728 | tf_op jit(solution)/shard_map/reduce_scatter | solution.py:600
  343.7 29.1 %collective-permute-start.15 = (bf16[2,2,2,16,2176]{4,3,1,0,2:T(8,128)(2,1)S(1)}, bf16[2,2,2,16,2176]{4,3,1,0,2:T(8,128)(2,1)S(1)}, u32[]{:S(2)}, u32[]{:S(2)}) collective-permute-start(bf16[2,2,2,16,2176]{4,3,1,0,2:T(8,128)(2,1)S(1)} %dynamic-slice_bitcast_fusion.1), channel_id=1, source_target_pairs={{0,1},{1,0},{2,3},{3,2},{4,5},{5,4},{6,7},{7,6},{8,9},{9,8},{10,11... | collective-permute-start | bytes 1671176 | tf_op jit(solution)/shard_map/ppermute | solution.py:558
  347.2 32.2 %copy-start.3 = (bf16[2,2,2,2,16,2176]{5,4,1,0,2,3:T(8,128)(2,1)S(1)}, bf16[2,2,2,2,16,2176]{5,4,1,0,2,3:T(8,128)(2,1)}, u32[]{:S(2)}) copy-start(bf16[2,2,2,2,16,2176]{5,4,1,0,2,3:T(8,128)(2,1)} %copy-done.2) | copy-start | bytes 3342340
  380.2 15.2 %all-to-all-start.10 = ((f32[32,1,128]{2,1,0:T(1,128)}), f32[32,1,128]{2,1,0:T(1,128)S(1)}, u32[]{:S(2)}, u32[]{:S(2)}) async-start(f32[32,1,128]{2,1,0:T(1,128)} %broadcast_in_dim.15), calls=%async_computation.10 | async-start | bytes 32768 | tf_op jit(solution)/shard_map/all_to_all | solution.py:894
  395.5 111.2 %copy-start.27 = (f32[2,8]{1,0:T(2,128)}, f32[2,8]{1,0:T(2,128)S(1)}, u32[]{:S(2)}) copy-start(f32[2,8]{1,0:T(2,128)S(1)} %reshape.172) | copy-start | bytes 196
  395.5 44.5 %all-to-all-start.11 = ((bf16[8,200,512]{2,1,0:T(8,128)(2,1)}), bf16[8,200,512]{2,1,0:T(8,128)(2,1)S(1)}, u32[]{:S(2)}, u32[]{:S(2)}) async-start(bf16[8,200,512]{2,1,0:T(8,128)(2,1)} %bitcast.234), calls=%async_computation.11 | async-start | bytes 3276800 | tf_op jit(solution)/shard_map/all_to_all | solution.py:697
  401.3 82.4 %reduce-scatter.7.cloned.1.call-start = ((), (), s32[]{:S(2)}) async-start(), calls=%async_computation.17 | async-start | bytes 3145728 | tf_op jit(solution)/shard_map/reduce_scatter | solution.py:600
  402.0 123.5 %reduce-scatter.11.cloned.1.call-start = ((), (), s32[]{:S(2)}) async-start(), calls=%async_computation.19 | async-start | bytes 2621440 | tf_op jit(solution)/shard_map/reduce_scatter | solution.py:834
  403.4 62.4 %copy-start.8 = (bf16[2,256,512]{2,1,0:T(8,128)(2,1)}, bf16[2,256,512]{2,1,0:T(8,128)(2,1)S(1)}, u32[]{:S(2)}) copy-start(bf16[2,256,512]{2,1,0:T(8,128)(2,1)S(1)} %get-tuple-element.188) | copy-start | bytes 1572868
  440.0 17.1 %collective-permute-start.16 = (bf16[2,256,512]{2,1,0:T(8,128)(2,1)S(1)}, bf16[2,256,512]{2,1,0:T(8,128)(2,1)S(1)}, u32[]{:S(2)}, u32[]{:S(2)}) collective-permute-start(bf16[2,256,512]{2,1,0:T(8,128)(2,1)S(1)} %get-tuple-element.186), channel_id=1, source_target_pairs={{8,12},{12,8},{9,13},{13,9},{10,14},{14,10},{11,15},{15,11},{24,28... | collective-permute-start | bytes 1572872 | tf_op jit(solution)/shard_map/ppermute | solution.py:564
  458.7 3.0 collective-permute-start.17
  458.8 67.6 %reduce-scatter.9.cloned.1.call-start = ((), (), s32[]{:S(2)}) async-start(), calls=%async_computation.18 | async-start | bytes 2621440 | tf_op jit(solution)/shard_map/reduce_scatter | solution.py:834
  464.3 14.9 %collective-permute-start.18 = (bf16[2,2,2,16,2176]{4,3,1,0,2:T(8,128)(2,1)}, bf16[2,2,2,16,2176]{4,3,1,0,2:T(8,128)(2,1)S(1)}, u32[]{:S(2)}, u32[]{:S(2)}) collective-permute-start(bf16[2,2,2,16,2176]{4,3,1,0,2:T(8,128)(2,1)} %dynamic-slice_bitcast_fusion), channel_id=1, source_target_pairs={{0,1},{1,0},{2,3},{3,2},{4,5},{5,4},{6,7},{7,6},{8,9},{9,8},{10,11... | collective-permute-start | bytes 1671176 | tf_op jit(solution)/shard_map/ppermute | solution.py:558
  465.8 1.5 collective-permute-start.19
  480.2 23.7 %collective-permute-start.20 = (bf16[2,2,2,16,2176]{4,3,2,1,0:T(8,128)(2,1)}, bf16[2,2,2,16,2176]{4,3,2,1,0:T(8,128)(2,1)}, u32[]{:S(2)}, u32[]{:S(2)}) collective-permute-start(bf16[2,2,2,16,2176]{4,3,2,1,0:T(8,128)(2,1)} %fusion.10), channel_id=1, source_target_pairs={{0,2},{2,0},{1,3},{3,1},{4,6},{6,4},{5,7},{7,5},{8,10},{10,8},{9,1... | collective-permute-start | bytes 1671176 | tf_op jit(solution)/shard_map/ppermute | solution.py:558
  486.0 3.2 collective-permute-start.21
  488.5 18.4 %collective-permute-start.23 = (bf16[2,256,512]{2,1,0:T(8,128)(2,1)}, bf16[2,256,512]{2,1,0:T(8,128)(2,1)S(1)}, u32[]{:S(2)}, u32[]{:S(2)}) collective-permute-start(bf16[2,256,512]{2,1,0:T(8,128)(2,1)} %get-tuple-element.192), channel_id=1, source_target_pairs={{8,12},{12,8},{9,13},{13,9},{10,14},{14,10},{11,15},{15,11},{24,28... | collective-permute-start | bytes 1572872 | tf_op jit(solution)/shard_map/ppermute | solution.py:564
  505.1 10.7 %collective-permute-start.22 = (bf16[2,2,16,2176]{3,2,1,0:T(8,128)(2,1)S(1)}, bf16[2,2,16,2176]{3,2,1,0:T(8,128)(2,1)S(1)}, u32[]{:S(2)}, u32[]{:S(2)}) collective-permute-start(bf16[2,2,16,2176]{3,2,1,0:T(8,128)(2,1)S(1)} %dynamic-slice_bitcast_fusion.2), channel_id=1, source_target_pairs={{0,16},{16,0},{1,17},{17,1},{2,18},{18,2},{3,19},{19,3},{4,20},{20... | collective-permute-start | bytes 835592 | tf_op jit(solution)/shard_map/ppermute | solution.py:558
  517.9 13.4 %collective-permute-start.28 = (bf16[256,512]{1,0:T(8,128)(2,1)}, bf16[256,512]{1,0:T(8,128)(2,1)}, u32[]{:S(2)}, u32[]{:S(2)}) collective-permute-start(bf16[256,512]{1,0:T(8,128)(2,1)} %get-tuple-element.274), channel_id=1, source_target_pairs={{0,8},{8,0},{1,9},{9,1},{2,10},{10,2},{3,11},{11,3},{4,12},{12,4},... | collective-permute-start | bytes 786440 | tf_op jit(solution)/shard_map/ppermute | solution.py:558
  519.9 11.5 %collective-permute-start.27 = (bf16[256,512]{1,0:T(8,128)(2,1)}, bf16[256,512]{1,0:T(8,128)(2,1)}, u32[]{:S(2)}, u32[]{:S(2)}) collective-permute-start(bf16[256,512]{1,0:T(8,128)(2,1)} %get-tuple-element.276), channel_id=1, source_target_pairs={{0,8},{8,0},{1,9},{9,1},{2,10},{10,2},{3,11},{11,3},{4,12},{12,4},... | collective-permute-start | bytes 786440 | tf_op jit(solution)/shard_map/ppermute | solution.py:558
  521.3 10.1 %collective-permute-start.26 = (bf16[256,512]{1,0:T(8,128)(2,1)}, bf16[256,512]{1,0:T(8,128)(2,1)}, u32[]{:S(2)}, u32[]{:S(2)}) collective-permute-start(bf16[256,512]{1,0:T(8,128)(2,1)} %get-tuple-element.278), channel_id=1, source_target_pairs={{0,8},{8,0},{1,9},{9,1},{2,10},{10,2},{3,11},{11,3},{4,12},{12,4},... | collective-permute-start | bytes 786440 | tf_op jit(solution)/shard_map/ppermute | solution.py:558
  523.1 8.2 %collective-permute-start.25 = (bf16[256,512]{1,0:T(8,128)(2,1)S(1)}, bf16[256,512]{1,0:T(8,128)(2,1)S(1)}, u32[]{:S(2)}, u32[]{:S(2)}) collective-permute-start(bf16[256,512]{1,0:T(8,128)(2,1)S(1)} %get-tuple-element.280), channel_id=1, source_target_pairs={{0,8},{8,0},{1,9},{9,1},{2,10},{10,2},{3,11},{11,3},{4,12},{12,4},... | collective-permute-start | bytes 786440 | tf_op jit(solution)/shard_map/ppermute | solution.py:558
  523.8 7.5 %collective-permute-start.24 = (bf16[2,16,2176]{2,1,0:T(8,128)(2,1)S(1)}, bf16[2,16,2176]{2,1,0:T(8,128)(2,1)S(1)}, u32[]{:S(2)}, u32[]{:S(2)}) collective-permute-start(bf16[2,16,2176]{2,1,0:T(8,128)(2,1)S(1)} %get-tuple-element.282), channel_id=1, source_target_pairs={{0,4},{4,0},{1,5},{5,1},{2,6},{6,2},{3,7},{7,3},{8,12},{12,8},{9,1... | collective-permute-start | bytes 417800 | tf_op jit(solution)/shard_map/ppermute | solution.py:558
  (24 other events, 86.9 us)
Sparse Core Ops, SparseCore 0:
  344.1 33.3 reduce-scatter.4
  405.0 33.2 reduce-scatter.6
  458.9 31.7 reduce-scatter.10
  493.8 32.5 reduce-scatter.8

commit v5 on v4

--- a/solution.py
+++ b/solution.py
@@ -20,6 +20,7 @@
 LANES = 128
 PIECES = 4
 VMEM = 56 * 1024 * 1024
+VMEM_EX = 47 * 1024 * 1024
 MOVED = (False, True)
 
 
@@ -314,7 +315,7 @@
             shape((slots, width), BF),
         ]
         + [shape((slots, LANES), BF)] * last,
-        compiler_params=pltpu.CompilerParams(vmem_limit_bytes=VMEM),
+        compiler_params=pltpu.CompilerParams(vmem_limit_bytes=VMEM_EX),
         cost_estimate=pl.CostEstimate(
             flops=4 * slots * width * hidden_units,
             bytes_accessed=slots * (hidden_units * 4 + width * 4) + 4 * width * hidden_units,
@@ -361,7 +362,7 @@
         out_specs=[rows_spec(hidden_units), rows_spec(width)] + [rows_spec(width)] * gated,
         out_shape=[shape((slots, hidden_units), BF), shape((slots, width), BF)]
         + [shape((slots, width), BF)] * gated,
-        compiler_params=pltpu.CompilerParams(vmem_limit_bytes=VMEM),
+        compiler_params=pltpu.CompilerParams(vmem_limit_bytes=VMEM_EX),
         cost_estimate=pl.CostEstimate(
             flops=4 * slots * width * hidden_units,
             bytes_accessed=slots * (hidden_units * 4 + width * 4) + 4 * width * hidden_units,
@@ -393,7 +394,7 @@
             pl.BlockSpec((1, block, width), lambda i: (i, 0, 0)),
         ],
         out_shape=[shape((pieces, width, block), BF), shape((pieces, block, width), BF)],
-        compiler_params=pltpu.CompilerParams(vmem_limit_bytes=VMEM),
+        compiler_params=pltpu.CompilerParams(vmem_limit_bytes=VMEM_EX),
         cost_estimate=pl.CostEstimate(
             flops=4 * slots * width * hidden_units,
             bytes_accessed=slots * (hidden_units * 4 + width * 4) + 4 * width * hidden_units,

time: 551 us -> 547 us (level)
  starting transfers between devices: 113 us -> 124 us
  waiting for transfers between devices: 163 us -> 153 us
    all_to_all x10, waiting for transfers between devices: 59.9 us -> 52.6 us  [exchange(): return lax.all_to_all(rows, over, split_axis=0, concat_axis=0, tiled=True)]
    all_to_all x10, starting transfers between devices: 48 us -> 53.9 us  [exchange(): return lax.all_to_all(rows, over, split_axis=0, concat_axis=0, tiled=True)]
  transfers between devices with their start and end apart: 44 -> 44, of which waited for: 16 -> 15; matrix products, arithmetic and copies ran while one was open for 11% -> 11% of each run, Pallas kernels for 27% -> 27%
where the time goes in v5:
time: 547 us; the launch traced here: 540 us
  waiting for transfers between devices  153 us (28%)
  Pallas kernels  151 us (28%)
  starting transfers between devices  124 us (23%)
  local copies, waits for them, and re-layouts  41.6 us (8%)
  other arithmetic  29.8 us (5%)
  blocking collectives  25.8 us (5%)
  between operations  14.7 us (3%)
    ppermute x21, waiting for transfers between devices, other(): return lax.ppermute(values, axis, [(0, 1), (1, 0)])  97.1 us
    pallas_call x8, Pallas kernels, call(): pl.pallas_call(functools.partial(behind, kernel, len(after)), in_specs=[p...  76 us
    ppermute x21, starting transfers between devices, other(): return lax.ppermute(values, axis, [(0, 1), (1, 0)])  55 us
    all_to_all x10, starting transfers between devices, exchange(): return lax.all_to_all(rows, over, split_axis=0, concat_axis=0, tiled=True)  53.9 us
    all_to_all x10, waiting for transfers between devices, exchange(): return lax.all_to_all(rows, over, split_axis=0, concat_axis=0, tiled=True)  52.6 us
    pallas_call x2, Pallas kernels, expert_forward(): pl.pallas_call(functools.partial(behind, functools.partial(expert_forward...  29.5 us
    all_to_all x1, blocking collectives, exchange(): return lax.all_to_all(rows, over, split_axis=0, concat_axis=0, tiled=True)  25.8 us
    pallas_call x2, Pallas kernels, expert_backward(): pl.pallas_call(functools.partial(expert_backward_kernel, gated), grid=(4,...  23.1 us
  transfers between devices with their start and end apart: 44, of which 15 were waited for; matrix products, arithmetic and copies ran while one was open for 11% of the time, Pallas kernels for 27%

profile of v5, /device:TPU:0, one launch (start us, length us, event | category | flops | bytes accessed | tf_op | source)
XLA Modules:
  0.0 539.9 jit_solution(17530420209923644702)
XLA Ops:
  9.0 3.0 collective-permute-start
  12.0 2.5 collective-permute-done
  15.4 3.1 collective-permute-start.1
  20.3 3.7 collective-permute-done.1
  27.6 3.0 slice_bitcast_fusion
  36.2 8.8 %shard_map.203 = (bf16[416,1600]{1,0:T(8,128)(2,1)}, bf16[416,1600]{1,0:T(8,128)(2,1)}, bf16[1600,416]{1,0:T(8,128)(2,1)}, bf16[1600,416]{1,0:T(8,128)(2,1)}, bf...) custom-call(s32[2,416,2]{2,1,0:T(8,128)} %copy.109.refs_0_, ...), custom_call_target="tpu_custom_call" | custom-call | flops 177209344 | bytes 12727296 | tf_op jit(solution)/shard_map/pallas_call | solution.py:132
  51.5 10.8 %collective-permute-done.4 = bf16[2,2,2,1,16,2176]{5,4,2,1,0,3:T(8,128)(2,1)S(1)} collective-permute-done((bf16[2,2,2,1,16,2176]{5,4,2,1,0,3:T(8,128)(2,1)S(1)}, bf16[2,2,2,1,16,2176]{5,4,2,1,0,3:T(8,128)(2,1)S(1)}, u32[]{:S(2)}, u32[]{:S(2)}) %collective-permute-start.4) | collective-permute-done | bytes 557088 | tf_op jit(solution)/shard_map/ppermute | solution.py:559
  62.6 11.5 %collective-permute-start.6 = (bf16[2,2,2,2,1,16,2176]{6,5,3,2,1,0,4:T(8,128)(2,1)S(1)}, bf16[2,2,2,2,1,16,2176]{6,5,3,2,1,0,4:T(8,128)(2,1)S(1)}, u32[]{:S(2)}, u32[]{:S(2)}) collective-permute-start(bf16[2,2,2,2,1,16,2176]{6,5,3,2,1,0,4:T(8,128)(2,1)S(1)} %pad_maximum_fusion.3), channel_id=1, source_target_pairs={{0,8},{8,0},{1,9},{9,1},{2,10},{10,2},{3,11},{11,3},{4,12},{12,4},... | collective-permute-start | bytes 3342344 | tf_op jit(solution)/shard_map/ppermute | solution.py:559
  78.7 8.7 %shard_map.204 = (f32[416,512]{1,0:T(8,128)}, bf16[416,1536]{1,0:T(8,128)(2,1)}, bf16[416,512]{1,0:T(8,128)(2,1)}, f32[416,128]{1,0:T(8,128)}, f32[416,128]{1,0:...) custom-call(f32[416,512]{1,0:T(8,128)} %bitcast_convert_fusion.refs_0_.refs_11_, ...), custom_call_target="tpu_custom_call" | custom-call | flops 2917138432 | bytes 10583296 | tf_op jit(solution)/shard_map/pallas_call | solution.py:132
  87.5 5.3 all-to-all-start
  95.9 18.6 %collective-permute-done.11 = bf16[2,2,1,16,2176]{4,3,1,0,2:T(8,128)(2,1)S(1)} collective-permute-done((bf16[2,2,1,16,2176]{4,3,1,0,2:T(8,128)(2,1)S(1)}, bf16[2,2,1,16,2176]{4,3,1,0,2:T(8,128)(2,1)S(1)}, u32[]{:S(2)}, u32[]{:S(2)}) %collective-permute-start.11) | collective-permute-done | bytes 278560 | tf_op jit(solution)/shard_map/ppermute | solution.py:559
  119.3 11.8 %all-to-all-done = bf16[8,200,512]{2,1,0:T(8,128)(2,1)S(1)} async-done(((bf16[8,200,512]{2,1,0:T(8,128)(2,1)}), bf16[8,200,512]{2,1,0:T(8,128)(2,1)S(1)}, u32[]{:S(2)}, u32[]{:S(2)}) %all-to-all-start) | async-done | bytes 1638432 | tf_op jit(solution)/shard_map/all_to_all | solution.py:698
  131.1 4.2 all-to-all-start.1
  135.6 14.6 %shard_map.205 = (bf16[1600,2048]{1,0:T(8,128)(2,1)}, bf16[1600,2048]{1,0:T(8,128)(2,1)}, bf16[1600,512]{1,0:T(8,128)(2,1)}) custom-call(bf16[512,1024]{1,0:T(8,128)(2,1)} %collective-permute-done.2.refs_0_, bf16[512,1024]{1,0:T(8,128)(2,1)} %collective-permute-done.7.refs_1_, bf16[1024,512]{1,0:T(8,128)(2,1)} %collective-permute-done.5.refs_2_, ...), custom_call_target="tpu_custom_call" | custom-call | flops 6710886400 | bytes 20578304 | tf_op jit(solution)/shard_map/pallas_call | solution.py:296
  150.2 4.0 all-to-all-start.2
  155.1 18.9 %collective-permute-start.13 = (bf16[2,2,2,2,1,16,2176]{6,5,3,2,1,0,4:T(8,128)(2,1)S(1)}, bf16[2,2,2,2,1,16,2176]{6,5,3,2,1,0,4:T(8,128)(2,1)}, u32[]{:S(2)}, u32[]{:S(2)}) collective-permute-start(bf16[2,2,2,2,1,16,2176]{6,5,3,2,1,0,4:T(8,128)(2,1)S(1)} %bitcast.209), channel_id=1, source_target_pairs={{0,8},{8,0},{1,9},{9,1},{2,10},{10,2},{3,11},{11,3},{4,12},{12,4},... | collective-permute-start | bytes 3342344 | tf_op jit(solution)/shard_map/ppermute | solution.py:559
  174.0 2.4 bitcast_select_fusion.1
  184.4 13.8 %all-to-all-start.3 = ((bf16[8,200,256]{2,1,0:T(8,128)(2,1)}), bf16[8,200,256]{2,1,0:T(8,128)(2,1)S(1)}, u32[]{:S(2)}, u32[]{:S(2)}) async-start(bf16[8,200,256]{2,1,0:T(8,128)(2,1)} %bitcast.244), calls=%async_computation.3 | async-start | bytes 1638400 | tf_op jit(solution)/shard_map/all_to_all | solution.py:698
  201.6 12.7 %shard_map.206 = (f32[416,512]{1,0:T(8,128)}, bf16[416,512]{1,0:T(8,128)(2,1)}, bf16[416,512]{1,0:T(8,128)(2,1)}, f32[416,512]{1,0:T(8,128)}, bf16[416,1536]{1,0...) custom-call(bf16[512,2048]{1,0:T(8,128)(2,1)} %pad_maximum_fusion.1., ...), custom_call_target="tpu_custom_call" | custom-call | flops 2917138432 | bytes 17210624 | tf_op jit(solution)/shard_map/pallas_call | solution.py:132
  214.3 25.8 %all_to_all.128 = bf16[8,200,512]{2,1,0:T(8,128)(2,1)S(1)} all-to-all(bf16[8,200,512]{2,1,0:T(8,128)(2,1)} %bitcast.236), channel_id=1, replica_groups=mesh['d0'=2,'d1'=2,'e0'=2,'e1'=2,'e2'=2] {'d1','e1','e2'}, dimensions={0} | all-to-all | bytes 3276800 | tf_op jit(solution)/shard_map/all_to_all | solution.py:698
  240.1 3.5 all-to-all-start.5
  243.6 14.9 %shard_map.207 = (bf16[1600,2048]{1,0:T(8,128)(2,1)}, bf16[1600,2048]{1,0:T(8,128)(2,1)}, bf16[1600,512]{1,0:T(8,128)(2,1)}, bf16[1600,128]{1,0:T(8,128)(2,1)}) custom-call(bf16[1600,256]{1,0:T(8,128)(2,1)} %bitcast.48.refs_0_, bf16[1600,256]{1,0:T(8,128)(2,1)S(1)} %bitcast.216, bf16[1600,512]{1,0:T(8,128)(2,1)S(1)} %bitcast.214, ...), custom_call_target="tpu_custom_call" | custom-call | flops 6710886400 | bytes 20578304 | tf_op jit(solution)/shard_map/pallas_call | solution.py:296
  258.5 4.1 all-to-all-start.6
  262.6 11.9 %shard_map.208 = (bf16[1600,2048]{1,0:T(8,128)(2,1)}, bf16[1600,512]{1,0:T(8,128)(2,1)}, bf16[1600,512]{1,0:T(8,128)(2,1)S(1)}) custom-call(bf16[1600,256]{1,0:T(8,128)(2,1)} %bitcast.48.refs_0_, bf16[1600,256]{1,0:T(8,128)(2,1)S(1)} %bitcast.217, bf16[1600,128]{1,0:T(8,128)(2,1)S(1)} %bitcast.218, bf16[1600,2048]{1,0:T(8,128)(2,1)} %get-tuple-element.147.refs_3_, ...), custom_call_target="tpu_custom_call" | custom-call | flops 6710886400 | bytes 20578304 | tf_op jit(solution)/shard_map/pallas_call | solution.py:352
  276.5 4.6 all-to-all-start.7
  281.1 11.2 %shard_map.209 = (bf16[4,512,512]{2,1,0:T(8,128)(2,1)}, bf16[4,512,512]{2,1,0:T(8,128)(2,1)}) custom-call(bf16[1600,512]{1,0:T(8,128)(2,1)S(1)} %bitcast.215, bf16[1600,2048]{1,0:T(8,128)(2,1)} %get-tuple-element.151.hidden_ref, bf16[1600,2048]{1,0:T(8,128)(2,1)} %get-tuple-element.152.active_ref, bf16[1600,512]{1,0:T(8,128)(2,1)S(1)} %copy-done.3), custom_call_target="tpu_custom_call" | custom-call | flops 6710886400 | bytes 20578304 | tf_op jit(solution)/shard_map/pallas_call | solution.py:383
  292.2 10.0 %all-to-all-done.7 = bf16[8,200,512]{2,1,0:T(8,128)(2,1)} async-done(((bf16[8,200,512]{2,1,0:T(8,128)(2,1)}), bf16[8,200,512]{2,1,0:T(8,128)(2,1)}, u32[]{:S(2)}, u32[]{:S(2)}) %all-to-all-start.7) | async-done | bytes 1638432 | tf_op jit(solution)/shard_map/all_to_all | solution.py:698
  302.3 3.7 all-to-all-start.8
  307.1 18.5 %shard_map.211 = (f32[416,512]{1,0:T(8,128)}, bf16[512,2176]{1,0:T(8,128)(2,1)}, bf16[1600,512]{1,0:T(8,128)(2,1)}) custom-call(bf16[4,512,512]{2,1,0:T(8,128)(2,1)} %get-tuple-element.154.refs_0_, bf16[4,512,512]{2,1,0:T(8,128)(2,1)} %get-tuple-element.155.refs_1_, f32[416,512]{1,0:T(8,128)} %bitcast_convert_fusion.1.refs_2_, ...), custom_call_target="tpu_custom_call" | custom-call | flops 5834276864 | bytes 19434752 | tf_op jit(solution)/shard_map/pallas_call | solution.py:132
  325.6 2.8 constant_dynamic-slice_fusion.2
  331.0 4.7 all-to-all-start.9
  343.2 5.4 shard_map.210
  348.5 19.7 %collective-permute-done.15 = bf16[2,2,2,16,2176]{4,3,1,0,2:T(8,128)(2,1)} collective-permute-done((bf16[2,2,2,16,2176]{4,3,1,0,2:T(8,128)(2,1)S(1)}, bf16[2,2,2,16,2176]{4,3,1,0,2:T(8,128)(2,1)}, u32[]{:S(2)}, u32[]{:S(2)}) %collective-permute-start.15) | collective-permute-done | bytes 557088 | tf_op jit(solution)/shard_map/ppermute | solution.py:559
  368.2 6.5 %all-to-all-done.9 = bf16[8,200,512]{2,1,0:T(8,128)(2,1)S(1)} async-done(((bf16[8,200,512]{2,1,0:T(8,128)(2,1)}), bf16[8,200,512]{2,1,0:T(8,128)(2,1)S(1)}, u32[]{:S(2)}, u32[]{:S(2)}) %all-to-all-start.9) | async-done | bytes 1638432 | tf_op jit(solution)/shard_map/all_to_all | solution.py:698
  377.3 3.3 all-to-all-start.10
  380.6 11.1 %shard_map.212 = (bf16[1600,2048]{1,0:T(8,128)(2,1)}, bf16[1600,512]{1,0:T(8,128)(2,1)}) custom-call(bf16[1600,512]{1,0:T(8,128)(2,1)S(1)} %bitcast.212, bf16[1600,2048]{1,0:T(8,128)(2,1)} %get-tuple-element.167.refs_1_, bf16[2,1,512,2048]{3,2,1,0:T(8,128)(2,1)} %refs_2_.1, bf16[2,1,2048,512]{3,2,1,0:T(8,128)(2,1)} %refs_3_.3), custom_call_target="tpu_custom_call" | custom-call | flops 6710886400 | bytes 20578304 | tf_op jit(solution)/shard_map/pallas_call | solution.py:352
  391.9 5.8 %all-to-all-start.11 = ((bf16[8,200,512]{2,1,0:T(8,128)(2,1)}), bf16[8,200,512]{2,1,0:T(8,128)(2,1)}, u32[]{:S(2)}, u32[]{:S(2)}) async-start(bf16[8,200,512]{2,1,0:T(8,128)(2,1)} %bitcast.83), calls=%async_computation.11 | async-start | bytes 3276800 | tf_op jit(solution)/shard_map/all_to_all | solution.py:698
  398.5 2.3 fusion.20
  400.8 11.4 %shard_map.213 = (bf16[4,512,512]{2,1,0:T(8,128)(2,1)}, bf16[4,512,512]{2,1,0:T(8,128)(2,1)}) custom-call(bf16[1600,512]{1,0:T(8,128)(2,1)S(1)} %bitcast.211, bf16[1600,2048]{1,0:T(8,128)(2,1)} %get-tuple-element.168.hidden_ref, bf16[1600,2048]{1,0:T(8,128)(2,1)} %get-tuple-element.169.active_ref, bf16[1600,512]{1,0:T(8,128)(2,1)S(1)} %bitcast.213), custom_call_target="tpu_custom_call" | custom-call | flops 6710886400 | bytes 20578304 | tf_op jit(solution)/shard_map/pallas_call | solution.py:383
  412.2 24.3 %all-to-all-done.11 = bf16[8,200,512]{2,1,0:T(8,128)(2,1)} async-done(((bf16[8,200,512]{2,1,0:T(8,128)(2,1)}), bf16[8,200,512]{2,1,0:T(8,128)(2,1)}, u32[]{:S(2)}, u32[]{:S(2)}) %all-to-all-start.11) | async-done | bytes 1638432 | tf_op jit(solution)/shard_map/all_to_all | solution.py:698
  437.4 15.9 %shard_map.214 = (f32[416,512]{1,0:T(8,128)}, bf16[512,2176]{1,0:T(8,128)(2,1)}) custom-call(bf16[4,512,512]{2,1,0:T(8,128)(2,1)} %get-tuple-element.170.refs_0_, bf16[4,512,512]{2,1,0:T(8,128)(2,1)} %get-tuple-element.171.refs_1_, f32[416,512]{1,0:T(8,128)} %get-tuple-element.172.refs_2_, bf16[1600,512]{1,0:T(8,128)(2,1)} %bitcast.84.refs_3_, ...), custom_call_target="tpu_custom_call" | custom-call | flops 5834276864 | bytes 15363328 | tf_op jit(solution)/shard_map/pallas_call | solution.py:132
  455.2 2.5 collective-permute-done.17
  462.7 11.9 %collective-permute-done.18 = bf16[2,2,2,16,2176]{4,3,1,0,2:T(8,128)(2,1)S(1)} collective-permute-done((bf16[2,2,2,16,2176]{4,3,1,0,2:T(8,128)(2,1)S(1)}, bf16[2,2,2,16,2176]{4,3,1,0,2:T(8,128)(2,1)S(1)}, u32[]{:S(2)}, u32[]{:S(2)}) %collective-permute-start.18) | collective-permute-done | bytes 557088 | tf_op jit(solution)/shard_map/ppermute | solution.py:559
  475.6 3.6 collective-permute-start.20
  484.7 14.4 %collective-permute-done.20 = bf16[2,2,2,16,2176]{4,3,2,1,0:T(8,128)(2,1)} collective-permute-done((bf16[2,2,2,16,2176]{4,3,2,1,0:T(8,128)(2,1)}, bf16[2,2,2,16,2176]{4,3,2,1,0:T(8,128)(2,1)}, u32[]{:S(2)}, u32[]{:S(2)}) %collective-permute-start.20) | collective-permute-done | bytes 557088 | tf_op jit(solution)/shard_map/ppermute | solution.py:559
  502.1 8.0 %collective-permute-done.22 = bf16[2,2,16,2176]{3,2,1,0:T(8,128)(2,1)S(1)} collective-permute-done((bf16[2,2,16,2176]{3,2,1,0:T(8,128)(2,1)S(1)}, bf16[2,2,16,2176]{3,2,1,0:T(8,128)(2,1)S(1)}, u32[]{:S(2)}, u32[]{:S(2)}) %collective-permute-start.22) | collective-permute-done | bytes 278560 | tf_op jit(solution)/shard_map/ppermute | solution.py:559
  521.8 4.9 collective-permute-done.24.refs_1_
  527.5 4.2 shard_map.215
  (215 shorter events, 92.7 us)
Async XLA Ops:
  9.0 5.5 %collective-permute-start = (bf16[1,16,2176]{2,1,0:T(8,128)(2,1)}, bf16[1,16,2176]{2,1,0:T(8,128)(2,1)S(1)}, u32[]{:S(2)}, u32[]{:S(2)}) collective-permute-start(bf16[1,16,2176]{2,1,0:T(8,128)(2,1)} %bitcast.248), channel_id=1, source_target_pairs={{0,2},{2,0},{1,3},{3,1},{4,6},{6,4},{5,7},{7,5},{8,10},{10,8},{9,1... | collective-permute-start | bytes 208904 | tf_op jit(solution)/shard_map/ppermute | solution.py:559
  15.4 8.6 %collective-permute-start.1 = (bf16[2,1,16,2176]{3,2,0,1:T(8,128)(2,1)S(1)}, bf16[2,1,16,2176]{3,2,0,1:T(8,128)(2,1)S(1)}, u32[]{:S(2)}, u32[]{:S(2)}) collective-permute-start(bf16[2,1,16,2176]{3,2,0,1:T(8,128)(2,1)S(1)} %pad_maximum_fusion.9), channel_id=1, source_target_pairs={{0,4},{4,0},{1,5},{5,1},{2,6},{6,2},{3,7},{7,3},{8,12},{12,8},{9,1... | collective-permute-start | bytes 417800 | tf_op jit(solution)/shard_map/ppermute | solution.py:559
  25.9 22.1 %collective-permute-start.2 = (bf16[512,1024]{1,0:T(8,128)(2,1)}, bf16[512,1024]{1,0:T(8,128)(2,1)}, u32[]{:S(2)}, u32[]{:S(2)}) collective-permute-start(bf16[512,1024]{1,0:T(8,128)(2,1)} %constant_dynamic-slice_fusion.4), channel_id=1, source_target_pairs={{8,12},{12,8},{9,13},{13,9},{10,14},{14,10},{11,15},{15,11},{24,28... | collective-permute-start | bytes 3145736 | tf_op jit(solution)/shard_map/ppermute | solution.py:565
  30.7 17.3 %collective-permute-start.3 = (bf16[2,2,1,16,2176]{4,3,1,0,2:T(8,128)(2,1)}, bf16[2,2,1,16,2176]{4,3,1,0,2:T(8,128)(2,1)}, u32[]{:S(2)}, u32[]{:S(2)}) collective-permute-start(bf16[2,2,1,16,2176]{4,3,1,0,2:T(8,128)(2,1)} %pad_maximum_fusion.7), channel_id=1, source_target_pairs={{0,1},{1,0},{2,3},{3,2},{4,5},{5,4},{6,7},{7,6},{8,9},{9,8},{10,11... | collective-permute-start | bytes 835592 | tf_op jit(solution)/shard_map/ppermute | solution.py:559
  46.1 5.4 %collective-permute-start.5 = (bf16[1024,512]{1,0:T(8,128)(2,1)}, bf16[1024,512]{1,0:T(8,128)(2,1)}, u32[]{:S(2)}, u32[]{:S(2)}) collective-permute-start(bf16[1024,512]{1,0:T(8,128)(2,1)} %constant_dynamic-slice_fusion.3), channel_id=1, source_target_pairs={{8,12},{12,8},{9,13},{13,9},{10,14},{14,10},{11,15},{15,11},{24,28... | collective-permute-start | bytes 3145736 | tf_op jit(solution)/shard_map/ppermute | solution.py:565
  49.1 13.2 %collective-permute-start.4 = (bf16[2,2,2,1,16,2176]{5,4,2,1,0,3:T(8,128)(2,1)S(1)}, bf16[2,2,2,1,16,2176]{5,4,2,1,0,3:T(8,128)(2,1)S(1)}, u32[]{:S(2)}, u32[]{:S(2)}) collective-permute-start(bf16[2,2,2,1,16,2176]{5,4,2,1,0,3:T(8,128)(2,1)S(1)} %pad_maximum_fusion.5), channel_id=1, source_target_pairs={{0,16},{16,0},{1,17},{17,1},{2,18},{18,2},{3,19},{19,3},{4,20},{20... | collective-permute-start | bytes 1671176 | tf_op jit(solution)/shard_map/ppermute | solution.py:559
  50.7 24.4 %collective-permute-start.9 = (bf16[1,16,2176]{2,1,0:T(8,128)(2,1)}, bf16[1,16,2176]{2,1,0:T(8,128)(2,1)S(1)}, u32[]{:S(2)}, u32[]{:S(2)}) collective-permute-start(bf16[1,16,2176]{2,1,0:T(8,128)(2,1)} %bitcast.28), channel_id=1, source_target_pairs={{0,2},{2,0},{1,3},{3,1},{4,6},{6,4},{5,7},{7,5},{8,10},{10,8},{9,1... | collective-permute-start | bytes 208904 | tf_op jit(solution)/shard_map/ppermute | solution.py:559
  62.6 14.1 %collective-permute-start.6 = (bf16[2,2,2,2,1,16,2176]{6,5,3,2,1,0,4:T(8,128)(2,1)S(1)}, bf16[2,2,2,2,1,16,2176]{6,5,3,2,1,0,4:T(8,128)(2,1)S(1)}, u32[]{:S(2)}, u32[]{:S(2)}) collective-permute-start(bf16[2,2,2,2,1,16,2176]{6,5,3,2,1,0,4:T(8,128)(2,1)S(1)} %pad_maximum_fusion.3), channel_id=1, source_target_pairs={{0,8},{8,0},{1,9},{9,1},{2,10},{10,2},{3,11},{11,3},{4,12},{12,4},... | collective-permute-start | bytes 3342344 | tf_op jit(solution)/shard_map/ppermute | solution.py:559
  76.7 16.1 %collective-permute-start.10 = (bf16[2,1,16,2176]{3,2,0,1:T(8,128)(2,1)}, bf16[2,1,16,2176]{3,2,0,1:T(8,128)(2,1)}, u32[]{:S(2)}, u32[]{:S(2)}) collective-permute-start(bf16[2,1,16,2176]{3,2,0,1:T(8,128)(2,1)} %pad_maximum_fusion.10), channel_id=1, source_target_pairs={{0,4},{4,0},{1,5},{5,1},{2,6},{6,2},{3,7},{7,3},{8,12},{12,8},{9,1... | collective-permute-start | bytes 417800 | tf_op jit(solution)/shard_map/ppermute | solution.py:559
  87.5 43.6 %all-to-all-start = ((bf16[8,200,512]{2,1,0:T(8,128)(2,1)}), bf16[8,200,512]{2,1,0:T(8,128)(2,1)S(1)}, u32[]{:S(2)}, u32[]{:S(2)}) async-start(bf16[8,200,512]{2,1,0:T(8,128)(2,1)} %bitcast.235), calls=%async_computation | async-start | bytes 3276800 | tf_op jit(solution)/shard_map/all_to_all | solution.py:698
  93.8 20.7 %collective-permute-start.11 = (bf16[2,2,1,16,2176]{4,3,1,0,2:T(8,128)(2,1)S(1)}, bf16[2,2,1,16,2176]{4,3,1,0,2:T(8,128)(2,1)S(1)}, u32[]{:S(2)}, u32[]{:S(2)}) collective-permute-start(bf16[2,2,1,16,2176]{4,3,1,0,2:T(8,128)(2,1)S(1)} %pad_maximum_fusion.8), channel_id=1, source_target_pairs={{0,1},{1,0},{2,3},{3,2},{4,5},{5,4},{6,7},{7,6},{8,9},{9,8},{10,11... | collective-permute-start | bytes 835592 | tf_op jit(solution)/shard_map/ppermute | solution.py:559
  114.6 20.8 %collective-permute-start.12 = (bf16[2,2,2,1,16,2176]{5,4,2,1,0,3:T(8,128)(2,1)S(1)}, bf16[2,2,2,1,16,2176]{5,4,2,1,0,3:T(8,128)(2,1)S(1)}, u32[]{:S(2)}, u32[]{:S(2)}) collective-permute-start(bf16[2,2,2,1,16,2176]{5,4,2,1,0,3:T(8,128)(2,1)S(1)} %pad_maximum_fusion.6), channel_id=1, source_target_pairs={{0,16},{16,0},{1,17},{17,1},{2,18},{18,2},{3,19},{19,3},{4,20},{20... | collective-permute-start | bytes 1671176 | tf_op jit(solution)/shard_map/ppermute | solution.py:559
  116.0 19.5 %collective-permute-start.8 = (bf16[1024,512]{1,0:T(8,128)(2,1)}, bf16[1024,512]{1,0:T(8,128)(2,1)}, u32[]{:S(2)}, u32[]{:S(2)}) collective-permute-start(bf16[1024,512]{1,0:T(8,128)(2,1)} %collective-permute-done.5.refs_2_), channel_id=1, source_target_pairs={{8,24},{24,8},{9,25},{25,9},{10,26},{26,10},{11,27},{27,11},{12,28... | collective-permute-start | bytes 3145736 | tf_op jit(solution)/shard_map/ppermute | solution.py:564
  117.7 17.9 %collective-permute-start.7 = (bf16[512,1024]{1,0:T(8,128)(2,1)}, bf16[512,1024]{1,0:T(8,128)(2,1)}, u32[]{:S(2)}, u32[]{:S(2)}) collective-permute-start(bf16[512,1024]{1,0:T(8,128)(2,1)} %collective-permute-done.2.refs_0_), channel_id=1, source_target_pairs={{8,24},{24,8},{9,25},{25,9},{10,26},{26,10},{11,27},{27,11},{12,28... | collective-permute-start | bytes 3145736 | tf_op jit(solution)/shard_map/ppermute | solution.py:564
  131.1 19.1 %all-to-all-start.1 = ((bf16[8,200,256]{2,1,0:T(8,128)(2,1)}), bf16[8,200,256]{2,1,0:T(8,128)(2,1)}, u32[]{:S(2)}, u32[]{:S(2)}) async-start(bf16[8,200,256]{2,1,0:T(8,128)(2,1)} %bitcast.245), calls=%async_computation.1 | async-start | bytes 1638400 | tf_op jit(solution)/shard_map/all_to_all | solution.py:698
  150.2 33.0 %all-to-all-start.2 = ((bf16[8,200,512]{2,1,0:T(8,128)(2,1)}), bf16[8,200,512]{2,1,0:T(8,128)(2,1)S(1)}, u32[]{:S(2)}, u32[]{:S(2)}) async-start(bf16[8,200,512]{2,1,0:T(8,128)(2,1)} %bitcast.49), calls=%async_computation.2 | async-start | bytes 3276800 | tf_op jit(solution)/shard_map/all_to_all | solution.py:698
  155.1 27.0 %collective-permute-start.13 = (bf16[2,2,2,2,1,16,2176]{6,5,3,2,1,0,4:T(8,128)(2,1)S(1)}, bf16[2,2,2,2,1,16,2176]{6,5,3,2,1,0,4:T(8,128)(2,1)}, u32[]{:S(2)}, u32[]{:S(2)}) collective-permute-start(bf16[2,2,2,2,1,16,2176]{6,5,3,2,1,0,4:T(8,128)(2,1)S(1)} %bitcast.209), channel_id=1, source_target_pairs={{0,8},{8,0},{1,9},{9,1},{2,10},{10,2},{3,11},{11,3},{4,12},{12,4},... | collective-permute-start | bytes 3342344 | tf_op jit(solution)/shard_map/ppermute | solution.py:559
  184.4 30.0 %all-to-all-start.3 = ((bf16[8,200,256]{2,1,0:T(8,128)(2,1)}), bf16[8,200,256]{2,1,0:T(8,128)(2,1)S(1)}, u32[]{:S(2)}, u32[]{:S(2)}) async-start(bf16[8,200,256]{2,1,0:T(8,128)(2,1)} %bitcast.244), calls=%async_computation.3 | async-start | bytes 1638400 | tf_op jit(solution)/shard_map/all_to_all | solution.py:698
  240.1 18.4 %all-to-all-start.5 = ((bf16[8,200,128]{2,1,0:T(8,128)(2,1)}), bf16[8,200,128]{2,1,0:T(8,128)(2,1)S(1)}, u32[]{:S(2)}, u32[]{:S(2)}) async-start(bf16[8,200,128]{2,1,0:T(8,128)(2,1)} %bitcast.64), calls=%async_computation.5 | async-start | bytes 819200 | tf_op jit(solution)/shard_map/all_to_all | solution.py:698
  258.5 17.2 %all-to-all-start.6 = ((bf16[8,200,128]{2,1,0:T(8,128)(2,1)}), bf16[8,200,128]{2,1,0:T(8,128)(2,1)S(1)}, u32[]{:S(2)}, u32[]{:S(2)}) async-start(bf16[8,200,128]{2,1,0:T(8,128)(2,1)} %bitcast.66), calls=%async_computation.6 | async-start | bytes 819200 | tf_op jit(solution)/shard_map/all_to_all | solution.py:698
  276.5 25.8 %all-to-all-start.7 = ((bf16[8,200,512]{2,1,0:T(8,128)(2,1)}), bf16[8,200,512]{2,1,0:T(8,128)(2,1)}, u32[]{:S(2)}, u32[]{:S(2)}) async-start(bf16[8,200,512]{2,1,0:T(8,128)(2,1)} %bitcast.68), calls=%async_computation.7 | async-start | bytes 3276800 | tf_op jit(solution)/shard_map/all_to_all | solution.py:698
  302.3 27.6 %all-to-all-start.8 = ((bf16[8,200,512]{2,1,0:T(8,128)(2,1)}), bf16[8,200,512]{2,1,0:T(8,128)(2,1)S(1)}, u32[]{:S(2)}, u32[]{:S(2)}) async-start(bf16[8,200,512]{2,1,0:T(8,128)(2,1)} %bitcast.70), calls=%async_computation.8 | async-start | bytes 3276800 | tf_op jit(solution)/shard_map/all_to_all | solution.py:698
  329.4 7.1 %collective-permute-start.14 = (bf16[2,2,2,2,16,2176]{5,4,1,0,2,3:T(8,128)(2,1)}, bf16[2,2,2,2,16,2176]{5,4,1,0,2,3:T(8,128)(2,1)}, u32[]{:S(2)}, u32[]{:S(2)}) collective-permute-start(bf16[2,2,2,2,16,2176]{5,4,1,0,2,3:T(8,128)(2,1)} %bitcast.207), channel_id=1, source_target_pairs={{0,8},{8,0},{1,9},{9,1},{2,10},{10,2},{3,11},{11,3},{4,12},{12,4},... | collective-permute-start | bytes 3342344 | tf_op jit(solution)/shard_map/ppermute | solution.py:559
  331.0 43.7 %all-to-all-start.9 = ((bf16[8,200,512]{2,1,0:T(8,128)(2,1)}), bf16[8,200,512]{2,1,0:T(8,128)(2,1)S(1)}, u32[]{:S(2)}, u32[]{:S(2)}) async-start(bf16[8,200,512]{2,1,0:T(8,128)(2,1)} %bitcast.234), calls=%async_computation.9 | async-start | bytes 3276800 | tf_op jit(solution)/shard_map/all_to_all | solution.py:698
  335.8 62.7 %reduce-scatter.5.cloned.1.call-start = ((), (), s32[]{:S(2)}) async-start(), calls=%async_computation.16 | async-start | bytes 3145728 | tf_op jit(solution)/shard_map/reduce_scatter | solution.py:601
  339.6 28.6 %collective-permute-start.15 = (bf16[2,2,2,16,2176]{4,3,1,0,2:T(8,128)(2,1)S(1)}, bf16[2,2,2,16,2176]{4,3,1,0,2:T(8,128)(2,1)}, u32[]{:S(2)}, u32[]{:S(2)}) collective-permute-start(bf16[2,2,2,16,2176]{4,3,1,0,2:T(8,128)(2,1)S(1)} %dynamic-slice_bitcast_fusion.1), channel_id=1, source_target_pairs={{0,1},{1,0},{2,3},{3,2},{4,5},{5,4},{6,7},{7,6},{8,9},{9,8},{10,11... | collective-permute-start | bytes 1671176 | tf_op jit(solution)/shard_map/ppermute | solution.py:559
  343.2 31.5 %copy-start.12 = (bf16[2,2,2,2,16,2176]{5,4,1,0,2,3:T(8,128)(2,1)S(1)}, bf16[2,2,2,2,16,2176]{5,4,1,0,2,3:T(8,128)(2,1)}, u32[]{:S(2)}) copy-start(bf16[2,2,2,2,16,2176]{5,4,1,0,2,3:T(8,128)(2,1)} %copy-done.11) | copy-start | bytes 3342340
  377.3 14.4 %all-to-all-start.10 = ((f32[32,1,128]{2,1,0:T(1,128)}), f32[32,1,128]{2,1,0:T(1,128)S(1)}, u32[]{:S(2)}, u32[]{:S(2)}) async-start(f32[32,1,128]{2,1,0:T(1,128)} %broadcast_in_dim.15), calls=%async_computation.10 | async-start | bytes 32768 | tf_op jit(solution)/shard_map/all_to_all | solution.py:895
  391.9 110.1 %copy-start.32 = (f32[2,8]{1,0:T(2,128)}, f32[2,8]{1,0:T(2,128)S(1)}, u32[]{:S(2)}) copy-start(f32[2,8]{1,0:T(2,128)S(1)} %reshape.172) | copy-start | bytes 196
  391.9 44.6 %all-to-all-start.11 = ((bf16[8,200,512]{2,1,0:T(8,128)(2,1)}), bf16[8,200,512]{2,1,0:T(8,128)(2,1)}, u32[]{:S(2)}, u32[]{:S(2)}) async-start(bf16[8,200,512]{2,1,0:T(8,128)(2,1)} %bitcast.83), calls=%async_computation.11 | async-start | bytes 3276800 | tf_op jit(solution)/shard_map/all_to_all | solution.py:698
  397.7 81.5 %reduce-scatter.7.cloned.1.call-start = ((), (), s32[]{:S(2)}) async-start(), calls=%async_computation.17 | async-start | bytes 3145728 | tf_op jit(solution)/shard_map/reduce_scatter | solution.py:601
  398.4 121.2 %reduce-scatter.11.cloned.1.call-start = ((), (), s32[]{:S(2)}) async-start(), calls=%async_computation.19 | async-start | bytes 2621440 | tf_op jit(solution)/shard_map/reduce_scatter | solution.py:835
  436.5 16.8 %collective-permute-start.16 = (bf16[2,256,512]{2,1,0:T(8,128)(2,1)}, bf16[2,256,512]{2,1,0:T(8,128)(2,1)S(1)}, u32[]{:S(2)}, u32[]{:S(2)}) collective-permute-start(bf16[2,256,512]{2,1,0:T(8,128)(2,1)} %get-tuple-element.186), channel_id=1, source_target_pairs={{8,12},{12,8},{9,13},{13,9},{10,14},{14,10},{11,15},{15,11},{24,28... | collective-permute-start | bytes 1572872 | tf_op jit(solution)/shard_map/ppermute | solution.py:565
  454.8 3.0 collective-permute-start.17
  455.2 66.6 %reduce-scatter.9.cloned.1.call-start = ((), (), s32[]{:S(2)}) async-start(), calls=%async_computation.18 | async-start | bytes 2621440 | tf_op jit(solution)/shard_map/reduce_scatter | solution.py:835
  459.6 15.1 %copy-start.8 = (bf16[2,2,2,16,2176]{4,3,1,0,2:T(8,128)(2,1)S(1)}, bf16[2,2,2,16,2176]{4,3,1,0,2:T(8,128)(2,1)}, u32[]{:S(2)}) copy-start(bf16[2,2,2,16,2176]{4,3,1,0,2:T(8,128)(2,1)} %fusion.5) | copy-start | bytes 1671172
  459.7 14.9 %collective-permute-start.18 = (bf16[2,2,2,16,2176]{4,3,1,0,2:T(8,128)(2,1)S(1)}, bf16[2,2,2,16,2176]{4,3,1,0,2:T(8,128)(2,1)S(1)}, u32[]{:S(2)}, u32[]{:S(2)}) collective-permute-start(bf16[2,2,2,16,2176]{4,3,1,0,2:T(8,128)(2,1)S(1)} %dynamic-slice_bitcast_fusion), channel_id=1, source_target_pairs={{0,1},{1,0},{2,3},{3,2},{4,5},{5,4},{6,7},{7,6},{8,9},{9,8},{10,11... | collective-permute-start | bytes 1671176 | tf_op jit(solution)/shard_map/ppermute | solution.py:559
  461.2 1.5 collective-permute-start.19
  475.6 23.5 %collective-permute-start.20 = (bf16[2,2,2,16,2176]{4,3,2,1,0:T(8,128)(2,1)}, bf16[2,2,2,16,2176]{4,3,2,1,0:T(8,128)(2,1)}, u32[]{:S(2)}, u32[]{:S(2)}) collective-permute-start(bf16[2,2,2,16,2176]{4,3,2,1,0:T(8,128)(2,1)} %fusion.10), channel_id=1, source_target_pairs={{0,2},{2,0},{1,3},{3,1},{4,6},{6,4},{5,7},{7,5},{8,10},{10,8},{9,1... | collective-permute-start | bytes 1671176 | tf_op jit(solution)/shard_map/ppermute | solution.py:559
  481.4 3.2 collective-permute-start.21
  484.0 18.0 %copy-start.31 = (f32[2,8]{1,0:T(2,128)S(1)}, f32[2,8]{1,0:T(2,128)}, u32[]{:S(2)}) copy-start(f32[2,8]{1,0:T(2,128)} %param.20) | copy-start | bytes 196
  484.0 18.2 %collective-permute-start.23 = (bf16[2,256,512]{2,1,0:T(8,128)(2,1)}, bf16[2,256,512]{2,1,0:T(8,128)(2,1)S(1)}, u32[]{:S(2)}, u32[]{:S(2)}) collective-permute-start(bf16[2,256,512]{2,1,0:T(8,128)(2,1)} %get-tuple-element.192), channel_id=1, source_target_pairs={{8,12},{12,8},{9,13},{13,9},{10,14},{14,10},{11,15},{15,11},{24,28... | collective-permute-start | bytes 1572872 | tf_op jit(solution)/shard_map/ppermute | solution.py:565
  500.3 9.8 %collective-permute-start.22 = (bf16[2,2,16,2176]{3,2,1,0:T(8,128)(2,1)S(1)}, bf16[2,2,16,2176]{3,2,1,0:T(8,128)(2,1)S(1)}, u32[]{:S(2)}, u32[]{:S(2)}) collective-permute-start(bf16[2,2,16,2176]{3,2,1,0:T(8,128)(2,1)S(1)} %dynamic-slice_bitcast_fusion.2), channel_id=1, source_target_pairs={{0,16},{16,0},{1,17},{17,1},{2,18},{18,2},{3,19},{19,3},{4,20},{20... | collective-permute-start | bytes 835592 | tf_op jit(solution)/shard_map/ppermute | solution.py:559
  512.0 14.7 %collective-permute-start.28 = (bf16[256,512]{1,0:T(8,128)(2,1)S(1)}, bf16[256,512]{1,0:T(8,128)(2,1)}, u32[]{:S(2)}, u32[]{:S(2)}) collective-permute-start(bf16[256,512]{1,0:T(8,128)(2,1)S(1)} %get-tuple-element.274), channel_id=1, source_target_pairs={{0,8},{8,0},{1,9},{9,1},{2,10},{10,2},{3,11},{11,3},{4,12},{12,4},... | collective-permute-start | bytes 786440 | tf_op jit(solution)/shard_map/ppermute | solution.py:559
  514.0 12.7 %collective-permute-start.27 = (bf16[256,512]{1,0:T(8,128)(2,1)}, bf16[256,512]{1,0:T(8,128)(2,1)}, u32[]{:S(2)}, u32[]{:S(2)}) collective-permute-start(bf16[256,512]{1,0:T(8,128)(2,1)} %get-tuple-element.276), channel_id=1, source_target_pairs={{0,8},{8,0},{1,9},{9,1},{2,10},{10,2},{3,11},{11,3},{4,12},{12,4},... | collective-permute-start | bytes 786440 | tf_op jit(solution)/shard_map/ppermute | solution.py:559
  515.3 11.4 %collective-permute-start.26 = (bf16[256,512]{1,0:T(8,128)(2,1)S(1)}, bf16[256,512]{1,0:T(8,128)(2,1)S(1)}, u32[]{:S(2)}, u32[]{:S(2)}) collective-permute-start(bf16[256,512]{1,0:T(8,128)(2,1)S(1)} %get-tuple-element.278), channel_id=1, source_target_pairs={{0,8},{8,0},{1,9},{9,1},{2,10},{10,2},{3,11},{11,3},{4,12},{12,4},... | collective-permute-start | bytes 786440 | tf_op jit(solution)/shard_map/ppermute | solution.py:559
  517.2 9.5 %collective-permute-start.25 = (bf16[256,512]{1,0:T(8,128)(2,1)S(1)}, bf16[256,512]{1,0:T(8,128)(2,1)S(1)}, u32[]{:S(2)}, u32[]{:S(2)}) collective-permute-start(bf16[256,512]{1,0:T(8,128)(2,1)S(1)} %get-tuple-element.280), channel_id=1, source_target_pairs={{0,8},{8,0},{1,9},{9,1},{2,10},{10,2},{3,11},{11,3},{4,12},{12,4},... | collective-permute-start | bytes 786440 | tf_op jit(solution)/shard_map/ppermute | solution.py:559
  517.9 8.8 %collective-permute-start.24 = (bf16[2,16,2176]{2,1,0:T(8,128)(2,1)S(1)}, bf16[2,16,2176]{2,1,0:T(8,128)(2,1)S(1)}, u32[]{:S(2)}, u32[]{:S(2)}) collective-permute-start(bf16[2,16,2176]{2,1,0:T(8,128)(2,1)S(1)} %get-tuple-element.282), channel_id=1, source_target_pairs={{0,4},{4,0},{1,5},{5,1},{2,6},{6,2},{3,7},{7,3},{8,12},{12,8},{9,1... | collective-permute-start | bytes 417800 | tf_op jit(solution)/shard_map/ppermute | solution.py:559
  (29 other events, 114.4 us)
Sparse Core Ops, SparseCore 0:
  339.4 32.7 reduce-scatter.4
  401.4 33.2 reduce-scatter.6
  455.3 31.7 reduce-scatter.10
  490.2 31.5 reduce-scatter.8
